TPU v7x, 32 devices: a whole 2x2x4 slice. The times are simulated.
32 devices in a mesh: groups: 2 (over x), dp: 4 (over z), tensor: 4 (over y, core).
Axes of the slice: x: 2, y: 2, z: 4, core: 2. Of those that a mesh axis runs over, the one named last changes fastest.
Arguments:
- queries: bfloat16 [4096, 8192], P(('groups', 'dp'), 'tensor'), parts along dimension 0, may hold values from -8 to 8
- suffix_rotated_key_slots: bfloat16 [4096, 1024], P(('groups', 'dp'), 'tensor'), parts along dimension 0, may hold values from -8 to 8, as said below
- suffix_value_slots: bfloat16 [4096, 1024], P(('groups', 'dp'), 'tensor'), parts along dimension 0, may hold values from -8 to 8, as said below
- shared_prefix_key_slots: bfloat16 [4096, 1024], P(('groups', 'dp'), 'tensor'), parts along dimension 0, may hold values from -8 to 8, as said below
- shared_prefix_value_slots: bfloat16 [4096, 1024], P(('groups', 'dp'), 'tensor'), parts along dimension 0, may hold values from -8 to 8, as said below
- lengths: int32 [8, 4], P(('groups', 'dp')), parts along dimension 0, may hold values from 1 to 256, 512 in all within a row
- request_adapter_index: int32 [8, 4], P(('groups', 'dp')), parts along dimension 0, may hold values from 0 to 63
- output_weight_matrix: bfloat16 [8192, 8192], P('tensor'), may hold values from -0.5 to 0.5
- adapter_down_factors: bfloat16 [64, 8192, 64], P('dp', 'tensor'), may hold values from -0.5 to 0.5
- adapter_up_factors: bfloat16 [64, 64, 8192], P('dp', None, 'tensor'), may hold values from -0.75 to 0.75
Outputs:
- projected: bfloat16 [4096, 8192], P(('groups', 'dp'), 'tensor'), parts along dimension 0
There are 2 independent parts, one for each index of `groups`. A program takes and returns all parts, laid end to end along the dimension named above; an argument that names none is the same for every part. Nothing has to cross between parts.
Inputs may be any that keep to these rules, and one draw needn't show every extreme that they name: `shared_prefix_key_slots`: cache slot s holds key-value head s * 1; slots of the same head are equal. `shared_prefix_value_slots`: cache slot s holds key-value head s * 1; slots of the same head are equal. `suffix_rotated_key_slots`: cache slot s holds key-value head s * 1; slots of the same head are equal. `suffix_value_slots`: cache slot s holds key-value head s * 1; slots of the same head are equal.
All inputs are finite; a program needn't handle non-finite values.
Results may differ from a plain program's by a relative error of at most 0.014.
Values may be sent and summed in bfloat16 or wider, within the bound.
No kernel may reach another device: no remote copies, remote signals or barrier semaphores. Data moves between devices by JAX's collectives and lax.ppermute only.
A program may use at most 320 MiB of HBM per device.

v0:
```python
import math

import jax
import jax.numpy as jnp
from jax import lax
from jax.sharding import PartitionSpec as P

HD = 128


def attend_part(query_heads, key_rows, value_rows, allowed):
    slot_count = query_heads.shape[1]
    key_heads = key_rows.reshape(key_rows.shape[0], slot_count, HD)
    value_heads = value_rows.reshape(value_rows.shape[0], slot_count, HD)
    scores = jnp.einsum(
        "tsgd,ksd->sgtk", query_heads, key_heads, preferred_element_type=jnp.float32
    ) * (1.0 / math.sqrt(HD))
    if allowed is not None:
        scores = jnp.where(allowed[None, None], scores, -1e30)
    peak = jnp.max(scores, axis=-1)
    weights = jnp.exp(scores - peak[..., None])
    totals = jnp.sum(weights, axis=-1)
    weighted = jnp.einsum(
        "sgtk,ksd->tsgd",
        weights.astype(jnp.bfloat16),
        value_heads,
        preferred_element_type=jnp.float32,
    )
    return (peak, totals, weighted)


def to_rows(factor):
    return jnp.transpose(factor, (2, 0, 1))[..., None]


def combine_two(first, second):
    peak = jnp.maximum(first[0], second[0])
    first_factor = jnp.exp(first[0] - peak)
    second_factor = jnp.exp(second[0] - peak)
    totals = first[1] * first_factor + second[1] * second_factor
    weighted = first[2] * to_rows(first_factor) + second[2] * to_rows(second_factor)
    return (peak, totals, weighted)


def per_device(
    queries,
    suffix_rotated_key_slots,
    suffix_value_slots,
    shared_prefix_key_slots,
    shared_prefix_value_slots,
    lengths,
    request_adapter_index,
    output_weight_matrix,
    adapter_down_factors,
    adapter_up_factors,
):
    tokens_here = queries.shape[0]
    slot_count = suffix_rotated_key_slots.shape[1] // HD
    group_size = queries.shape[1] // HD // slot_count
    query_heads = queries.reshape(tokens_here, slot_count, group_size, HD)
    position = jnp.arange(tokens_here, dtype=jnp.int32)
    seg_ends = jnp.cumsum(lengths[0])
    request_of = jnp.sum((position[:, None] >= seg_ends[None, :]).astype(jnp.int32), axis=1)
    allowed = (request_of[:, None] == request_of[None, :]) & (
        position[None, :] <= position[:, None]
    )
    local_part = attend_part(query_heads, suffix_rotated_key_slots, suffix_value_slots, allowed)
    merged = combine_two(
        local_part,
        attend_part(
            query_heads,
            lax.all_gather(shared_prefix_key_slots, "dp", axis=0, tiled=True),
            lax.all_gather(shared_prefix_value_slots, "dp", axis=0, tiled=True),
            None,
        ),
    )
    attended = (
        (merged[2] / to_rows(merged[1])).reshape(tokens_here, queries.shape[1]).astype(jnp.bfloat16)
    )
    down_all, up_all = (
        lax.all_gather(adapter_down_factors, "dp", axis=0, tiled=True),
        lax.all_gather(adapter_up_factors, "dp", axis=0, tiled=True),
    )
    picked_down_factors = down_all[request_adapter_index[0]]
    picked_up_factors = up_all[request_adapter_index[0]]
    select = (request_of[:, None] == jnp.arange(lengths.shape[1], dtype=jnp.int32)[None, :]).astype(
        jnp.float32
    )
    first_products = jnp.einsum(
        "tk,rkq->trq", attended, picked_down_factors, preferred_element_type=jnp.float32
    )
    partial_shrink = jnp.sum(first_products * select[:, :, None], axis=1)
    shrink = lax.psum(partial_shrink.astype(jnp.bfloat16), "tensor")
    second_products = jnp.einsum(
        "tq,rqd->trd", shrink, picked_up_factors, preferred_element_type=jnp.float32
    )
    expand = jnp.sum(second_products * select[:, :, None], axis=1)
    own_share = lax.psum_scatter(
        lax.dot_general(
            output_weight_matrix,
            attended,
            (((0,), (1,)), ((), ())),
            preferred_element_type=jnp.float32,
        ).astype(jnp.bfloat16),
        "tensor",
        scatter_dimension=0,
        tiled=True,
    ).astype(jnp.float32)
    base = jnp.transpose(own_share)
    return (base + expand).astype(jnp.bfloat16)


def solution(mesh):
    return jax.shard_map(
        per_device,
        mesh=mesh,
        in_specs=(
            P(("groups", "dp"), "tensor"),
            P(("groups", "dp"), "tensor"),
            P(("groups", "dp"), "tensor"),
            P(("groups", "dp"), "tensor"),
            P(("groups", "dp"), "tensor"),
            P(("groups", "dp"), None),
            P(("groups", "dp"), None),
            P("tensor", None),
            P("dp", "tensor", None),
            P("dp", None, "tensor"),
        ),
        out_specs=P(("groups", "dp"), "tensor"),
        check_vma=False,
    )
```

profile of v0, /device:TPU:0, one launch (start us, length us, event | category | flops | bytes accessed | tf_op | source)
XLA Modules:
  0.0 760.5 jit_solution(14219182961953242141)
XLA Ops:
  6.5 0.7 all-gather.7.cloned.1.call-update
  7.3 1.8 copy.43
  9.2 0.7 all-gather.9.cloned.1.call-update
  9.9 0.5 all-gather.11.cloned.1.call-update
  10.5 2.2 copy.61
  12.7 1.0 reshape.136
  13.7 1.8 copy.58
  15.5 0.8 reduce-window.8
  16.3 0.7 fusion.29
  17.0 0.1 convert_reduce_fusion
  17.1 0.2 fusion.22
  17.3 7.5 fusion.7
  24.8 9.3 %fusion.5 = f32[2,8,512]{2,1,0:T(8,128)S(1)} fusion(f32[2,512,512,8]{2,1,3,0:T(8,128)} %get-tuple-element.11, f32[2,8,512]{2,1,0:T(8,128)S(1)} %get-tuple-element.10, pred[512,512]{0,1:T(8,128)(4,1)S(1)} %fusion.22), kind=kLoop, calls=%fused_computation.11 | loop fusion | flops 16769024 | bytes 17104896 | tf_op jit(solution)/shard_map/reduce_sum | solution.py:22
  34.1 5.5 all-gather.7.cloned.1.call-done
  39.6 1.5 copy.46
  41.1 27.5 %all-gather.5.cloned.1.call-done = bf16[2048,256]{0,1:T(8,128)(2,1)} async-done(((bf16[512,256]{0,1:T(8,128)(2,1)}), bf16[2048,256]{0,1:T(8,128)(2,1)}) %all-gather.5.cloned.1.call-update) | async-done | bytes 1048592 | tf_op jit(solution)/shard_map/all_gather | solution.py:72
  68.6 29.1 %bitcast_reduce_fusion = (f32[2,8,512]{2,1,0:T(8,128)S(1)}, f32[2,2048,512,8]{2,1,3,0:T(8,128)}) fusion(bf16[2048,2,128,1]{0,2,3,1:T(8,128)(2,1)} %bitcast.103, bf16[512,2,8,128]{3,2,1,0:T(8,128)(2,1)S(1)} %bitcast.99), kind=kOutput, calls=%fused_computation.3 | convolution fusion | flops 4328513536 | bytes 70287360 | tf_op jit(solution)/shard_map/tsgd,ksd->sgtk/dot_general | solution.py:15
  97.7 21.6 %fusion.1 = f32[2,8,512]{2,1,0:T(8,128)S(1)} fusion(f32[2,2048,512,8]{2,1,3,0:T(8,128)} %get-tuple-element.9, f32[2,8,512]{2,1,0:T(8,128)S(1)} %get-tuple-element.8), kind=kLoop, calls=%fused_computation.5 | loop fusion | flops 50323456 | bytes 67174400 | tf_op jit(solution)/shard_map/reduce_sum | solution.py:22
  119.4 23.9 %fusion.3 = f32[2,8,512,128]{2,3,1,0:T(8,128)S(1)} fusion(bf16[2048,2,128,1]{0,2,3,1:T(8,128)(2,1)S(1)} %bitcast.100, f32[2,2048,512,8]{2,1,3,0:T(8,128)} %get-tuple-element.9, f32[2,8,512]{2,1,0:T(8,128)S(1)} %get-tuple-element.8), kind=kOutput, calls=%fused_computation.7 | convolution fusion | flops 4345298944 | bytes 72384512 | tf_op jit(solution)/shard_map/sgtk,ksd->tsgd/dot_general | solution.py:23
  143.3 8.5 %fusion.15 = bf16[512,2,8,128]{0,3,2,1:T(8,128)(2,1)S(1)} fusion(f32[2,8,512,128]{2,3,1,0:T(8,128)S(1)} %fusion.3, bf16[512,2,128,1]{0,2,3,1:T(8,128)(2,1)S(1)} %bitcast.106, f32[2,512,512,8]{2,1,3,0:T(8,128)} %get-tuple-element.11, f32[2,8,512]{2,1,0:T(8,128)S(1)} %get-tuple-element.10, pred[512,512]{0,1:T(8,128)(4,1)S(1)} %fusion.22, ...), kind=kOutput, calls=%fused_computation.23 | convolution fusion | flops 1095761920 | bytes 23724032 | tf_op jit(solution)/shard_map/sgtk,ksd->tsgd/dot_general | solution.py:23
  151.8 204.7 %all-gather.9.cloned.1.call-done = bf16[64,2048,64]{1,2,0:T(8,128)(2,1)} async-done(((bf16[16,2048,64]{1,2,0:T(8,128)(2,1)}), bf16[64,2048,64]{1,2,0:T(8,128)(2,1)}) %all-gather.9.cloned.1.call-update) | async-done | bytes 16777232 | tf_op jit(solution)/shard_map/all_gather | solution.py:81
  356.5 6.4 gather_fusion
  362.9 0.7 fusion.35
  363.6 0.7 multiply_reduce_fusion.1
  364.3 0.0 reduce-scatter.2.cloned.1.call-start
  364.3 28.0 %fusion.8 = bf16[8192,512]{0,1:T(8,128)(2,1)} fusion(bf16[512,2048]{0,1:T(8,128)(2,1)S(1)} %bitcast.110, bf16[2048,8192]{1,0:T(8,128)(2,1)} %param.17), kind=kOutput, calls=%fused_computation.15 | convolution fusion | flops 17184063488 | bytes 44040192 | tf_op jit(solution)/shard_map/dot_general | solution.py:99
  392.3 250.6 %all-gather.11.cloned.1.call-done = bf16[64,64,2048]{2,1,0:T(8,128)(2,1)} async-done(((bf16[16,64,2048]{2,1,0:T(8,128)(2,1)}), bf16[64,64,2048]{2,1,0:T(8,128)(2,1)}) %all-gather.11.cloned.1.call-update) | async-done | bytes 16777232 | tf_op jit(solution)/shard_map/all_gather | solution.py:82
  642.9 6.4 gather_fusion.1
  649.3 25.1 %all-reduce.2.cloned.1.call-done = bf16[512,64]{0,1:T(8,128)(2,1)} async-done(((bf16[512,64]{0,1:T(8,128)(2,1)}), bf16[512,64]{0,1:T(8,128)(2,1)}) %all-reduce.2.cloned.1.call-update) | async-done | bytes 65552 | tf_op jit(solution)/shard_map/psum | solution.py:93
  674.4 5.5 multiply_reduce_fusion
  679.9 68.9 %reduce-scatter.2.cloned.1.call-done = bf16[2048,512]{0,1:T(8,128)(2,1)} async-done(((bf16[8192,512]{0,1:T(8,128)(2,1)}), bf16[2048,512]{0,1:T(8,128)(2,1)}) %reduce-scatter.2.cloned.1.call-update) | async-done | bytes 2097168 | tf_op jit(solution)/shard_map/reduce_scatter | solution.py:98
  748.7 4.9 fusion.12
  (13 shorter events, 0.3 us)
Async XLA Ops:
  6.5 33.1 %all-gather.7.cloned.1.call-start = ((), (), s32[]{:S(2)}) async-start(), calls=%async_computation.2 | async-start | bytes 1310720 | tf_op jit(solution)/shard_map/all_gather | solution.py:73
  7.3 61.4 %all-gather.5.cloned.1.call-start = ((), (), s32[]{:S(2)}) async-start(), calls=%async_computation.1 | async-start | bytes 1310720 | tf_op jit(solution)/shard_map/all_gather | solution.py:72
  9.1 347.4 %all-gather.9.cloned.1.call-start = ((), (), s32[]{:S(2)}) async-start(), calls=%async_computation.4 | async-start | bytes 20971520 | tf_op jit(solution)/shard_map/all_gather | solution.py:81
  9.9 633.1 %all-gather.11.cloned.1.call-start = ((), (), s32[]{:S(2)}) async-start(), calls=%async_computation.6 | async-start | bytes 20971520 | tf_op jit(solution)/shard_map/all_gather | solution.py:82
  10.4 663.9 %all-reduce.2.cloned.1.call-start = ((), (), s32[]{:S(2)}) async-start(), calls=%async_computation.5 | async-start | bytes 131072 | tf_op jit(solution)/shard_map/psum | solution.py:93
  119.4 23.9 %copy-start = (bf16[512,256]{0,1:T(8,128)(2,1)S(1)}, bf16[512,256]{0,1:T(8,128)(2,1)}, u32[]{:S(2)}) copy-start(bf16[512,256]{0,1:T(8,128)(2,1)} %copy.58) | copy-start | bytes 786436
  364.3 384.4 %reduce-scatter.2.cloned.1.call-start = ((), (), s32[]{:S(2)}) async-start(), calls=%async_computation.3 | async-start | bytes 10485760 | tf_op jit(solution)/shard_map/reduce_scatter | solution.py:98
Sparse Core Ops, SparseCore 0:
  8.9 30.6 all-gather.6
  41.2 27.4 all-gather.4
  70.2 286.2 all-gather.8
  357.9 284.9 all-gather.10
  645.1 29.2 all-reduce.1
  677.0 71.6 reduce-scatter.1
where the time goes:
time: 761 us; the launch traced here: 760 us
  waiting for transfers between devices  584 us (77%)
  matrix products  103 us (14%)
  other arithmetic  38.3 us (5%)
  local copies, waits for them, and re-layouts  21.1 us (3%)
  between operations  13.6 us (2%)
    all_gather x1, waiting for transfers between devices, per_device(): lax.all_gather(adapter_up_factors, 'dp', axis=0, tiled=True)  251 us
    all_gather x1, waiting for transfers between devices, per_device(): lax.all_gather(adapter_down_factors, 'dp', axis=0, tiled=True)  205 us
    reduce_scatter x1, waiting for transfers between devices, per_device(): lax.psum_scatter(lax.dot_general(output_weight_matrix, attended, (((0,),...  68.9 us
    dot_general x2, matrix products, attend_part(): jnp.einsum('tsgd,ksd->sgtk', query_heads, key_heads, preferred_element_ty...  36.6 us
    dot_general x2, matrix products, attend_part(): jnp.einsum('sgtk,ksd->tsgd', weights.astype(jnp.bfloat16), value_heads, p...  32.4 us
    reduce_sum x2, other arithmetic, attend_part(): totals = jnp.sum(weights, axis=-1)  30.9 us
    dot_general x1, matrix products, per_device(): lax.dot_general(output_weight_matrix, attended, (((0,), (1,)), ((), ())),...  28 us
    all_gather x1, waiting for transfers between devices, per_device(): lax.all_gather(shared_prefix_key_slots, 'dp', axis=0, tiled=True)  27.5 us
  transfers between devices with their start and end apart: 6, of which 6 were waited for; matrix products, arithmetic and copies ran while one was open for 21% of the time, Pallas kernels for 0%

commit v1 on v0

v1 whole, which is shorter than its diff:
```python
import functools
import math

import jax
import jax.numpy as jnp
from jax import lax
from jax.experimental import pallas as pl
from jax.experimental.pallas import tpu as pltpu
from jax.sharding import PartitionSpec as P

HD = 128
LAG = 2
ROUNDS = 6
CHUNKS = 2
F32 = jnp.float32
BF16 = jnp.bfloat16
SMEM = pltpu.MemorySpace.SMEM
VMEM = pltpu.MemorySpace.VMEM


def params(mib=32, **more):
    return pltpu.CompilerParams(vmem_limit_bytes=mib * 1024 * 1024, **more)


def attend_kernel(blocks, rows, scale, q_ref, seg_q, seg_k, *refs):
    keys, values = refs[: blocks + 1], refs[blocks + 1 : 2 * blocks + 2]
    out_ref, bias = refs[-2], refs[-1]

    @pl.when(pl.program_id(0) == 0)
    def _():
        same = seg_q[:, 0:1] == seg_k[0:1, :]
        first = seg_q[:, 1:2]
        where_k = lax.broadcasted_iota(jnp.int32, bias.shape, 1)
        bias[...] = jnp.where(same & (where_k <= first), 0.0, -1e30)

    q = q_ref[...]
    dims = (((1,), (1,)), ((), ()))
    scores = [lax.dot_general(q, k[...], dims, preferred_element_type=F32) for k in keys]
    scores[0] = scores[0] + bias[...]
    peak = functools.reduce(jnp.maximum, [jnp.max(s, axis=1, keepdims=True) for s in scores])
    factor = scale * math.log2(math.e)
    total = jnp.zeros((q.shape[0], 1), F32)
    summed = jnp.zeros((q.shape[0], HD), F32)
    for s, v in zip(scores, values):
        w = jnp.exp2((s - peak) * factor)
        total = total + jnp.sum(w, axis=1, keepdims=True)
        summed = summed + jnp.dot(w.astype(BF16), v[...], preferred_element_type=F32)
    out_ref[...] = (summed / total).astype(BF16)


def attend(q, seg_q, seg_k, keys, values, chunk, chunks):
    tokens, width = q.shape
    rows = tokens // chunks
    heads, slots = width // HD, keys[0].shape[1] // HD
    group = heads // slots
    blocks = len(keys) - 1
    kv_specs = [pl.BlockSpec((k.shape[0], HD), lambda h: (0, h // group)) for k in keys]
    n_keys = sum(k.shape[0] for k in keys)
    return pl.pallas_call(
        functools.partial(attend_kernel, blocks, rows, 1.0 / math.sqrt(HD)),
        grid=(heads,),
        out_shape=jax.ShapeDtypeStruct((rows, width), BF16),
        in_specs=[
            pl.BlockSpec((rows, HD), lambda h: (chunk, h)),
            pl.BlockSpec((rows, 2), lambda h: (chunk, 0)),
            pl.BlockSpec((1, tokens), lambda h: (0, 0)),
            *kv_specs,
            *kv_specs,
        ],
        out_specs=pl.BlockSpec((rows, HD), lambda h: (0, h)),
        scratch_shapes=[pltpu.VMEM((rows, tokens), F32)],
        compiler_params=params(40),
        cost_estimate=pl.CostEstimate(
            flops=8 * rows * n_keys * width, bytes_accessed=4 * rows * width, transcendentals=0
        ),
        name="attend",
    )(q, seg_q, seg_k, *keys, *values)


def project_kernel(which, a_ref, w_ref, out_ref):
    out_ref[...] = jnp.dot(a_ref[...], w_ref[...], preferred_element_type=F32).astype(BF16)


def project(a, w, block, count):
    rows, depth = a.shape
    wide = w.shape[1] // count
    tile = min(512, wide)
    steps = wide // tile
    return pl.pallas_call(
        project_kernel,
        out_shape=jax.ShapeDtypeStruct((rows, wide), BF16),
        grid_spec=pltpu.PrefetchScalarGridSpec(
            num_scalar_prefetch=1,
            grid=(steps,),
            in_specs=[
                pl.BlockSpec((rows, depth), lambda j, which: (0, 0)),
                pl.BlockSpec((depth, tile), lambda j, which: (0, which[0] * steps + j)),
            ],
            out_specs=pl.BlockSpec((rows, tile), lambda j, which: (0, j)),
        ),
        compiler_params=params(24),
        cost_estimate=pl.CostEstimate(
            flops=2 * rows * depth * wide, bytes_accessed=2 * depth * wide, transcendentals=0
        ),
        name="project",
    )(block, a, w)


def most_rounds(n_dp, requests):
    return requests * (n_dp - 1) + LAG * n_dp


def schedule_kernel(n_dp, requests, per, idx_ref, z_ref, out_ref):
    limit = most_rounds(n_dp, requests)
    idx = idx_ref[...]
    shape = idx.shape
    z = z_ref[0]
    lane = lax.broadcasted_iota(jnp.int32, shape, 1)
    row = lax.broadcasted_iota(jnp.int32, shape, 0)
    valid = (lane < n_dp * requests) & (row < 4)
    down = (row % 2) == 1
    taker = lane // requests
    holder = idx // per
    local = idx % per
    own = valid & (taker == holder)
    dst = jnp.where(down, n_dp - 1 - taker, taker)
    src = jnp.where(down, n_dp - 1 - holder, holder)
    me = jnp.where(down, n_dp - 1 - z, z)
    moving = valid & (src < dst)
    dst = jnp.where(moving, dst, 0)
    pos = jnp.where(moving, src, 0)
    zero = jnp.zeros(shape, jnp.int32)

    def one_round(carry):
        k, _, pos, ready, came, codes = carry
        sent_code = zero
        for link in range(n_dp - 1):
            can = (pos == link) & (dst > link) & (ready <= k)
            key = jnp.where(can, dst * 256 + 255 - lane, -1)
            best = jnp.max(key, axis=1, keepdims=True)
            chosen = can & (key == best)
            code = jnp.where(src == me, local, per + came)
            sent_code = jnp.where(chosen & (me == link), code, sent_code)
            came = jnp.where(chosen & (me == link + 1), k, came)
            pos = jnp.where(chosen, link + 1, pos)
            ready = jnp.where(chosen, k + LAG, ready)
        total = jnp.sum(sent_code, axis=1, keepdims=True)
        codes = jnp.where(lane == k, total, codes)
        left = jnp.max(jnp.where(pos < dst, 1, 0))
        return k + 1, left, pos, ready, came, codes

    first = jnp.max(jnp.where(pos < dst, 1, 0))
    rounds, _, _, _, came, codes = lax.while_loop(
        lambda c: (c[1] > 0) & (c[0] < limit), one_round, (jnp.int32(0), first, pos, zero, zero, zero)
    )
    place = jnp.where(own & (row == 0), local, 0)
    place = place + jnp.where(moving & (row == 0), per + came, 0)
    place = place + jnp.where(moving & (row == 1), per + limit + came, 0)
    place = jnp.sum(jnp.where(row < 2, place, 0), axis=0, keepdims=True)
    out = jnp.where(row < 2, codes, 0)
    out = jnp.where(row == 2, place, out)
    out_ref[...] = jnp.where(row == 3, rounds, out)


def make_schedule(n_dp, requests, per, idx_rows, z):
    return pl.pallas_call(
        functools.partial(schedule_kernel, n_dp, requests, per),
        out_shape=jax.ShapeDtypeStruct((8, 128), jnp.int32),
        in_specs=[pl.BlockSpec(memory_space=VMEM), pl.BlockSpec(memory_space=SMEM)],
        out_specs=pl.BlockSpec(memory_space=VMEM),
        name="schedule",
    )(idx_rows, z)


def fetch(code, per, own, ups, downs, limit, out, sem):
    @pl.when(code < per)
    def _():
        pltpu.make_async_copy(own.at[jnp.minimum(code, per - 1)], out, sem).start()

    for base, came in ((per, ups), (per + limit, downs)):
        for k, ref in enumerate(came):

            @pl.when(code == base + k)
            def _(ref=ref):
                pltpu.make_async_copy(ref, out, sem).start()


def pick_kernel(first, count, per, limit, n_up, n_down, sched, own, *refs):
    ups, downs = refs[:n_up], refs[n_up : n_up + n_down]
    outs, sems = refs[n_up + n_down : -1], refs[-1]
    for i in range(count):
        fetch(sched[0, first + i], per, own, ups, (), limit, outs[2 * i], sems.at[2 * i])
        fetch(sched[1, first + i], per, own, downs, (), limit, outs[2 * i + 1], sems.at[2 * i + 1])
    for i in range(2 * count):
        pltpu.make_async_copy(own.at[0], outs[i], sems.at[i]).wait()


def pick_sends(sched, own, ups, downs, first, count, limit):
    anywhere = pl.BlockSpec(memory_space=pl.ANY)
    one = jax.ShapeDtypeStruct(own.shape[1:], own.dtype)
    return pl.pallas_call(
        functools.partial(
            pick_kernel, first, count, own.shape[0], limit, len(ups), len(downs)
        ),
        out_shape=[one] * (2 * count),
        in_specs=[pl.BlockSpec(memory_space=SMEM)] + [anywhere] * (1 + len(ups) + len(downs)),
        out_specs=[anywhere] * (2 * count),
        scratch_shapes=[pltpu.SemaphoreType.DMA((2 * count,))],
        name="pick",
    )(sched, own, *ups, *downs)


def gather_kernel(per, limit, requests, n_up, n_down, sched, z, own, *refs):
    ups, downs = refs[:n_up], refs[n_up : n_up + n_down]
    out, sems = refs[-2], refs[-1]
    for r in range(requests):
        fetch(sched[2, z[0] * requests + r], per, own, ups, downs, limit, out.at[r], sems.at[r])
    for r in range(requests):
        pltpu.make_async_copy(own.at[0], out.at[r], sems.at[r]).wait()


def gather_own(sched, z, own, ups, downs, requests, limit):
    anywhere = pl.BlockSpec(memory_space=pl.ANY)
    return pl.pallas_call(
        functools.partial(gather_kernel, own.shape[0], limit, requests, len(ups), len(downs)),
        out_shape=jax.ShapeDtypeStruct((requests,) + own.shape[1:], own.dtype),
        in_specs=[pl.BlockSpec(memory_space=SMEM)] * 2 + [anywhere] * (1 + len(ups) + len(downs)),
        out_specs=anywhere,
        scratch_shapes=[pltpu.SemaphoreType.DMA((requests,))],
        name="gather_own",
    )(sched, z, own, *ups, *downs)


def later_rounds(sched, z, own, ups, downs, requests, limit, n_dp):
    up, down = line(n_dp)
    per = own.shape[0]
    made = len(ups)
    spare = jnp.zeros((limit - made,) + own.shape[1:], own.dtype)
    up_all = jnp.concatenate([jnp.stack(ups), spare])
    down_all = jnp.concatenate([jnp.stack(downs), spare])

    def choose(code, came):
        held = lax.dynamic_index_in_dim(own, jnp.minimum(code, per - 1), 0, keepdims=False)
        passed = lax.dynamic_index_in_dim(came, jnp.clip(code - per, 0, limit - 1), 0, keepdims=False)
        return jnp.where(code < per, held, passed)

    def step(carry):
        k, up_all, down_all = carry
        from_below = lax.ppermute(choose(sched[0, k], up_all), "dp", up)
        from_above = lax.ppermute(choose(sched[1, k], down_all), "dp", down)
        up_all = lax.dynamic_update_index_in_dim(up_all, from_below, k, 0)
        down_all = lax.dynamic_update_index_in_dim(down_all, from_above, k, 0)
        return k + 1, up_all, down_all

    _, up_all, down_all = lax.while_loop(
        lambda c: c[0] < sched[3, 0], step, (jnp.int32(made), up_all, down_all)
    )
    places = lax.dynamic_slice(sched, (2, z[0] * requests), (1, requests))[0]
    picked = []
    for r in range(requests):
        code = places[r]
        below = choose(code, up_all)
        above = lax.dynamic_index_in_dim(
            down_all, jnp.clip(code - per - limit, 0, limit - 1), 0, keepdims=False
        )
        picked.append(jnp.where(code >= per + limit, above, below))
    return jnp.stack(picked)


def line(n):
    return [(i, i + 1) for i in range(n - 1)], [(i + 1, i) for i in range(n - 1)]


def bring_adapters(sched, z, own, requests, n_dp):
    up, down = line(n_dp)
    limit = most_rounds(n_dp, requests)
    rounds = min(ROUNDS, limit)
    ups, downs = [], []
    ahead = []
    for k in range(rounds):
        if k < LAG:
            if k == 0:
                ahead = pick_sends(sched, own, [], [], 0, min(LAG, rounds), limit)
            sends = ahead[2 * k : 2 * k + 2]
        else:
            known = k - LAG + 1
            sends = pick_sends(sched, own, ups[:known], downs[:known], k, 1, limit)
        ups.append(lax.ppermute(sends[0], "dp", up))
        downs.append(lax.ppermute(sends[1], "dp", down))
    return lax.cond(
        sched[3, 0] > rounds,
        lambda: later_rounds(sched, z, own, ups, downs, requests, limit, n_dp),
        lambda: gather_own(sched, z, own, ups, downs, requests, limit),
    )


def by_core(n):
    return [(i, i ^ 1) for i in range(n)]


def by_chip(n):
    return [(i, i ^ 2) for i in range(n)]


def added(a, b):
    return (a.astype(F32) + b.astype(F32)).astype(BF16)


def all_sum(x, n_tensor):
    if n_tensor != 4:
        return lax.psum(x, "tensor")
    x = added(x, lax.ppermute(x, "tensor", by_core(n_tensor)))
    return added(x, lax.ppermute(x, "tensor", by_chip(n_tensor)))


def prefix_order(n):
    table = []
    for z in range(n):
        seen = []
        for hop in range(1, n):
            seen += [(hop, True)] if hop <= z else []
            seen += [(hop, False)] if hop <= n - 1 - z else []
        table.append(seen)
    return [[table[z][s] for z in range(n)] for s in range(n - 1)]


def per_device(
    n_groups,
    n_dp,
    n_tensor,
    queries,
    suffix_rotated_key_slots,
    suffix_value_slots,
    shared_prefix_key_slots,
    shared_prefix_value_slots,
    lengths,
    request_adapter_index,
    output_weight_matrix,
    adapter_down_factors,
    adapter_up_factors,
):
    tokens, width = queries.shape
    requests = lengths.shape[1]
    per = adapter_down_factors.shape[0]
    zi = lax.axis_index("dp").astype(jnp.int32)
    z = zi.reshape(1)
    ti = lax.axis_index("tensor").astype(jnp.int32)
    up, down = line(n_dp)

    lane = jnp.arange(128, dtype=jnp.int32) - zi * requests
    mine = jnp.zeros((128,), jnp.int32)
    for r in range(requests):
        mine = jnp.where(lane == r, request_adapter_index[0, r], mine)
    mine = mine[None]
    groups = [mine] + [
        lax.ppermute(mine, "groups", [(i, (i + s) % n_groups) for i in range(n_groups)])
        for s in range(1, n_groups)
    ]
    both = jnp.concatenate(groups, axis=0)
    known = both
    for s in range(1, n_dp):
        known = known + lax.ppermute(both, "dp", [(i, (i + s) % n_dp) for i in range(n_dp)])
    spare = [jnp.zeros((1, 128), jnp.int32)] * 4
    idx_rows = jnp.concatenate([known[0:1], known[0:1], known[1:2], known[1:2], *spare], axis=0)

    below = [(shared_prefix_key_slots, shared_prefix_value_slots)]
    above = [(shared_prefix_key_slots, shared_prefix_value_slots)]
    for hop in range(1, n_dp):
        below.append(tuple(lax.ppermute(a, "dp", up) for a in below[-1]))
        above.append(tuple(lax.ppermute(a, "dp", down) for a in above[-1]))

    position = jnp.arange(tokens, dtype=jnp.int32)
    seg_ends = jnp.cumsum(lengths[0])
    request_of = jnp.sum((position[:, None] >= seg_ends[None, :]).astype(jnp.int32), axis=1)
    seg_q = jnp.stack([request_of, position], axis=1)
    seg_k = request_of[None]

    keys = [suffix_rotated_key_slots, shared_prefix_key_slots]
    values = [suffix_value_slots, shared_prefix_value_slots]
    for choices in prefix_order(n_dp):
        pick = None
        for place, (hop, from_below) in enumerate(choices):
            arrived = below[hop] if from_below else above[hop]
            if pick is None:
                pick = arrived
            else:
                pick = tuple(jnp.where(zi == place, a, b) for a, b in zip(arrived, pick))
        keys.append(pick[0])
        values.append(pick[1])

    sched = make_schedule(n_dp, requests, per, idx_rows, z)
    down_rows = jnp.transpose(adapter_down_factors, (0, 2, 1))
    picked_down = bring_adapters(sched, z, down_rows, requests, n_dp)
    picked_up = bring_adapters(sched, z, adapter_up_factors, requests, n_dp)

    chunks = CHUNKS
    bases, attended = [], []
    for c in range(chunks):
        part = attend(queries, seg_q, seg_k, keys, values, c, chunks)
        attended.append(part)
        if n_tensor == 4:
            far_other, far_same, near_other, near_same = (
                project(part, output_weight_matrix, (ti ^ m).reshape(1), n_tensor)
                for m in (3, 2, 1, 0)
            )
            core, chip = by_core(n_tensor), by_chip(n_tensor)
            send = added(far_same, lax.ppermute(far_other, "tensor", core))
            arriving = lax.ppermute(send, "tensor", chip)
            near = near_same.astype(F32) + lax.ppermute(near_other, "tensor", core).astype(F32)
            bases.append(near + arriving.astype(F32))
        else:
            whole = project(part, output_weight_matrix, jnp.zeros((1,), jnp.int32), 1)
            share = lax.psum_scatter(whole, "tensor", scatter_dimension=1, tiled=True)
            bases.append(share.astype(F32))
    base = jnp.concatenate(bases, axis=0)
    attended = jnp.concatenate(attended, axis=0)

    select = request_of[:, None] == jnp.arange(requests, dtype=jnp.int32)[None, :]
    first = lax.dot_general(
        attended,
        picked_down.reshape(-1, width),
        (((1,), (1,)), ((), ())),
        preferred_element_type=F32,
    ).reshape(tokens, requests, -1)
    partial_shrink = jnp.sum(jnp.where(select[:, :, None], first, 0.0), axis=1).astype(BF16)
    shrink = all_sum(partial_shrink, n_tensor)
    spread = jnp.where(select[:, :, None], shrink[:, None, :], 0).reshape(tokens, -1)
    expand = jnp.dot(
        spread, picked_up.reshape(spread.shape[1], -1), preferred_element_type=F32
    )
    return (base + expand).astype(BF16)


def solution(mesh):
    return jax.shard_map(
        functools.partial(
            per_device, mesh.shape["groups"], mesh.shape["dp"], mesh.shape["tensor"]
        ),
        mesh=mesh,
        in_specs=(
            P(("groups", "dp"), "tensor"),
            P(("groups", "dp"), "tensor"),
            P(("groups", "dp"), "tensor"),
            P(("groups", "dp"), "tensor"),
            P(("groups", "dp"), "tensor"),
            P(("groups", "dp"), None),
            P(("groups", "dp"), None),
            P("tensor", None),
            P("dp", "tensor", None),
            P("dp", None, "tensor"),
        ),
        out_specs=P(("groups", "dp"), "tensor"),
        check_vma=False,
    )
```

time: 761 us -> 553 us (0.73)
  waiting for transfers between devices: 584 us -> 60.7 us
  Pallas kernels: 0 us -> 356 us
  starting transfers between devices: 0.2 us -> 110 us
  matrix products: 103 us -> 2.96 us
  other arithmetic: 38.3 us -> 11.6 us
  local copies, waits for them, and re-layouts: 21.1 us -> 7.46 us
  between operations: 13.6 us -> 1.65 us
    all_gather x4 -> x0, waiting for transfers between devices: 488 us -> none  [the longest x1 251 us: per_device(): lax.all_gather(adapter_up_factors, 'dp', axis=0, tiled=True)]
    pallas_call x0 -> x23, Pallas kernels: none -> 356 us  [the longest x10 209 us: pick_sends(): pl.pallas_call(functools.partial(pick_kernel, first, count, own.shape[0],...]
    ppermute x0 -> x48, starting transfers between devices: none -> 110 us  [the longest x12 39.9 us: bring_adapters(): ups.append(lax.ppermute(sends[0], 'dp', up))]
    dot_general x6 -> x2, matrix products: 102 us -> 2.96 us  [the longest x1 2.07 us: per_device(): jnp.dot(spread, picked_up.reshape(spread.shape[1], -1), preferred_element...]
    reduce_scatter x1 -> x0, waiting for transfers between devices: 68.9 us -> none  [per_device(): lax.psum_scatter(lax.dot_general(output_weight_matrix, attended, (((0,),...]
    ppermute x0 -> x48, waiting for transfers between devices: none -> 60.7 us  [the longest x1 38.4 us: all_sum(): return added(x, lax.ppermute(x, 'tensor', by_chip(n_tensor)))]
    reduce_sum x3 -> x0, other arithmetic: 31.6 us -> none  [the longest x2 30.9 us: attend_part(): totals = jnp.sum(weights, axis=-1)]
    psum x1 -> x0, waiting for transfers between devices: 25.1 us -> none  [per_device(): shrink = lax.psum(partial_shrink.astype(jnp.bfloat16), 'tensor')]
  transfers between devices with their start and end apart: 6 -> 48, of which waited for: 6 -> 11; matrix products, arithmetic and copies ran while one was open for 21% -> 2% of each run, Pallas kernels for 0% -> 51%
where the time goes in v1:
time: 553 us; the launch traced here: 551 us
  Pallas kernels  356 us (64%)
  starting transfers between devices  110 us (20%)
  waiting for transfers between devices  60.7 us (11%)
  other arithmetic  11.6 us (2%)
  local copies, waits for them, and re-layouts  7.46 us (1%)
    pallas_call x10, Pallas kernels, pick_sends(): pl.pallas_call(functools.partial(pick_kernel, first, count, own.shape[0],...  209 us
    pallas_call x2, Pallas kernels, gather_own(): pl.pallas_call(functools.partial(gather_kernel, own.shape[0], limit, requ...  51.4 us
    pallas_call x8, Pallas kernels, project(): pl.pallas_call(project_kernel, out_shape=jax.ShapeDtypeStruct((rows, wide...  46.7 us
    pallas_call x2, Pallas kernels, attend(): pl.pallas_call(functools.partial(attend_kernel, blocks, rows, 1.0 / math....  43.4 us
    ppermute x12, starting transfers between devices, bring_adapters(): ups.append(lax.ppermute(sends[0], 'dp', up))  39.9 us
    ppermute x1, waiting for transfers between devices, all_sum(): return added(x, lax.ppermute(x, 'tensor', by_chip(n_tensor)))  38.4 us
    ppermute x6, starting transfers between devices, per_device(): below.append(tuple((lax.ppermute(a, 'dp', up) for a in below[-1])))  32.8 us
    ppermute x12, starting transfers between devices, bring_adapters(): downs.append(lax.ppermute(sends[1], 'dp', down))  15.8 us
  transfers between devices with their start and end apart: 48, of which 11 were waited for; matrix products, arithmetic and copies ran while one was open for 2% of the time, Pallas kernels for 51%

profile of v1, /device:TPU:0, one launch (start us, length us, event | category | flops | bytes accessed | tf_op | source)
XLA Modules:
  0.0 551.0 jit_solution(13489919185442099774)
XLA Ops:
  17.4 5.6 %schedule.1.sched = s32[8,128]{1,0:T(8,128)} custom-call(s32[8,128]{1,0:T(8,128)} %add_add_fusion.idx_ref, s32[1]{0:T(128)} %bitcast.99.z_ref), custom_call_target="tpu_custom_call" | custom-call | tf_op jit(solution)/shard_map/schedule/pallas_call | solution.py:166
  23.0 33.6 %pick.10 = (bf16[64,2048]{1,0:T(8,128)(2,1)}, bf16[64,2048]{1,0:T(8,128)(2,1)}, bf16[64,2048]{1,0:T(8,128)(2,1)}, bf16[64,2048]{1,0:T(8,128)(2,1)}) custom-call(s32[8,128]{1,0:T(8,128)} %schedule.1.sched, bf16[16,64,2048]{2,1,0:T(8,128)(2,1)} %bitcast.185), custom_call_target="tpu_custom_call" | custom-call | tf_op jit(solution)/shard_map/pick/pallas_call | solution.py:201
  75.3 17.7 %pick.12 = (bf16[64,2048]{1,0:T(8,128)(2,1)}, bf16[64,2048]{1,0:T(8,128)(2,1)}) custom-call(s32[8,128]{1,0:T(8,128)} %schedule.1.sched, bf16[16,64,2048]{2,1,0:T(8,128)(2,1)} %bitcast.186, bf16[64,2048]{1,0:T(8,128)(2,1)S(1)} %collective-permute-done.26.refs_0_, bf16[64,2048]{1,0:T(8,128)(2,1)S(1)} %collective-permute-done.27.refs_1_, ...), custom_call_target="tpu_custom_call" | custom-call | tf_op jit(solution)/shard_map/pick/pallas_call | solution.py:201
  95.7 17.7 %pick.11 = (bf16[64,2048]{1,0:T(8,128)(2,1)}, bf16[64,2048]{1,0:T(8,128)(2,1)}) custom-call(s32[8,128]{1,0:T(8,128)} %schedule.1.sched, bf16[16,64,2048]{2,1,0:T(8,128)(2,1)} %bitcast.187, bf16[64,2048]{1,0:T(8,128)(2,1)S(1)} %collective-permute-done.26.refs_0_, bf16[64,2048]{1,0:T(8,128)(2,1)S(1)} %collective-permute-done.28.refs_1_.refs_2_.refs_3_.refs_4_), custom_call_target="tpu_custom_call" | custom-call | tf_op jit(solution)/shard_map/pick/pallas_call | solution.py:201
  123.4 17.7 %pick.14 = (bf16[64,2048]{1,0:T(8,128)(2,1)}, bf16[64,2048]{1,0:T(8,128)(2,1)}) custom-call(s32[8,128]{1,0:T(8,128)} %schedule.1.sched, bf16[16,64,2048]{2,1,0:T(8,128)(2,1)} %bitcast.188, bf16[64,2048]{1,0:T(8,128)(2,1)S(1)} %collective-permute-done.26.refs_0_, bf16[64,2048]{1,0:T(8,128)(2,1)S(1)} %collective-permute-done.27.refs_1_, ...), custom_call_target="tpu_custom_call" | custom-call | tf_op jit(solution)/shard_map/pick/pallas_call | solution.py:201
  141.1 6.4 %collective-permute-start.35 = (bf16[64,2048]{1,0:T(8,128)(2,1)}, bf16[64,2048]{1,0:T(8,128)(2,1)S(1)}, u32[]{:S(2)}, u32[]{:S(2)}) collective-permute-start(bf16[64,2048]{1,0:T(8,128)(2,1)} %get-tuple-element.396), channel_id=1, source_target_pairs={{0,4},{4,8},{8,12},{1,5},{5,9},{9,13},{2,6},{6,10},{10,14},{3,7},{... | collective-permute-start | bytes 786440 | tf_op jit(solution)/shard_map/ppermute | solution.py:288
  148.8 17.7 %pick.13 = (bf16[64,2048]{1,0:T(8,128)(2,1)}, bf16[64,2048]{1,0:T(8,128)(2,1)}) custom-call(s32[8,128]{1,0:T(8,128)} %schedule.1.sched, bf16[16,64,2048]{2,1,0:T(8,128)(2,1)} %bitcast.189, bf16[64,2048]{1,0:T(8,128)(2,1)S(1)} %collective-permute-done.26.refs_0_, bf16[64,2048]{1,0:T(8,128)(2,1)S(1)} %collective-permute-done.27.refs_1_, ...), custom_call_target="tpu_custom_call" | custom-call | tf_op jit(solution)/shard_map/pick/pallas_call | solution.py:201
  175.7 6.5 %collective-permute-start.4 = (bf16[512,256]{1,0:T(8,128)(2,1)S(1)}, bf16[512,256]{1,0:T(8,128)(2,1)}, u32[]{:S(2)}, u32[]{:S(2)}) collective-permute-start(bf16[512,256]{1,0:T(8,128)(2,1)S(1)} %copy-done.5), channel_id=1, source_target_pairs={{0,4},{4,8},{8,12},{1,5},{5,9},{9,13},{2,6},{6,10},{10,14},{3,7},{... | collective-permute-start | bytes 786440 | tf_op jit(solution)/shard_map/ppermute | solution.py:369
  184.2 17.8 %conditional.2 = (bf16[4,64,2048]{2,1,0:T(8,128)(2,1)}) conditional(s32[]{:T(128)} %bitcast.100, (s32[8,128]{1,0:T(8,128)}, s32[1]{0:T(128)}, bf16[16,64,2048]{2,1,0:T(8,128)(2,1)}, bf16[64,2048]{1,0:T(8,128)(2,1)S(1)}, bf16[64,2048]{1,0:T(8,128)(2,1)S(1)}, /*index=5*/bf16[64,2048]{1,0:T(8,128)(2,1)S(1)}, bf16[64,2048]{1,0:T(8,128)(2,1)S(1)}, ...), branch_computations={%region_2.3_spmd, %region_3.6_spmd} | conditional | flops 2883659 | bytes 24642886 | solution.py:290
  184.2 17.8 %gather_own.2 = bf16[4,64,2048]{2,1,0:T(8,128)(2,1)} custom-call(s32[8,128]{1,0:T(8,128)} %get-tuple-element.285.sched, s32[1]{0:T(128)} %get-tuple-element.286.z, bf16[16,64,2048]{2,1,0:T(8,128)(2,1)} %get-tuple-element.287.own, bf16[64,2048]{1,0:T(8,128)(2,1)S(1)} %get-tuple-element.288.refs_0_, bf16[64,2048]{1,0:T(8,128)(2,1)S(1)} %get-tuple-element.289.refs_1_, ...), custom_call_target="tpu_custom_call" | custom-call | tf_op jit(solution)/shard_map/cond/branch_0_fun/gather_own/pallas_call | solution.py:224
  203.3 33.6 %pick.15 = (bf16[64,2048]{1,0:T(8,128)(2,1)}, bf16[64,2048]{1,0:T(8,128)(2,1)}, bf16[64,2048]{1,0:T(8,128)(2,1)}, bf16[64,2048]{1,0:T(8,128)(2,1)}) custom-call(s32[8,128]{1,0:T(8,128)} %schedule.1.sched, bf16[16,64,2048]{2,1,0:T(8,128)(2,1)} %own.9), custom_call_target="tpu_custom_call" | custom-call | tf_op jit(solution)/shard_map/pick/pallas_call | solution.py:201
  247.4 5.9 %collective-permute-start.12 = (bf16[512,256]{1,0:T(8,128)(2,1)}, bf16[512,256]{1,0:T(8,128)(2,1)}, u32[]{:S(2)}, u32[]{:S(2)}) collective-permute-start(bf16[512,256]{1,0:T(8,128)(2,1)} %collective-permute-done.10), channel_id=1, source_target_pairs={{0,4},{4,8},{8,12},{1,5},{5,9},{9,13},{2,6},{6,10},{10,14},{3,7},{... | collective-permute-start | bytes 786440 | tf_op jit(solution)/shard_map/ppermute | solution.py:369
  261.1 17.7 %pick.17 = (bf16[64,2048]{1,0:T(8,128)(2,1)}, bf16[64,2048]{1,0:T(8,128)(2,1)}) custom-call(s32[8,128]{1,0:T(8,128)} %schedule.1.sched, bf16[16,64,2048]{2,1,0:T(8,128)(2,1)} %own.9, bf16[64,2048]{1,0:T(8,128)(2,1)S(1)} %collective-permute-done.40.refs_0_, bf16[64,2048]{1,0:T(8,128)(2,1)S(1)} %collective-permute-done.41.refs_1_, ...), custom_call_target="tpu_custom_call" | custom-call | tf_op jit(solution)/shard_map/pick/pallas_call | solution.py:201
  280.5 17.7 %pick.16 = (bf16[64,2048]{1,0:T(8,128)(2,1)}, bf16[64,2048]{1,0:T(8,128)(2,1)}) custom-call(s32[8,128]{1,0:T(8,128)} %schedule.1.sched, bf16[16,64,2048]{2,1,0:T(8,128)(2,1)} %own.9, bf16[64,2048]{1,0:T(8,128)(2,1)S(1)} %collective-permute-done.40.refs_0_, bf16[64,2048]{1,0:T(8,128)(2,1)S(1)} %collective-permute-done.42.refs_1_.refs_2_.refs_3_.refs_4_), custom_call_target="tpu_custom_call" | custom-call | tf_op jit(solution)/shard_map/pick/pallas_call | solution.py:201
  306.1 5.3 collective-permute-start.14
  319.5 17.7 %pick.19 = (bf16[64,2048]{1,0:T(8,128)(2,1)}, bf16[64,2048]{1,0:T(8,128)(2,1)}) custom-call(s32[8,128]{1,0:T(8,128)} %schedule.1.sched, bf16[16,64,2048]{2,1,0:T(8,128)(2,1)} %own.9, bf16[64,2048]{1,0:T(8,128)(2,1)S(1)} %collective-permute-done.40.refs_0_, bf16[64,2048]{1,0:T(8,128)(2,1)S(1)} %collective-permute-done.41.refs_1_, ...), custom_call_target="tpu_custom_call" | custom-call | tf_op jit(solution)/shard_map/pick/pallas_call | solution.py:201
  337.3 5.4 collective-permute-start.49
  342.7 17.7 %pick.18 = (bf16[64,2048]{1,0:T(8,128)(2,1)}, bf16[64,2048]{1,0:T(8,128)(2,1)}) custom-call(s32[8,128]{1,0:T(8,128)} %schedule.1.sched, bf16[16,64,2048]{2,1,0:T(8,128)(2,1)} %own.9, bf16[64,2048]{1,0:T(8,128)(2,1)S(1)} %collective-permute-done.40.refs_0_, bf16[64,2048]{1,0:T(8,128)(2,1)S(1)} %collective-permute-done.41.refs_1_, ...), custom_call_target="tpu_custom_call" | custom-call | tf_op jit(solution)/shard_map/pick/pallas_call | solution.py:201
  361.8 5.3 collective-permute-start.47
  372.8 21.7 %attend.2.a_ref = bf16[256,2048]{1,0:T(8,128)(2,1)S(1)} custom-call(bf16[512,2048]{1,0:T(8,128)(2,1)S(1)} %copy-done.3, s32[512,2]{1,0:T(8,128)S(1)} %copy.14.seg_q, s32[1,512]{1,0:T(1,128)S(1)} %bitcast.183, bf16[512,256]{1,0:T(8,128)(2,1)S(1)} %copy-done.4, bf16[512,256]{1,0:T(8,128)(2,1)S(1)} %copy-done.5, ...), custom_call_target="tpu_custom_call" | custom-call | flops 10737418240 | bytes 2097152 | tf_op jit(solution)/shard_map/attend/pallas_call | solution.py:59
  394.4 21.7 %attend.3.a_ref = bf16[256,2048]{1,0:T(8,128)(2,1)S(1)} custom-call(bf16[512,2048]{1,0:T(8,128)(2,1)S(1)} %copy-done.3, s32[512,2]{1,0:T(8,128)S(1)} %copy.14.seg_q, s32[1,512]{1,0:T(1,128)S(1)} %bitcast.184, bf16[512,256]{1,0:T(8,128)(2,1)S(1)} %copy-done.4, bf16[512,256]{1,0:T(8,128)(2,1)S(1)} %copy-done.5, ...), custom_call_target="tpu_custom_call" | custom-call | flops 10737418240 | bytes 2097152 | tf_op jit(solution)/shard_map/attend/pallas_call | solution.py:59
  416.2 6.3 %project.11 = bf16[256,2048]{1,0:T(8,128)(2,1)} custom-call(s32[1]{0:T(128)} %bitcast.93.which, bf16[256,2048]{1,0:T(8,128)(2,1)S(1)} %attend.2.a_ref, bf16[2048,8192]{1,0:T(8,128)(2,1)} %w_ref.15), custom_call_target="tpu_custom_call" | custom-call | flops 2147483648 | bytes 8388608 | tf_op jit(solution)/shard_map/project/pallas_call | solution.py:89
  422.5 5.5 %project.10 = bf16[256,2048]{1,0:T(8,128)(2,1)S(1)} custom-call(s32[1]{0:T(128)} %bitcast.92.which, bf16[256,2048]{1,0:T(8,128)(2,1)S(1)} %attend.2.a_ref, bf16[2048,8192]{1,0:T(8,128)(2,1)} %w_ref.15), custom_call_target="tpu_custom_call" | custom-call | flops 2147483648 | bytes 8388608 | tf_op jit(solution)/shard_map/project/pallas_call | solution.py:89
  429.0 6.3 %project.15 = bf16[256,2048]{1,0:T(8,128)(2,1)} custom-call(s32[1]{0:T(128)} %bitcast.93.which, bf16[256,2048]{1,0:T(8,128)(2,1)S(1)} %attend.3.a_ref, bf16[2048,8192]{1,0:T(8,128)(2,1)} %w_ref.15), custom_call_target="tpu_custom_call" | custom-call | flops 2147483648 | bytes 8388608 | tf_op jit(solution)/shard_map/project/pallas_call | solution.py:89
  435.3 5.5 %project.14 = bf16[256,2048]{1,0:T(8,128)(2,1)S(1)} custom-call(s32[1]{0:T(128)} %bitcast.92.which, bf16[256,2048]{1,0:T(8,128)(2,1)S(1)} %attend.3.a_ref, bf16[2048,8192]{1,0:T(8,128)(2,1)} %w_ref.15), custom_call_target="tpu_custom_call" | custom-call | flops 2147483648 | bytes 8388608 | tf_op jit(solution)/shard_map/project/pallas_call | solution.py:89
  440.8 6.4 %project.9 = bf16[256,2048]{1,0:T(8,128)(2,1)} custom-call(s32[1]{0:T(128)} %bitcast.91.which, bf16[256,2048]{1,0:T(8,128)(2,1)S(1)} %attend.2.a_ref, bf16[2048,8192]{1,0:T(8,128)(2,1)} %w_ref.15), custom_call_target="tpu_custom_call" | custom-call | flops 2147483648 | bytes 8388608 | tf_op jit(solution)/shard_map/project/pallas_call | solution.py:89
  447.7 5.5 %project.13 = bf16[256,2048]{1,0:T(8,128)(2,1)S(1)} custom-call(s32[1]{0:T(128)} %bitcast.91.which, bf16[256,2048]{1,0:T(8,128)(2,1)S(1)} %attend.3.a_ref, bf16[2048,8192]{1,0:T(8,128)(2,1)} %w_ref.15), custom_call_target="tpu_custom_call" | custom-call | flops 2147483648 | bytes 8388608 | tf_op jit(solution)/shard_map/project/pallas_call | solution.py:89
  454.3 33.9 %conditional.3 = (bf16[4,64,2048]{2,1,0:T(8,128)(2,1)}) conditional(s32[]{:T(128)} %bitcast.100, (s32[8,128]{1,0:T(8,128)}, s32[1]{0:T(128)}, bf16[16,64,2048]{2,1,0:T(8,128)(2,1)}, bf16[64,2048]{1,0:T(8,128)(2,1)S(1)}, bf16[64,2048]{1,0:T(8,128)(2,1)}, /*index=5*/bf16[64,2048]{1,0:T(8,128)(2,1)}, bf16[64,2048]{1,0:T(8,128)(2,1)}, ...), branch_computations={%region_7.8_spmd, %region_8.11_spmd} | conditional | flops 2883659 | bytes 24642886 | solution.py:290
  454.3 33.6 %gather_own.3 = bf16[4,64,2048]{2,1,0:T(8,128)(2,1)} custom-call(s32[8,128]{1,0:T(8,128)} %get-tuple-element.324.sched, s32[1]{0:T(128)} %get-tuple-element.325.z, bf16[16,64,2048]{2,1,0:T(8,128)(2,1)} %get-tuple-element.326.own, bf16[64,2048]{1,0:T(8,128)(2,1)S(1)} %get-tuple-element.327.refs_0_, bf16[64,2048]{1,0:T(8,128)(2,1)} %get-tuple-element.328.refs_1_, ...), custom_call_target="tpu_custom_call" | custom-call | tf_op jit(solution)/shard_map/cond/branch_0_fun/gather_own/pallas_call | solution.py:224
  488.7 5.6 %project.8 = bf16[256,2048]{1,0:T(8,128)(2,1)S(1)} custom-call(s32[1]{0:T(128)} %bitcast.86.which, bf16[256,2048]{1,0:T(8,128)(2,1)S(1)} %attend.2.a_ref, bf16[2048,8192]{1,0:T(8,128)(2,1)} %w_ref.15), custom_call_target="tpu_custom_call" | custom-call | flops 2147483648 | bytes 8388608 | tf_op jit(solution)/shard_map/project/pallas_call | solution.py:89
  502.6 5.5 %project.12 = bf16[256,2048]{1,0:T(8,128)(2,1)S(1)} custom-call(s32[1]{0:T(128)} %bitcast.86.which, bf16[256,2048]{1,0:T(8,128)(2,1)S(1)} %attend.3.a_ref, bf16[2048,8192]{1,0:T(8,128)(2,1)} %w_ref.15), custom_call_target="tpu_custom_call" | custom-call | flops 2147483648 | bytes 8388608 | tf_op jit(solution)/shard_map/project/pallas_call | solution.py:89
  508.1 38.4 %collective-permute-done.39 = bf16[512,64]{0,1:T(8,128)(2,1)S(1)} collective-permute-done((bf16[512,64]{0,1:T(8,128)(2,1)S(1)}, bf16[512,64]{0,1:T(8,128)(2,1)S(1)}, u32[]{:S(2)}, u32[]{:S(2)}) %collective-permute-start.39) | collective-permute-done | bytes 65568 | tf_op jit(solution)/shard_map/ppermute | solution.py:313
  (158 shorter events, 119.9 us)
Async XLA Ops:
  93.1 23.1 %collective-permute-start.31 = (bf16[64,2048]{1,0:T(8,128)(2,1)}, bf16[64,2048]{1,0:T(8,128)(2,1)S(1)}, u32[]{:S(2)}, u32[]{:S(2)}) collective-permute-start(bf16[64,2048]{1,0:T(8,128)(2,1)} %get-tuple-element.392), channel_id=1, source_target_pairs={{0,4},{4,8},{8,12},{1,5},{5,9},{9,13},{2,6},{6,10},{10,14},{3,7},{... | collective-permute-start | bytes 786440 | tf_op jit(solution)/shard_map/ppermute | solution.py:288
  94.4 21.8 %collective-permute-start.34 = (bf16[64,2048]{1,0:T(8,128)(2,1)}, bf16[64,2048]{1,0:T(8,128)(2,1)S(1)}, u32[]{:S(2)}, u32[]{:S(2)}) collective-permute-start(bf16[64,2048]{1,0:T(8,128)(2,1)} %get-tuple-element.395), channel_id=1, source_target_pairs={{4,0},{8,4},{12,8},{5,1},{9,5},{13,9},{6,2},{10,6},{14,10},{7,3},{... | collective-permute-start | bytes 786440 | tf_op jit(solution)/shard_map/ppermute | solution.py:289
  141.1 33.3 %collective-permute-start.35 = (bf16[64,2048]{1,0:T(8,128)(2,1)}, bf16[64,2048]{1,0:T(8,128)(2,1)S(1)}, u32[]{:S(2)}, u32[]{:S(2)}) collective-permute-start(bf16[64,2048]{1,0:T(8,128)(2,1)} %get-tuple-element.396), channel_id=1, source_target_pairs={{0,4},{4,8},{8,12},{1,5},{5,9},{9,13},{2,6},{6,10},{10,14},{3,7},{... | collective-permute-start | bytes 786440 | tf_op jit(solution)/shard_map/ppermute | solution.py:288
  147.5 28.2 %collective-permute-start.37 = (bf16[64,2048]{1,0:T(8,128)(2,1)}, bf16[64,2048]{1,0:T(8,128)(2,1)}, u32[]{:S(2)}, u32[]{:S(2)}) collective-permute-start(bf16[64,2048]{1,0:T(8,128)(2,1)} %get-tuple-element.398), channel_id=1, source_target_pairs={{4,0},{8,4},{12,8},{5,1},{9,5},{13,9},{6,2},{10,6},{14,10},{7,3},{... | collective-permute-start | bytes 786440 | tf_op jit(solution)/shard_map/ppermute | solution.py:289
  166.5 17.7 %collective-permute-start.33 = (bf16[64,2048]{1,0:T(8,128)(2,1)}, bf16[64,2048]{1,0:T(8,128)(2,1)S(1)}, u32[]{:S(2)}, u32[]{:S(2)}) collective-permute-start(bf16[64,2048]{1,0:T(8,128)(2,1)} %get-tuple-element.394), channel_id=1, source_target_pairs={{0,4},{4,8},{8,12},{1,5},{5,9},{9,13},{2,6},{6,10},{10,14},{3,7},{... | collective-permute-start | bytes 786440 | tf_op jit(solution)/shard_map/ppermute | solution.py:288
  167.8 16.4 %collective-permute-start.36 = (bf16[64,2048]{1,0:T(8,128)(2,1)}, bf16[64,2048]{1,0:T(8,128)(2,1)S(1)}, u32[]{:S(2)}, u32[]{:S(2)}) collective-permute-start(bf16[64,2048]{1,0:T(8,128)(2,1)} %get-tuple-element.397), channel_id=1, source_target_pairs={{4,0},{8,4},{12,8},{5,1},{9,5},{13,9},{6,2},{10,6},{14,10},{7,3},{... | collective-permute-start | bytes 786440 | tf_op jit(solution)/shard_map/ppermute | solution.py:289
  169.1 72.4 %collective-permute-start.10 = (bf16[512,256]{1,0:T(8,128)(2,1)S(1)}, bf16[512,256]{1,0:T(8,128)(2,1)}, u32[]{:S(2)}, u32[]{:S(2)}) collective-permute-start(bf16[512,256]{1,0:T(8,128)(2,1)S(1)} %copy-done.7), channel_id=1, source_target_pairs={{0,4},{4,8},{8,12},{1,5},{5,9},{9,13},{2,6},{6,10},{10,14},{3,7},{... | collective-permute-start | bytes 786440 | tf_op jit(solution)/shard_map/ppermute | solution.py:369
  174.4 70.4 %collective-permute-start.11 = (bf16[512,256]{1,0:T(8,128)(2,1)S(1)}, bf16[512,256]{1,0:T(8,128)(2,1)}, u32[]{:S(2)}, u32[]{:S(2)}) collective-permute-start(bf16[512,256]{1,0:T(8,128)(2,1)S(1)} %copy-done.7), channel_id=1, source_target_pairs={{4,0},{8,4},{12,8},{5,1},{9,5},{13,9},{6,2},{10,6},{14,10},{7,3},{... | collective-permute-start | bytes 786440 | tf_op jit(solution)/shard_map/ppermute | solution.py:370
  175.7 70.4 %collective-permute-start.4 = (bf16[512,256]{1,0:T(8,128)(2,1)S(1)}, bf16[512,256]{1,0:T(8,128)(2,1)}, u32[]{:S(2)}, u32[]{:S(2)}) collective-permute-start(bf16[512,256]{1,0:T(8,128)(2,1)S(1)} %copy-done.5), channel_id=1, source_target_pairs={{0,4},{4,8},{8,12},{1,5},{5,9},{9,13},{2,6},{6,10},{10,14},{3,7},{... | collective-permute-start | bytes 786440 | tf_op jit(solution)/shard_map/ppermute | solution.py:369
  202.0 45.4 %collective-permute-start.5 = (bf16[512,256]{1,0:T(8,128)(2,1)S(1)}, bf16[512,256]{1,0:T(8,128)(2,1)S(1)}, u32[]{:S(2)}, u32[]{:S(2)}) collective-permute-start(bf16[512,256]{1,0:T(8,128)(2,1)S(1)} %copy-done.5), channel_id=1, source_target_pairs={{4,0},{8,4},{12,8},{5,1},{9,5},{13,9},{6,2},{10,6},{14,10},{7,3},{... | collective-permute-start | bytes 786440 | tf_op jit(solution)/shard_map/ppermute | solution.py:370
  236.9 16.4 %collective-permute-start.40 = (bf16[64,2048]{1,0:T(8,128)(2,1)}, bf16[64,2048]{1,0:T(8,128)(2,1)S(1)}, u32[]{:S(2)}, u32[]{:S(2)}) collective-permute-start(bf16[64,2048]{1,0:T(8,128)(2,1)} %get-tuple-element.399), channel_id=1, source_target_pairs={{0,4},{4,8},{8,12},{1,5},{5,9},{9,13},{2,6},{6,10},{10,14},{3,7},{... | collective-permute-start | bytes 786440 | tf_op jit(solution)/shard_map/ppermute | solution.py:288
  247.4 50.8 %collective-permute-start.12 = (bf16[512,256]{1,0:T(8,128)(2,1)}, bf16[512,256]{1,0:T(8,128)(2,1)}, u32[]{:S(2)}, u32[]{:S(2)}) collective-permute-start(bf16[512,256]{1,0:T(8,128)(2,1)} %collective-permute-done.10), channel_id=1, source_target_pairs={{0,4},{4,8},{8,12},{1,5},{5,9},{9,13},{2,6},{6,10},{10,14},{3,7},{... | collective-permute-start | bytes 786440 | tf_op jit(solution)/shard_map/ppermute | solution.py:369
  253.3 46.2 %collective-permute-start.13 = (bf16[512,256]{1,0:T(8,128)(2,1)}, bf16[512,256]{1,0:T(8,128)(2,1)S(1)}, u32[]{:S(2)}, u32[]{:S(2)}) collective-permute-start(bf16[512,256]{1,0:T(8,128)(2,1)} %collective-permute-done.11), channel_id=1, source_target_pairs={{4,0},{8,4},{12,8},{5,1},{9,5},{13,9},{6,2},{10,6},{14,10},{7,3},{... | collective-permute-start | bytes 786440 | tf_op jit(solution)/shard_map/ppermute | solution.py:370
  254.6 50.2 %collective-permute-start.6 = (bf16[512,256]{1,0:T(8,128)(2,1)}, bf16[512,256]{1,0:T(8,128)(2,1)S(1)}, u32[]{:S(2)}, u32[]{:S(2)}) collective-permute-start(bf16[512,256]{1,0:T(8,128)(2,1)} %collective-permute-done.4), channel_id=1, source_target_pairs={{0,4},{4,8},{8,12},{1,5},{5,9},{9,13},{2,6},{6,10},{10,14},{3,7},{... | collective-permute-start | bytes 786440 | tf_op jit(solution)/shard_map/ppermute | solution.py:369
  259.2 46.9 %collective-permute-start.7 = (bf16[512,256]{1,0:T(8,128)(2,1)S(1)}, bf16[512,256]{1,0:T(8,128)(2,1)S(1)}, u32[]{:S(2)}, u32[]{:S(2)}) collective-permute-start(bf16[512,256]{1,0:T(8,128)(2,1)S(1)} %collective-permute-done.5), channel_id=1, source_target_pairs={{4,0},{8,4},{12,8},{5,1},{9,5},{13,9},{6,2},{10,6},{14,10},{7,3},{... | collective-permute-start | bytes 786440 | tf_op jit(solution)/shard_map/ppermute | solution.py:370
  278.9 32.5 %collective-permute-start.45 = (bf16[64,2048]{1,0:T(8,128)(2,1)}, bf16[64,2048]{1,0:T(8,128)(2,1)S(1)}, u32[]{:S(2)}, u32[]{:S(2)}) collective-permute-start(bf16[64,2048]{1,0:T(8,128)(2,1)} %get-tuple-element.404), channel_id=1, source_target_pairs={{0,4},{4,8},{8,12},{1,5},{5,9},{9,13},{2,6},{6,10},{10,14},{3,7},{... | collective-permute-start | bytes 786440 | tf_op jit(solution)/shard_map/ppermute | solution.py:288
  300.2 18.0 %collective-permute-start.43 = (bf16[64,2048]{1,0:T(8,128)(2,1)}, bf16[64,2048]{1,0:T(8,128)(2,1)S(1)}, u32[]{:S(2)}, u32[]{:S(2)}) collective-permute-start(bf16[64,2048]{1,0:T(8,128)(2,1)} %get-tuple-element.402), channel_id=1, source_target_pairs={{0,4},{4,8},{8,12},{1,5},{5,9},{9,13},{2,6},{6,10},{10,14},{3,7},{... | collective-permute-start | bytes 786440 | tf_op jit(solution)/shard_map/ppermute | solution.py:288
  306.1 54.4 %collective-permute-start.14 = (bf16[512,256]{1,0:T(8,128)(2,1)}, bf16[512,256]{1,0:T(8,128)(2,1)}, u32[]{:S(2)}, u32[]{:S(2)}) collective-permute-start(bf16[512,256]{1,0:T(8,128)(2,1)} %collective-permute-done.12), channel_id=1, source_target_pairs={{0,4},{4,8},{8,12},{1,5},{5,9},{9,13},{2,6},{6,10},{10,14},{3,7},{... | collective-permute-start | bytes 786440 | tf_op jit(solution)/shard_map/ppermute | solution.py:369
  311.4 50.4 %collective-permute-start.15 = (bf16[512,256]{1,0:T(8,128)(2,1)}, bf16[512,256]{1,0:T(8,128)(2,1)}, u32[]{:S(2)}, u32[]{:S(2)}) collective-permute-start(bf16[512,256]{1,0:T(8,128)(2,1)} %copy-done.20), channel_id=1, source_target_pairs={{4,0},{8,4},{12,8},{5,1},{9,5},{13,9},{6,2},{10,6},{14,10},{7,3},{... | collective-permute-start | bytes 786440 | tf_op jit(solution)/shard_map/ppermute | solution.py:370
  312.9 55.5 %collective-permute-start.8 = (bf16[512,256]{1,0:T(8,128)(2,1)S(1)}, bf16[512,256]{1,0:T(8,128)(2,1)}, u32[]{:S(2)}, u32[]{:S(2)}) collective-permute-start(bf16[512,256]{1,0:T(8,128)(2,1)S(1)} %collective-permute-done.6), channel_id=1, source_target_pairs={{0,4},{4,8},{8,12},{1,5},{5,9},{9,13},{2,6},{6,10},{10,14},{3,7},{... | collective-permute-start | bytes 786440 | tf_op jit(solution)/shard_map/ppermute | solution.py:369
  318.2 51.7 %collective-permute-start.9 = (bf16[512,256]{1,0:T(8,128)(2,1)}, bf16[512,256]{1,0:T(8,128)(2,1)}, u32[]{:S(2)}, u32[]{:S(2)}) collective-permute-start(bf16[512,256]{1,0:T(8,128)(2,1)} %copy-done.19), channel_id=1, source_target_pairs={{4,0},{8,4},{12,8},{5,1},{9,5},{13,9},{6,2},{10,6},{14,10},{7,3},{... | collective-permute-start | bytes 786440 | tf_op jit(solution)/shard_map/ppermute | solution.py:370
  337.3 109.9 %collective-permute-start.49 = (bf16[64,2048]{1,0:T(8,128)(2,1)}, bf16[64,2048]{1,0:T(8,128)(2,1)}, u32[]{:S(2)}, u32[]{:S(2)}) collective-permute-start(bf16[64,2048]{1,0:T(8,128)(2,1)} %get-tuple-element.408), channel_id=1, source_target_pairs={{0,4},{4,8},{8,12},{1,5},{5,9},{9,13},{2,6},{6,10},{10,14},{3,7},{... | collective-permute-start | bytes 786440 | tf_op jit(solution)/shard_map/ppermute | solution.py:288
  360.5 93.7 %collective-permute-start.51 = (bf16[64,2048]{1,0:T(8,128)(2,1)}, bf16[64,2048]{1,0:T(8,128)(2,1)}, u32[]{:S(2)}, u32[]{:S(2)}) collective-permute-start(bf16[64,2048]{1,0:T(8,128)(2,1)} %get-tuple-element.410), channel_id=1, source_target_pairs={{4,0},{8,4},{12,8},{5,1},{9,5},{13,9},{6,2},{10,6},{14,10},{7,3},{... | collective-permute-start | bytes 786440 | tf_op jit(solution)/shard_map/ppermute | solution.py:289
  361.8 92.5 %collective-permute-start.47 = (bf16[64,2048]{1,0:T(8,128)(2,1)}, bf16[64,2048]{1,0:T(8,128)(2,1)}, u32[]{:S(2)}, u32[]{:S(2)}) collective-permute-start(bf16[64,2048]{1,0:T(8,128)(2,1)} %get-tuple-element.406), channel_id=1, source_target_pairs={{0,4},{4,8},{8,12},{1,5},{5,9},{9,13},{2,6},{6,10},{10,14},{3,7},{... | collective-permute-start | bytes 786440 | tf_op jit(solution)/shard_map/ppermute | solution.py:288
  368.4 85.9 %collective-permute-start.50 = (bf16[64,2048]{1,0:T(8,128)(2,1)}, bf16[64,2048]{1,0:T(8,128)(2,1)}, u32[]{:S(2)}, u32[]{:S(2)}) collective-permute-start(bf16[64,2048]{1,0:T(8,128)(2,1)} %get-tuple-element.409), channel_id=1, source_target_pairs={{4,0},{8,4},{12,8},{5,1},{9,5},{13,9},{6,2},{10,6},{14,10},{7,3},{... | collective-permute-start | bytes 786440 | tf_op jit(solution)/shard_map/ppermute | solution.py:289
  422.5 72.9 %collective-permute-start.17 = (bf16[256,2048]{1,0:T(8,128)(2,1)}, bf16[256,2048]{1,0:T(8,128)(2,1)}, u32[]{:S(2)}, u32[]{:S(2)}) collective-permute-start(bf16[256,2048]{1,0:T(8,128)(2,1)} %project.11), channel_id=1, source_target_pairs={{0,1},{1,0},{2,3},{3,2},{4,5},{5,4},{6,7},{7,6},{8,9},{9,8},{10,11... | collective-permute-start | bytes 3145736 | tf_op jit(solution)/shard_map/ppermute | solution.py:407
  447.2 51.5 %collective-permute-start.20 = (bf16[256,2048]{1,0:T(8,128)(2,1)}, bf16[256,2048]{1,0:T(8,128)(2,1)}, u32[]{:S(2)}, u32[]{:S(2)}) collective-permute-start(bf16[256,2048]{1,0:T(8,128)(2,1)} %project.15), channel_id=1, source_target_pairs={{0,1},{1,0},{2,3},{3,2},{4,5},{5,4},{6,7},{7,6},{8,9},{9,8},{10,11... | collective-permute-start | bytes 3145736 | tf_op jit(solution)/shard_map/ppermute | solution.py:407
  454.2 92.3 %collective-permute-start.16 = (bf16[256,2048]{1,0:T(8,128)(2,1)}, bf16[256,2048]{1,0:T(8,128)(2,1)}, u32[]{:S(2)}, u32[]{:S(2)}) collective-permute-start(bf16[256,2048]{1,0:T(8,128)(2,1)} %project.9), channel_id=1, source_target_pairs={{0,1},{1,0},{2,3},{3,2},{4,5},{5,4},{6,7},{7,6},{8,9},{9,8},{10,11... | collective-permute-start | bytes 3145736 | tf_op jit(solution)/shard_map/ppermute | solution.py:409
  488.2 60.1 %collective-permute-start.19 = (bf16[256,2048]{1,0:T(8,128)(2,1)}, bf16[256,2048]{1,0:T(8,128)(2,1)S(1)}, u32[]{:S(2)}, u32[]{:S(2)}) collective-permute-start(bf16[256,2048]{1,0:T(8,128)(2,1)} %copy-done.2), channel_id=1, source_target_pairs={{0,1},{1,0},{2,3},{3,2},{4,5},{5,4},{6,7},{7,6},{8,9},{9,8},{10,11... | collective-permute-start | bytes 3145736 | tf_op jit(solution)/shard_map/ppermute | solution.py:409
  497.2 49.3 %collective-permute-start.18 = (bf16[256,2048]{1,0:T(8,128)(2,1)S(1)}, bf16[256,2048]{1,0:T(8,128)(2,1)S(1)}, u32[]{:S(2)}, u32[]{:S(2)}) collective-permute-start(bf16[256,2048]{1,0:T(8,128)(2,1)S(1)} %add_convert_fusion.1), channel_id=1, source_target_pairs={{0,2},{1,3},{2,0},{3,1},{4,6},{5,7},{6,4},{7,5},{8,10},{9,11},{10,... | collective-permute-start | bytes 3145736 | tf_op jit(solution)/shard_map/ppermute | solution.py:408
  500.4 48.0 %collective-permute-start.21 = (bf16[256,2048]{1,0:T(8,128)(2,1)S(1)}, bf16[256,2048]{1,0:T(8,128)(2,1)S(1)}, u32[]{:S(2)}, u32[]{:S(2)}) collective-permute-start(bf16[256,2048]{1,0:T(8,128)(2,1)S(1)} %add_convert_fusion), channel_id=1, source_target_pairs={{0,2},{1,3},{2,0},{3,1},{4,6},{5,7},{6,4},{7,5},{8,10},{9,11},{10,... | collective-permute-start | bytes 3145736 | tf_op jit(solution)/shard_map/ppermute | solution.py:408
  501.0 45.5 %collective-permute-start.39 = (bf16[512,64]{0,1:T(8,128)(2,1)S(1)}, bf16[512,64]{0,1:T(8,128)(2,1)S(1)}, u32[]{:S(2)}, u32[]{:S(2)}) collective-permute-start(bf16[512,64]{0,1:T(8,128)(2,1)S(1)} %add_convert_fusion.3), channel_id=1, source_target_pairs={{0,2},{1,3},{2,0},{3,1},{4,6},{5,7},{6,4},{7,5},{8,10},{9,11},{10,... | collective-permute-start | bytes 196616 | tf_op jit(solution)/shard_map/ppermute | solution.py:313
  (38 other events, 943.6 us)

commit v2 on v1

v2 whole, which is shorter than its diff:
```python
import functools
import math

import jax
import jax.numpy as jnp
from jax import lax
from jax.experimental import pallas as pl
from jax.experimental.pallas import tpu as pltpu
from jax.sharding import PartitionSpec as P

HD = 128
CAPS = (2, 2, 2, 1)
F32 = jnp.float32
BF16 = jnp.bfloat16
SMEM = pltpu.MemorySpace.SMEM
VMEM = pltpu.MemorySpace.VMEM


def params(mib=32, **more):
    return pltpu.CompilerParams(vmem_limit_bytes=mib * 1024 * 1024, **more)


def attend_kernel(order, scale, place, seg_q, seg_k, q_ref, key_ref, value_ref, own_ref, *refs):
    hops = len(order)
    below, above = refs[:hops], refs[hops : 2 * hops]
    out_ref, bias, ones_beside, held, sems = refs[2 * hops :]
    tokens, group = q_ref.shape[0], q_ref.shape[1] // HD
    rows = own_ref.shape[0]
    slots = own_ref.shape[1] // (2 * HD)
    slot = pl.program_id(0)

    @pl.when(slot == 0)
    def _():
        pltpu.make_async_copy(own_ref, held.at[0], sems.at[0]).start()
        for step, choices in enumerate(order):
            for hop, from_below in sorted(set(choices)):
                here = functools.reduce(
                    jnp.logical_or,
                    [place[0] == i for i, c in enumerate(choices) if c == (hop, from_below)],
                )

                @pl.when(here)
                def _(ref=(below if from_below else above)[hop - 1], to=step + 1):
                    pltpu.make_async_copy(ref, held.at[to], sems.at[to]).start()

        same = seg_q[:, 0:1] == seg_k[0:1, :]
        last = seg_q[:, 1:2]
        where_k = lax.broadcasted_iota(jnp.int32, bias.shape, 1)
        bias[...] = jnp.where(same & (where_k <= last), 0.0, -1e30)
        ones_beside[:, HD:] = jnp.ones((ones_beside.shape[0], HD), BF16)
        for i in range(hops + 1):
            pltpu.make_async_copy(own_ref, held.at[i], sems.at[i]).wait()

    key_at = pl.ds(pl.multiple_of(slot * HD, HD), HD)
    value_at = pl.ds(pl.multiple_of((slots + slot) * HD, HD), HD)
    ones_beside[:tokens, :HD] = value_ref[...]
    for i in range(hops + 1):
        ones_beside[tokens + i * rows : tokens + (i + 1) * rows, :HD] = held[i, :, value_at]
    dims = (((1,), (1,)), ((), ()))
    factor = scale * math.log2(math.e)
    for h in range(group):
        q = q_ref[:, h * HD : (h + 1) * HD]
        peak = None
        for i in range(hops + 2):
            keys = key_ref[...] if i == 0 else held[i - 1, :, key_at]
            s = lax.dot_general(q, keys, dims, preferred_element_type=F32)
            if i == 0:
                s = s + bias[...]
                at = slice(0, tokens)
            else:
                at = slice(tokens + (i - 1) * rows, tokens + i * rows)
            high = jnp.max(s, axis=1, keepdims=True)
            high = high if peak is None else jnp.maximum(peak, high)
            w = jnp.exp2((s - high) * factor)
            o = jnp.dot(w.astype(BF16), ones_beside[at, :], preferred_element_type=F32)
            summed = o if peak is None else summed * jnp.exp2((peak - high) * factor) + o
            peak = high
        out_ref[:, h * HD : (h + 1) * HD] = (summed[:, :HD] / summed[:, HD:]).astype(BF16)


def attend(z, q, seg_q, seg_k, keys, values, own, below, above):
    tokens, width = q.shape
    rows = own.shape[0]
    slots = own.shape[1] // (2 * HD)
    wide = width // slots
    order = prefix_order(len(below) + 1)
    n_keys = tokens + (len(below) + 1) * rows
    anywhere = pl.BlockSpec(memory_space=pl.ANY)
    return pl.pallas_call(
        functools.partial(attend_kernel, order, 1.0 / math.sqrt(HD)),
        grid=(slots,),
        out_shape=jax.ShapeDtypeStruct((tokens, width), BF16),
        in_specs=[
            pl.BlockSpec(memory_space=SMEM),
            pl.BlockSpec((tokens, 2), lambda s: (0, 0)),
            pl.BlockSpec((1, tokens), lambda s: (0, 0)),
            pl.BlockSpec((tokens, wide), lambda s: (0, s)),
            pl.BlockSpec((tokens, HD), lambda s: (0, s)),
            pl.BlockSpec((tokens, HD), lambda s: (0, s)),
            anywhere,
        ]
        + [anywhere] * (2 * len(below)),
        out_specs=pl.BlockSpec((tokens, wide), lambda s: (0, s)),
        scratch_shapes=[
            pltpu.VMEM((tokens, tokens), F32),
            pltpu.VMEM((n_keys, 2 * HD), BF16),
            pltpu.VMEM((len(below) + 1,) + own.shape, BF16),
            pltpu.SemaphoreType.DMA((len(below) + 1,)),
        ],
        compiler_params=params(44),
        cost_estimate=pl.CostEstimate(
            flops=8 * tokens * n_keys * width, bytes_accessed=4 * tokens * width, transcendentals=0
        ),
        name="attend",
    )(z, seg_q, seg_k, q, keys, values, own, *below, *above)


def project_kernel(which, a_ref, w_ref, out_ref):
    out_ref[...] = jnp.dot(a_ref[...], w_ref[...], preferred_element_type=F32).astype(BF16)


def project(a, w, block, count):
    rows, depth = a.shape
    wide = w.shape[1] // count
    tile = min(1024, wide)
    steps = wide // tile
    return pl.pallas_call(
        project_kernel,
        out_shape=jax.ShapeDtypeStruct((rows, wide), BF16),
        grid_spec=pltpu.PrefetchScalarGridSpec(
            num_scalar_prefetch=1,
            grid=(steps,),
            in_specs=[
                pl.BlockSpec((rows, depth), lambda j, which: (0, 0)),
                pl.BlockSpec((depth, tile), lambda j, which: (0, which[0] * steps + j)),
            ],
            out_specs=pl.BlockSpec((rows, tile), lambda j, which: (0, j)),
        ),
        compiler_params=params(32),
        cost_estimate=pl.CostEstimate(
            flops=2 * rows * depth * wide, bytes_accessed=2 * depth * wide, transcendentals=0
        ),
        name="project",
    )(block, a, w)


def most_slots(n_dp, requests):
    return sum(CAPS) + requests * (n_dp - 1) + n_dp


def schedule_kernel(n_dp, requests, per, idx_ref, z_ref, out_ref):
    limit = most_slots(n_dp, requests)
    links = n_dp - 1
    idx = idx_ref[...]
    shape = idx.shape
    z = z_ref[0]
    lane = lax.broadcasted_iota(jnp.int32, shape, 1)
    row = lax.broadcasted_iota(jnp.int32, shape, 0)
    link = lax.broadcasted_iota(jnp.int32, (links,) + shape, 0)
    valid = (lane < n_dp * requests) & (row < 4)
    down = (row % 2) == 1
    taker = lane // requests
    holder = idx // per
    local = idx % per
    own = valid & (taker == holder)
    dst = jnp.where(down, n_dp - 1 - taker, taker)
    src = jnp.where(down, n_dp - 1 - holder, holder)
    me = jnp.where(down, n_dp - 1 - z, z)
    moving = valid & (src < dst)
    dst = jnp.where(moving, dst, 0)
    pos = jnp.where(moving, src, 0)
    rank = dst * 256 + 255 - lane
    zero = jnp.zeros(shape, jnp.int32)

    def one_round(first, slots, pos, came, codes):
        can = (pos[None] == link) & (dst[None] > link)
        code = jnp.where(src == me, local, per + came)
        moved = zero
        for slot in range(slots):
            key = jnp.where(can, rank[None], -1)
            best = jnp.max(key, axis=2, keepdims=True)
            chosen = can & (key == best)
            can = can & ~chosen
            sent = jnp.sum(jnp.where(chosen & (link == me[None]), code[None], 0), axis=0)
            codes = jnp.where(lane == first + slot, jnp.sum(sent, axis=1, keepdims=True), codes)
            got = jnp.sum(jnp.where(chosen & (link + 1 == me[None]), 1, 0), axis=0)
            came = jnp.where(got > 0, first + slot, came)
            moved = moved + jnp.sum(jnp.where(chosen, 1, 0), axis=0)
        return pos + moved, came, codes

    came, codes = zero, zero
    first = 0
    for slots in CAPS:
        pos, came, codes = one_round(first, slots, pos, came, codes)
        first += slots

    def left(pos):
        return jnp.max(jnp.where(pos < dst, 1, 0))

    def later(carry):
        k, _, pos, came, codes = carry
        pos, came, codes = one_round(k, 1, pos, came, codes)
        return k + 1, left(pos), pos, came, codes

    used, _, _, came, codes = lax.while_loop(
        lambda c: (c[1] > 0) & (c[0] < limit), later, (jnp.int32(first), left(pos), pos, came, codes)
    )
    place = jnp.where(own & (row == 0), local, 0)
    place = place + jnp.where(moving & (row == 0), per + came, 0)
    place = place + jnp.where(moving & (row == 1), per + limit + came, 0)
    place = jnp.sum(jnp.where(row < 2, place, 0), axis=0, keepdims=True)
    out = jnp.where(row < 2, codes, 0)
    out = jnp.where(row == 2, place, out)
    out_ref[...] = jnp.where(row == 3, used, out)


def make_schedule(n_dp, requests, per, idx_rows, z):
    return pl.pallas_call(
        functools.partial(schedule_kernel, n_dp, requests, per),
        out_shape=jax.ShapeDtypeStruct((8, 128), jnp.int32),
        in_specs=[pl.BlockSpec(memory_space=VMEM), pl.BlockSpec(memory_space=SMEM)],
        out_specs=pl.BlockSpec(memory_space=VMEM),
        name="schedule",
    )(idx_rows, z)


def slots_of(came):
    return [(r, j) for r, ref in enumerate(came) for j in range(CAPS[r])]


def fetch(code, per, own, ups, downs, limit, out, sems):
    rank = own[0].shape[1]

    @pl.when(code < per)
    def _():
        at = jnp.minimum(code, per - 1)
        for half in range(2):
            to = out.at[half * rank : (half + 1) * rank]
            pltpu.make_async_copy(own[half].at[at], to, sems.at[half]).start()

    for base, came in ((per, ups), (per + limit, downs)):
        for k, (r, j) in enumerate(slots_of(came)):

            @pl.when(code == base + k)
            def _(ref=came[r], j=j):
                for half in range(2):
                    part = slice(half * rank, (half + 1) * rank)
                    pltpu.make_async_copy(ref.at[j, part], out.at[part], sems.at[half]).start()


def fetched(own, out, sems):
    rank = own[0].shape[1]
    for half in range(2):
        to = out.at[half * rank : (half + 1) * rank]
        pltpu.make_async_copy(own[half].at[0], to, sems.at[half]).wait()


def pick_kernel(first, count, per, limit, n_came, sched, down_ref, up_ref, *refs):
    ups, downs = refs[:n_came], refs[n_came : 2 * n_came]
    outs, sems = refs[2 * n_came : -1], refs[-1]
    own = (down_ref, up_ref)
    for i in range(count):
        for way, came in enumerate((ups, downs)):
            code = sched[way, first + i]
            fetch(code, per, own, came, (), limit, outs[way].at[i], sems.at[way, i])
    for i in range(count):
        for way in range(2):
            fetched(own, outs[way].at[i], sems.at[way, i])


def slot_shape(own):
    return (2 * own[0].shape[1], own[0].shape[2])


def pick_sends(sched, own, ups, downs, number, limit):
    count, first = CAPS[number], sum(CAPS[:number])
    anywhere = pl.BlockSpec(memory_space=pl.ANY)
    in_vmem = pl.BlockSpec(memory_space=VMEM)
    out = jax.ShapeDtypeStruct((count,) + slot_shape(own), BF16)
    return pl.pallas_call(
        functools.partial(pick_kernel, first, count, own[0].shape[0], limit, len(ups)),
        out_shape=[out] * 2,
        in_specs=[pl.BlockSpec(memory_space=SMEM)] + [anywhere] * (2 + 2 * len(ups)),
        out_specs=[in_vmem] * 2,
        scratch_shapes=[pltpu.SemaphoreType.DMA((2, count, 2))],
        compiler_params=params(16),
        name="pick",
    )(sched, *own, *ups, *downs)


def gather_kernel(per, limit, requests, n_came, sched, z, down_ref, up_ref, *refs):
    ups, downs = refs[:n_came], refs[n_came : 2 * n_came]
    out, sems = refs[-2], refs[-1]
    own = (down_ref, up_ref)
    for r in range(requests):
        code = sched[2, z[0] * requests + r]
        fetch(code, per, own, ups, downs, limit, out.at[r], sems.at[r])
    for r in range(requests):
        fetched(own, out.at[r], sems.at[r])


def gather_own(sched, z, own, ups, downs, requests, limit):
    anywhere = pl.BlockSpec(memory_space=pl.ANY)
    return pl.pallas_call(
        functools.partial(gather_kernel, own[0].shape[0], limit, requests, len(ups)),
        out_shape=jax.ShapeDtypeStruct((requests,) + slot_shape(own), BF16),
        in_specs=[pl.BlockSpec(memory_space=SMEM)] * 2 + [anywhere] * (2 + 2 * len(ups)),
        out_specs=pl.BlockSpec(memory_space=VMEM),
        scratch_shapes=[pltpu.SemaphoreType.DMA((requests, 2))],
        compiler_params=params(16),
        name="gather_own",
    )(sched, z, *own, *ups, *downs)


def later_rounds(sched, z, own, ups, downs, requests, limit, n_dp):
    up, down = line(n_dp)
    per = own[0].shape[0]
    made = sum(CAPS)
    spare = jnp.zeros((limit - made,) + slot_shape(own), BF16)
    up_all = jnp.concatenate([*ups, spare])
    down_all = jnp.concatenate([*downs, spare])

    def choose(code, came):
        at = jnp.minimum(code, per - 1)
        held = [lax.dynamic_index_in_dim(o, at, 0, keepdims=False) for o in own]
        passed = lax.dynamic_index_in_dim(came, jnp.clip(code - per, 0, limit - 1), 0, keepdims=False)
        return jnp.where(code < per, jnp.concatenate(held), passed)

    def step(carry):
        k, up_all, down_all = carry
        from_below = lax.ppermute(choose(sched[0, k], up_all), "dp", up)
        from_above = lax.ppermute(choose(sched[1, k], down_all), "dp", down)
        up_all = lax.dynamic_update_index_in_dim(up_all, from_below, k, 0)
        down_all = lax.dynamic_update_index_in_dim(down_all, from_above, k, 0)
        return k + 1, up_all, down_all

    _, up_all, down_all = lax.while_loop(
        lambda c: c[0] < sched[3, 0], step, (jnp.int32(made), up_all, down_all)
    )
    places = lax.dynamic_slice(sched, (2, z[0] * requests), (1, requests))[0]
    picked = []
    for r in range(requests):
        code = places[r]
        below = choose(code, up_all)
        above = lax.dynamic_index_in_dim(
            down_all, jnp.clip(code - per - limit, 0, limit - 1), 0, keepdims=False
        )
        picked.append(jnp.where(code >= per + limit, above, below))
    return jnp.stack(picked)


def line(n):
    return [(i, i + 1) for i in range(n - 1)], [(i + 1, i) for i in range(n - 1)]


def bring_adapters(sched, z, own, requests, n_dp):
    up, down = line(n_dp)
    limit = most_slots(n_dp, requests)
    ups, downs = [], []
    for number in range(len(CAPS)):
        sends = pick_sends(sched, own, ups, downs, number, limit)
        ups.append(lax.ppermute(sends[0], "dp", up))
        downs.append(lax.ppermute(sends[1], "dp", down))
    return lax.cond(
        sched[3, 0] > sum(CAPS),
        lambda: later_rounds(sched, z, own, ups, downs, requests, limit, n_dp),
        lambda: gather_own(sched, z, own, ups, downs, requests, limit),
    )


def by_core(n):
    return [(i, i ^ 1) for i in range(n)]


def by_chip(n):
    return [(i, i ^ 2) for i in range(n)]


def added(a, b):
    return (a.astype(F32) + b.astype(F32)).astype(BF16)


def all_sum(x, n_tensor):
    if n_tensor != 4:
        return lax.psum(x, "tensor")
    x = added(x, lax.ppermute(x, "tensor", by_core(n_tensor)))
    return added(x, lax.ppermute(x, "tensor", by_chip(n_tensor)))


def prefix_order(n):
    table = []
    for z in range(n):
        seen = []
        for hop in range(1, n):
            seen += [(hop, True)] if hop <= z else []
            seen += [(hop, False)] if hop <= n - 1 - z else []
        table.append(seen)
    return [[table[z][s] for z in range(n)] for s in range(n - 1)]


def per_device(
    n_groups,
    n_dp,
    n_tensor,
    queries,
    suffix_rotated_key_slots,
    suffix_value_slots,
    shared_prefix_key_slots,
    shared_prefix_value_slots,
    lengths,
    request_adapter_index,
    output_weight_matrix,
    adapter_down_factors,
    adapter_up_factors,
):
    tokens, width = queries.shape
    requests = lengths.shape[1]
    per = adapter_down_factors.shape[0]
    zi = lax.axis_index("dp").astype(jnp.int32)
    z = zi.reshape(1)
    ti = lax.axis_index("tensor").astype(jnp.int32)
    up, down = line(n_dp)

    everyone = lax.all_gather(request_adapter_index, ("groups", "dp"), axis=0, tiled=True)
    everyone = jnp.pad(everyone.reshape(n_groups, -1), ((0, 0), (0, 128 - n_dp * requests)))
    gi = lax.axis_index("groups")
    mine = lax.dynamic_index_in_dim(everyone, gi, 0)
    other = lax.dynamic_index_in_dim(everyone, (gi + 1) % n_groups, 0)
    idx_rows = jnp.concatenate([mine, mine, other, other, jnp.zeros((4, 128), jnp.int32)], axis=0)

    own_rows = jnp.concatenate([shared_prefix_key_slots, shared_prefix_value_slots], axis=1)
    below, above = [own_rows], [own_rows]
    for hop in range(1, n_dp):
        below.append(lax.ppermute(below[-1], "dp", up[hop - 1 :]))
        above.append(lax.ppermute(above[-1], "dp", down[: n_dp - hop]))

    position = jnp.arange(tokens, dtype=jnp.int32)
    seg_ends = jnp.cumsum(lengths[0])
    request_of = jnp.sum((position[:, None] >= seg_ends[None, :]).astype(jnp.int32), axis=1)
    seg_q = jnp.stack([request_of, position], axis=1)
    seg_k = request_of[None]

    down_rows = jnp.transpose(adapter_down_factors, (0, 2, 1))
    idx_rows, _ = lax.optimization_barrier((idx_rows, (below[1], above[1])))
    sched = make_schedule(n_dp, requests, per, idx_rows, z)
    picked = bring_adapters(sched, z, (down_rows, adapter_up_factors), requests, n_dp)
    rank = picked.shape[1] // 2
    picked_down, picked_up = picked[:, :rank], picked[:, rank:]

    attended = attend(
        z,
        queries,
        seg_q,
        seg_k,
        suffix_rotated_key_slots,
        suffix_value_slots,
        own_rows,
        below[1:],
        above[1:],
    )
    if n_tensor == 4:
        far_other, far_same, near_other, near_same = (
            project(attended, output_weight_matrix, (ti ^ m).reshape(1), n_tensor)
            for m in (3, 2, 1, 0)
        )
        core, chip = by_core(n_tensor), by_chip(n_tensor)
        send = added(far_same, lax.ppermute(far_other, "tensor", core))
        arriving = lax.ppermute(send, "tensor", chip)
        near = near_same.astype(F32) + lax.ppermute(near_other, "tensor", core).astype(F32)
        base = near + arriving.astype(F32)
    else:
        whole = project(attended, output_weight_matrix, jnp.zeros((1,), jnp.int32), 1)
        share = lax.psum_scatter(whole, "tensor", scatter_dimension=1, tiled=True)
        base = share.astype(F32)

    select = request_of[:, None] == jnp.arange(requests, dtype=jnp.int32)[None, :]
    first = lax.dot_general(
        attended,
        picked_down.reshape(-1, width),
        (((1,), (1,)), ((), ())),
        preferred_element_type=F32,
    ).reshape(tokens, requests, -1)
    partial_shrink = jnp.sum(jnp.where(select[:, :, None], first, 0.0), axis=1).astype(BF16)
    shrink = all_sum(partial_shrink, n_tensor)
    spread = jnp.where(select[:, :, None], shrink[:, None, :], 0).reshape(tokens, -1)
    expand = jnp.dot(
        spread, picked_up.reshape(spread.shape[1], -1), preferred_element_type=F32
    )
    return (base + expand).astype(BF16)


def solution(mesh):
    return jax.shard_map(
        functools.partial(
            per_device, mesh.shape["groups"], mesh.shape["dp"], mesh.shape["tensor"]
        ),
        mesh=mesh,
        in_specs=(
            P(("groups", "dp"), "tensor"),
            P(("groups", "dp"), "tensor"),
            P(("groups", "dp"), "tensor"),
            P(("groups", "dp"), "tensor"),
            P(("groups", "dp"), "tensor"),
            P(("groups", "dp"), None),
            P(("groups", "dp"), None),
            P("tensor", None),
            P("dp", "tensor", None),
            P("dp", None, "tensor"),
        ),
        out_specs=P(("groups", "dp"), "tensor"),
        check_vma=False,
    )
```

time: 553 us -> 229 us (0.41)
  Pallas kernels: 356 us -> 75.7 us
  starting transfers between devices: 110 us -> 35.9 us
  blocking collectives: 0 us -> 25.9 us
  waiting for transfers between devices: 60.7 us -> 72.7 us
    pallas_call x14 -> x6, Pallas kernels: 304 us -> 43.2 us  [the longest x1 28.2 us: attend(): pl.pallas_call(functools.partial(attend_kernel, order, 1.0 / math.sqrt(HD...]
    ppermute x16 -> x6, starting transfers between devices: 49.5 us -> 11.7 us  [the longest x3 7.9 us: per_device(): below.append(lax.ppermute(below[-1], 'dp', up[hop - 1:]))]
    ppermute x16 -> x6, waiting for transfers between devices: 3.69 us -> 31.1 us  [the longest x3 31.1 us: per_device(): above.append(lax.ppermute(above[-1], 'dp', down[:n_dp - hop]))]
    all_gather x0 -> x1, blocking collectives: none -> 25.9 us  [per_device(): lax.all_gather(request_adapter_index, ('groups', 'dp'), axis=0, tiled=True)]
    ppermute x12 -> x4, starting transfers between devices: 39.9 us -> 15.6 us  [bring_adapters(): ups.append(lax.ppermute(sends[0], 'dp', up))]
    pallas_call x8 -> x4, Pallas kernels: 46.7 us -> 29.9 us  [project(): pl.pallas_call(project_kernel, out_shape=jax.ShapeDtypeStruct((rows, wide...]
    ppermute x1, waiting for transfers between devices: 38.4 us -> 22.9 us  [all_sum(): return added(x, lax.ppermute(x, 'tensor', by_chip(n_tensor)))]
    ppermute x12 -> x4, starting transfers between devices: 15.8 us -> 5.13 us  [bring_adapters(): downs.append(lax.ppermute(sends[1], 'dp', down))]
  transfers between devices with their start and end apart: 48 -> 19, of which waited for: 11 -> 8; matrix products, arithmetic and copies ran while one was open for 2% -> 4% of each run, Pallas kernels for 51% -> 31%
where the time goes in v2:
time: 229 us
  Pallas kernels  75.7 us (33%)
  waiting for transfers between devices  72.7 us (32%)
  starting transfers between devices  35.9 us (16%)
  blocking collectives  25.9 us (11%)
  other arithmetic  10 us (4%)
  local copies, waits for them, and re-layouts  4.52 us (2%)
  matrix products  2.73 us (1%)
    ppermute x3, waiting for transfers between devices, per_device(): above.append(lax.ppermute(above[-1], 'dp', down[:n_dp - hop]))  31.1 us
    pallas_call x4, Pallas kernels, project(): pl.pallas_call(project_kernel, out_shape=jax.ShapeDtypeStruct((rows, wide...  29.9 us
    pallas_call x1, Pallas kernels, attend(): pl.pallas_call(functools.partial(attend_kernel, order, 1.0 / math.sqrt(HD...  28.2 us
    all_gather x1, blocking collectives, per_device(): lax.all_gather(request_adapter_index, ('groups', 'dp'), axis=0, tiled=True)  25.9 us
    ppermute x1, waiting for transfers between devices, all_sum(): return added(x, lax.ppermute(x, 'tensor', by_chip(n_tensor)))  22.9 us
    ppermute x4, starting transfers between devices, bring_adapters(): ups.append(lax.ppermute(sends[0], 'dp', up))  15.6 us
    pallas_call x4, Pallas kernels, pick_sends(): pl.pallas_call(functools.partial(pick_kernel, first, count, own[0].shape[...  11.3 us
    ppermute x4, waiting for transfers between devices, bring_adapters(): downs.append(lax.ppermute(sends[1], 'dp', down))  9.23 us
  transfers between devices with their start and end apart: 19, of which 8 were waited for; matrix products, arithmetic and copies ran while one was open for 4% of the time, Pallas kernels for 31%

profile of v2, /device:TPU:0, one launch (start us, length us, event | category | flops | bytes accessed | tf_op | source)
XLA Modules:
  0.0 228.5 jit_solution(4071429701667309782)
XLA Ops:
  1.9 5.0 %collective-permute-start.2 = (bf16[512,512]{1,0:T(8,128)(2,1)S(1)}, bf16[512,512]{1,0:T(8,128)(2,1)S(1)}, u32[]{:S(2)}, u32[]{:S(2)}) collective-permute-start(bf16[512,512]{1,0:T(8,128)(2,1)S(1)} %constant_dynamic-update-slice_fusion.8.own_ref), channel_id=1, source_target_pairs={{0,4},{4,8},{8,12},{1,5},{5,9},{9,13},{2,6},{6,10},{10,14},{3,7},{... | collective-permute-start | bytes 1572872 | tf_op jit(solution)/shard_map/ppermute | solution.py:434
  8.2 25.9 %all-gather = s32[8,1,4]{2,1,0:T(1,128)S(1)} all-gather(s32[1,1,4]{2,1,0:T(1,128)} %bitcast.91), channel_id=1, replica_groups=mesh['groups'=2,'dp'=4,'tensor'=4] {'groups','dp'}, dimensions={0}, use_global_device_ids=true | all-gather | bytes 144 | tf_op jit(solution)/shard_map/all_gather | solution.py:424
  36.1 2.6 %schedule.1.sched = s32[8,128]{1,0:T(8,128)} custom-call(s32[8,128]{1,0:T(8,128)} %concatenate.43.idx_ref, s32[1]{0:T(128)} %bitcast.36.place.z_ref), custom_call_target="tpu_custom_call" | custom-call | tf_op jit(solution)/shard_map/schedule/pallas_call | solution.py:218
  38.7 2.6 %pick.4 = (bf16[2,128,2048]{2,1,0:T(8,128)(2,1)S(1)}, bf16[2,128,2048]{2,1,0:T(8,128)(2,1)S(1)}) custom-call(s32[8,128]{1,0:T(8,128)} %schedule.1.sched, bf16[16,64,2048]{2,1,0:T(8,128)(2,1)} %bitcast.47.down_ref, bf16[16,64,2048]{2,1,0:T(8,128)(2,1)} %up_ref.7), custom_call_target="tpu_custom_call" | custom-call | tf_op jit(solution)/shard_map/pick/pallas_call | solution.py:280
  41.3 5.0 %collective-permute-start.11 = (bf16[2,128,2048]{2,1,0:T(8,128)(2,1)S(1)}, bf16[2,128,2048]{2,1,0:T(8,128)(2,1)}, u32[]{:S(2)}, u32[]{:S(2)}) collective-permute-start(bf16[2,128,2048]{2,1,0:T(8,128)(2,1)S(1)} %get-tuple-element.190), channel_id=1, source_target_pairs={{0,4},{4,8},{8,12},{1,5},{5,9},{9,13},{2,6},{6,10},{10,14},{3,7},{... | collective-permute-start | bytes 3145736 | tf_op jit(solution)/shard_map/ppermute | solution.py:362
  47.6 1.5 collective-permute-start.3
  50.3 1.5 collective-permute-start.4
  51.8 28.8 %collective-permute-done.6.refs_4_ = bf16[512,512]{1,0:T(8,128)(2,1)} collective-permute-done((bf16[512,512]{1,0:T(8,128)(2,1)S(1)}, bf16[512,512]{1,0:T(8,128)(2,1)}, u32[]{:S(2)}, u32[]{:S(2)}) %collective-permute-start.6) | collective-permute-done | bytes 524320 | tf_op jit(solution)/shard_map/ppermute | solution.py:435
  82.5 2.7 %pick.5 = (bf16[2,128,2048]{2,1,0:T(8,128)(2,1)S(1)}, bf16[2,128,2048]{2,1,0:T(8,128)(2,1)S(1)}) custom-call(s32[8,128]{1,0:T(8,128)} %schedule.1.sched, bf16[16,64,2048]{2,1,0:T(8,128)(2,1)} %bitcast.47.down_ref, bf16[16,64,2048]{2,1,0:T(8,128)(2,1)} %up_ref.7, bf16[2,128,2048]{2,1,0:T(8,128)(2,1)} %collective-permute-done.11.refs_0_, ...), custom_call_target="tpu_custom_call" | custom-call | tf_op jit(solution)/shard_map/pick/pallas_call | solution.py:280
  85.2 6.0 %collective-permute-start.13 = (bf16[2,128,2048]{2,1,0:T(8,128)(2,1)S(1)}, bf16[2,128,2048]{2,1,0:T(8,128)(2,1)}, u32[]{:S(2)}, u32[]{:S(2)}) collective-permute-start(bf16[2,128,2048]{2,1,0:T(8,128)(2,1)S(1)} %get-tuple-element.192), channel_id=1, source_target_pairs={{0,4},{4,8},{8,12},{1,5},{5,9},{9,13},{2,6},{6,10},{10,14},{3,7},{... | collective-permute-start | bytes 3145736 | tf_op jit(solution)/shard_map/ppermute | solution.py:362
  92.5 2.3 %collective-permute-done.7.refs_5_ = bf16[512,512]{1,0:T(8,128)(2,1)} collective-permute-done((bf16[512,512]{1,0:T(8,128)(2,1)}, bf16[512,512]{1,0:T(8,128)(2,1)}, u32[]{:S(2)}, u32[]{:S(2)}) %collective-permute-start.7) | collective-permute-done | bytes 524320 | tf_op jit(solution)/shard_map/ppermute | solution.py:435
  94.8 28.2 %attend.1.a_ref = bf16[512,2048]{1,0:T(8,128)(2,1)S(1)} custom-call(s32[1]{0:T(128)} %bitcast.36.place.z_ref, s32[512,2]{1,0:T(8,128)S(1)} %copy.13.seg_q, s32[1,512]{1,0:T(1,128)S(1)} %bitcast.90, bf16[512,2048]{1,0:T(8,128)(2,1)S(1)} %copy-done, bf16[512,256]{1,0:T(8,128)(2,1)S(1)} %copy-done.4, bf16[512,256]{1,0:T(8,128)(2,1)S(1)} %copy-done.5, ...), custom_call_target="tpu_custom_call" | custom-call | flops 21474836480 | bytes 4194304 | tf_op jit(solution)/shard_map/attend/pallas_call | solution.py:89
  123.0 7.9 %project.7 = bf16[512,2048]{1,0:T(8,128)(2,1)} custom-call(s32[1]{0:T(128)} %bitcast.43.which, bf16[512,2048]{1,0:T(8,128)(2,1)S(1)} %attend.1.a_ref, bf16[2048,8192]{1,0:T(8,128)(2,1)} %w_ref.7), custom_call_target="tpu_custom_call" | custom-call | flops 4294967296 | bytes 8388608 | tf_op jit(solution)/shard_map/project/pallas_call | solution.py:127
  130.9 4.0 %pick.6 = (bf16[2,128,2048]{2,1,0:T(8,128)(2,1)}, bf16[2,128,2048]{2,1,0:T(8,128)(2,1)}) custom-call(s32[8,128]{1,0:T(8,128)} %schedule.1.sched, bf16[16,64,2048]{2,1,0:T(8,128)(2,1)} %bitcast.47.down_ref, bf16[16,64,2048]{2,1,0:T(8,128)(2,1)} %up_ref.7, bf16[2,128,2048]{2,1,0:T(8,128)(2,1)} %collective-permute-done.11.refs_0_, ...), custom_call_target="tpu_custom_call" | custom-call | tf_op jit(solution)/shard_map/pick/pallas_call | solution.py:280
  134.9 3.1 %collective-permute-start.15 = (bf16[2,128,2048]{2,1,0:T(8,128)(2,1)}, bf16[2,128,2048]{2,1,0:T(8,128)(2,1)}, u32[]{:S(2)}, u32[]{:S(2)}) collective-permute-start(bf16[2,128,2048]{2,1,0:T(8,128)(2,1)} %get-tuple-element.194), channel_id=1, source_target_pairs={{0,4},{4,8},{8,12},{1,5},{5,9},{9,13},{2,6},{6,10},{10,14},{3,7},{... | collective-permute-start | bytes 3145736 | tf_op jit(solution)/shard_map/ppermute | solution.py:362
  139.3 7.9 %project.5 = bf16[512,2048]{1,0:T(8,128)(2,1)} custom-call(s32[1]{0:T(128)} %bitcast.41.which, bf16[512,2048]{1,0:T(8,128)(2,1)S(1)} %attend.1.a_ref, bf16[2048,8192]{1,0:T(8,128)(2,1)} %w_ref.7), custom_call_target="tpu_custom_call" | custom-call | flops 4294967296 | bytes 8388608 | tf_op jit(solution)/shard_map/project/pallas_call | solution.py:127
  147.5 7.0 %project.6 = bf16[512,2048]{1,0:T(8,128)(2,1)S(1)} custom-call(s32[1]{0:T(128)} %bitcast.42.which, bf16[512,2048]{1,0:T(8,128)(2,1)S(1)} %attend.1.a_ref, bf16[2048,8192]{1,0:T(8,128)(2,1)} %w_ref.7), custom_call_target="tpu_custom_call" | custom-call | flops 4294967296 | bytes 8388608 | tf_op jit(solution)/shard_map/project/pallas_call | solution.py:127
  154.5 5.9 %collective-permute-done.15.refs_2_ = bf16[2,128,2048]{2,1,0:T(8,128)(2,1)} collective-permute-done((bf16[2,128,2048]{2,1,0:T(8,128)(2,1)}, bf16[2,128,2048]{2,1,0:T(8,128)(2,1)}, u32[]{:S(2)}, u32[]{:S(2)}) %collective-permute-start.15) | collective-permute-done | bytes 1048608 | tf_op jit(solution)/shard_map/ppermute | solution.py:362
  160.5 5.1 %collective-permute-done.16.refs_5_ = bf16[2,128,2048]{2,1,0:T(8,128)(2,1)} collective-permute-done((bf16[2,128,2048]{2,1,0:T(8,128)(2,1)}, bf16[2,128,2048]{2,1,0:T(8,128)(2,1)}, u32[]{:S(2)}, u32[]{:S(2)}) %collective-permute-start.16) | collective-permute-done | bytes 1048608 | tf_op jit(solution)/shard_map/ppermute | solution.py:363
  165.5 2.0 pick.7
  167.5 1.5 collective-permute-start.17
  170.3 3.9 %add_convert_fusion = bf16[512,2048]{1,0:T(8,128)(2,1)} fusion(bf16[512,2048]{1,0:T(8,128)(2,1)} %collective-permute-done.9, bf16[512,2048]{1,0:T(8,128)(2,1)S(1)} %project.6), kind=kLoop, calls=%fused_computation.40 | loop fusion | flops 4194304 | bytes 6291456 | tf_op jit(solution)/shard_map/convert_element_type | solution.py:380
  174.2 1.5 collective-permute-start.10
  177.6 2.2 collective-permute-done.17
  179.8 4.1 %collective-permute-done.18 = bf16[1,128,2048]{2,1,0:T(8,128)(2,1)S(1)} collective-permute-done((bf16[1,128,2048]{2,1,0:T(8,128)(2,1)S(1)}, bf16[1,128,2048]{2,1,0:T(8,128)(2,1)S(1)}, u32[]{:S(2)}, u32[]{:S(2)}) %collective-permute-start.18) | collective-permute-done | bytes 524320 | tf_op jit(solution)/shard_map/ppermute | solution.py:363
  184.0 3.7 %conditional.1 = (bf16[4,128,2048]{2,1,0:T(8,128)(2,1)}) conditional(s32[]{:T(128)} %bitcast.46, (s32[8,128]{1,0:T(8,128)}, s32[1]{0:T(128)}, bf16[16,64,2048]{2,1,0:T(8,128)(2,1)}, bf16[16,64,2048]{2,1,0:T(8,128)(2,1)}, bf16[2,128,2048]{2,1,0:T(8,128)(2,1)}, /*index=5*/bf16[2,128,2048]{2,1,0:T(8,128)(2,1)}, bf16[2,128,2048]{2,1,0:T(8,128)(2,1)}, ...), branch_computations={%region_2.3_spmd, %region_3.6_spmd} | conditional | flops 12058699 | bytes 111150632 | solution.py:364
  184.0 3.7 %gather_own.1 = bf16[4,128,2048]{2,1,0:T(8,128)(2,1)} custom-call(s32[8,128]{1,0:T(8,128)} %get-tuple-element.146.sched, s32[1]{0:T(128)} %get-tuple-element.147.z, bf16[16,64,2048]{2,1,0:T(8,128)(2,1)} %get-tuple-element.148.down_ref, bf16[16,64,2048]{2,1,0:T(8,128)(2,1)} %get-tuple-element.149.up_ref, bf16[2,128,2048]{2,1,0:T(8,128)(2,1)} %get-tuple-element.150.refs_0_, ...), custom_call_target="tpu_custom_call" | custom-call | tf_op jit(solution)/shard_map/cond/branch_0_fun/gather_own/pallas_call | solution.py:304
  187.6 2.0 fusion.10
  191.0 1.6 collective-permute-start.20
  192.6 7.1 %project.4 = bf16[512,2048]{1,0:T(8,128)(2,1)S(1)} custom-call(s32[1]{0:T(128)} %bitcast.35.which, bf16[512,2048]{1,0:T(8,128)(2,1)S(1)} %attend.1.a_ref, bf16[2048,8192]{1,0:T(8,128)(2,1)} %w_ref.7), custom_call_target="tpu_custom_call" | custom-call | flops 4294967296 | bytes 8388608 | tf_op jit(solution)/shard_map/project/pallas_call | solution.py:127
  199.7 22.9 %collective-permute-done.20 = bf16[512,64]{0,1:T(8,128)(2,1)S(1)} collective-permute-done((bf16[512,64]{0,1:T(8,128)(2,1)S(1)}, bf16[512,64]{0,1:T(8,128)(2,1)S(1)}, u32[]{:S(2)}, u32[]{:S(2)}) %collective-permute-start.20) | collective-permute-done | bytes 65568 | tf_op jit(solution)/shard_map/ppermute | solution.py:387
  223.4 5.1 %fusion.4 = bf16[512,2048]{1,0:T(8,128)(2,1)} fusion(f32[512,2048,1]{1,0,2:T(8,128)S(1)} %fusion.13, bf16[512,2048]{1,0:T(8,128)(2,1)} %collective-permute-done.10, bf16[512,2048]{1,0:T(8,128)(2,1)} %collective-permute-done.8, bf16[512,2048]{1,0:T(8,128)(2,1)S(1)} %project.4), kind=kLoop, calls=%fused_computation.39 | loop fusion | flops 7340032 | bytes 12582912 | tf_op jit(solution)/shard_map/convert_element_type | solution.py:489
  (56 shorter events, 16.8 us)
Async XLA Ops:
  1.9 34.1 %collective-permute-start.2 = (bf16[512,512]{1,0:T(8,128)(2,1)S(1)}, bf16[512,512]{1,0:T(8,128)(2,1)S(1)}, u32[]{:S(2)}, u32[]{:S(2)}) collective-permute-start(bf16[512,512]{1,0:T(8,128)(2,1)S(1)} %constant_dynamic-update-slice_fusion.8.own_ref), channel_id=1, source_target_pairs={{0,4},{4,8},{8,12},{1,5},{5,9},{9,13},{2,6},{6,10},{10,14},{3,7},{... | collective-permute-start | bytes 1572872 | tf_op jit(solution)/shard_map/ppermute | solution.py:434
  6.9 29.1 %collective-permute-start.5 = (bf16[512,512]{1,0:T(8,128)(2,1)S(1)}, bf16[512,512]{1,0:T(8,128)(2,1)S(1)}, u32[]{:S(2)}, u32[]{:S(2)}) collective-permute-start(bf16[512,512]{1,0:T(8,128)(2,1)S(1)} %constant_dynamic-update-slice_fusion.8.own_ref), channel_id=1, source_target_pairs={{4,0},{8,4},{12,8},{5,1},{9,5},{13,9},{6,2},{10,6},{14,10},{7,3},{... | collective-permute-start | bytes 1572872 | tf_op jit(solution)/shard_map/ppermute | solution.py:435
  36.1 2.6 %copy-start.1 = (bf16[512,512]{1,0:T(8,128)(2,1)}, bf16[512,512]{1,0:T(8,128)(2,1)S(1)}, u32[]{:S(2)}) copy-start(bf16[512,512]{1,0:T(8,128)(2,1)S(1)} %collective-permute-done.5.refs_3_) | copy-start | bytes 1572868
  38.7 10.4 %copy-start.2 = (bf16[512,512]{1,0:T(8,128)(2,1)S(1)}, bf16[512,512]{1,0:T(8,128)(2,1)}, u32[]{:S(2)}) copy-start(bf16[512,512]{1,0:T(8,128)(2,1)} %copy-done.1) | copy-start | bytes 1572868
  38.7 43.3 %copy-start.11 = (s32[1,4]{1,0:T(1,128)S(1)}, s32[1,4]{1,0:T(1,128)}, u32[]{:S(2)}) copy-start(s32[1,4]{1,0:T(1,128)} %param.19) | copy-start | bytes 52
  41.3 41.1 %collective-permute-start.11 = (bf16[2,128,2048]{2,1,0:T(8,128)(2,1)S(1)}, bf16[2,128,2048]{2,1,0:T(8,128)(2,1)}, u32[]{:S(2)}, u32[]{:S(2)}) collective-permute-start(bf16[2,128,2048]{2,1,0:T(8,128)(2,1)S(1)} %get-tuple-element.190), channel_id=1, source_target_pairs={{0,4},{4,8},{8,12},{1,5},{5,9},{9,13},{2,6},{6,10},{10,14},{3,7},{... | collective-permute-start | bytes 3145736 | tf_op jit(solution)/shard_map/ppermute | solution.py:362
  46.3 36.2 %collective-permute-start.12 = (bf16[2,128,2048]{2,1,0:T(8,128)(2,1)S(1)}, bf16[2,128,2048]{2,1,0:T(8,128)(2,1)}, u32[]{:S(2)}, u32[]{:S(2)}) collective-permute-start(bf16[2,128,2048]{2,1,0:T(8,128)(2,1)S(1)} %get-tuple-element.191), channel_id=1, source_target_pairs={{4,0},{8,4},{12,8},{5,1},{9,5},{13,9},{6,2},{10,6},{14,10},{7,3},{... | collective-permute-start | bytes 3145736 | tf_op jit(solution)/shard_map/ppermute | solution.py:363
  47.6 2.8 %collective-permute-start.3 = (bf16[512,512]{1,0:T(8,128)(2,1)S(1)}, bf16[512,512]{1,0:T(8,128)(2,1)}, u32[]{:S(2)}, u32[]{:S(2)}) collective-permute-start(bf16[512,512]{1,0:T(8,128)(2,1)S(1)} %collective-permute-done.2.refs_0_), channel_id=1, source_target_pairs={{4,8},{8,12},{5,9},{9,13},{6,10},{10,14},{7,11},{11,15},{20,24},{2... | collective-permute-start | bytes 1572872 | tf_op jit(solution)/shard_map/ppermute | solution.py:434
  49.0 31.6 %collective-permute-start.6 = (bf16[512,512]{1,0:T(8,128)(2,1)S(1)}, bf16[512,512]{1,0:T(8,128)(2,1)}, u32[]{:S(2)}, u32[]{:S(2)}) collective-permute-start(bf16[512,512]{1,0:T(8,128)(2,1)S(1)} %copy-done.2), channel_id=1, source_target_pairs={{4,0},{8,4},{5,1},{9,5},{6,2},{10,6},{7,3},{11,7},{20,16},{24,20},... | collective-permute-start | bytes 1572872 | tf_op jit(solution)/shard_map/ppermute | solution.py:435
  50.3 42.2 %collective-permute-start.4 = (bf16[512,512]{1,0:T(8,128)(2,1)}, bf16[512,512]{1,0:T(8,128)(2,1)}, u32[]{:S(2)}, u32[]{:S(2)}) collective-permute-start(bf16[512,512]{1,0:T(8,128)(2,1)} %collective-permute-done.3.refs_1_), channel_id=1, source_target_pairs={{8,12},{9,13},{10,14},{11,15},{24,28},{25,29},{26,30},{27,31}} | collective-permute-start | bytes 1572872 | tf_op jit(solution)/shard_map/ppermute | solution.py:434
  80.6 14.2 %collective-permute-start.7 = (bf16[512,512]{1,0:T(8,128)(2,1)}, bf16[512,512]{1,0:T(8,128)(2,1)}, u32[]{:S(2)}, u32[]{:S(2)}) collective-permute-start(bf16[512,512]{1,0:T(8,128)(2,1)} %collective-permute-done.6.refs_4_), channel_id=1, source_target_pairs={{4,0},{5,1},{6,2},{7,3},{20,16},{21,17},{22,18},{23,19}} | collective-permute-start | bytes 1572872 | tf_op jit(solution)/shard_map/ppermute | solution.py:435
  82.4 12.4 %copy-start = (bf16[512,2048]{1,0:T(8,128)(2,1)S(1)}, bf16[512,2048]{1,0:T(8,128)(2,1)}, u32[]{:S(2)}) copy-start(bf16[512,2048]{1,0:T(8,128)(2,1)} %q_ref.1) | copy-start | bytes 6291460
  82.4 12.4 %copy-start.3 = (bf16[512,512]{1,0:T(8,128)(2,1)S(1)}, bf16[512,512]{1,0:T(8,128)(2,1)}, u32[]{:S(2)}) copy-start(bf16[512,512]{1,0:T(8,128)(2,1)} %copy-done.1) | copy-start | bytes 1572868
  82.4 12.4 %copy-start.4 = (bf16[512,256]{1,0:T(8,128)(2,1)S(1)}, bf16[512,256]{1,0:T(8,128)(2,1)}, u32[]{:S(2)}) copy-start(bf16[512,256]{1,0:T(8,128)(2,1)} %key_ref.1) | copy-start | bytes 786436
  82.4 12.4 %copy-start.5 = (bf16[512,256]{1,0:T(8,128)(2,1)S(1)}, bf16[512,256]{1,0:T(8,128)(2,1)}, u32[]{:S(2)}) copy-start(bf16[512,256]{1,0:T(8,128)(2,1)} %value_ref.1) | copy-start | bytes 786436
  85.2 45.7 %collective-permute-start.13 = (bf16[2,128,2048]{2,1,0:T(8,128)(2,1)S(1)}, bf16[2,128,2048]{2,1,0:T(8,128)(2,1)}, u32[]{:S(2)}, u32[]{:S(2)}) collective-permute-start(bf16[2,128,2048]{2,1,0:T(8,128)(2,1)S(1)} %get-tuple-element.192), channel_id=1, source_target_pairs={{0,4},{4,8},{8,12},{1,5},{5,9},{9,13},{2,6},{6,10},{10,14},{3,7},{... | collective-permute-start | bytes 3145736 | tf_op jit(solution)/shard_map/ppermute | solution.py:362
  91.2 39.7 %collective-permute-start.14 = (bf16[2,128,2048]{2,1,0:T(8,128)(2,1)S(1)}, bf16[2,128,2048]{2,1,0:T(8,128)(2,1)}, u32[]{:S(2)}, u32[]{:S(2)}) collective-permute-start(bf16[2,128,2048]{2,1,0:T(8,128)(2,1)S(1)} %get-tuple-element.193), channel_id=1, source_target_pairs={{4,0},{8,4},{12,8},{5,1},{9,5},{13,9},{6,2},{10,6},{14,10},{7,3},{... | collective-permute-start | bytes 3145736 | tf_op jit(solution)/shard_map/ppermute | solution.py:363
  130.9 39.4 %collective-permute-start.9 = (bf16[512,2048]{1,0:T(8,128)(2,1)}, bf16[512,2048]{1,0:T(8,128)(2,1)}, u32[]{:S(2)}, u32[]{:S(2)}) collective-permute-start(bf16[512,2048]{1,0:T(8,128)(2,1)} %project.7), channel_id=1, source_target_pairs={{0,1},{1,0},{2,3},{3,2},{4,5},{5,4},{6,7},{7,6},{8,9},{9,8},{10,11... | collective-permute-start | bytes 6291464 | tf_op jit(solution)/shard_map/ppermute | solution.py:467
  134.9 25.5 %collective-permute-start.15 = (bf16[2,128,2048]{2,1,0:T(8,128)(2,1)}, bf16[2,128,2048]{2,1,0:T(8,128)(2,1)}, u32[]{:S(2)}, u32[]{:S(2)}) collective-permute-start(bf16[2,128,2048]{2,1,0:T(8,128)(2,1)} %get-tuple-element.194), channel_id=1, source_target_pairs={{0,4},{4,8},{8,12},{1,5},{5,9},{9,13},{2,6},{6,10},{10,14},{3,7},{... | collective-permute-start | bytes 3145736 | tf_op jit(solution)/shard_map/ppermute | solution.py:362
  138.0 27.5 %collective-permute-start.16 = (bf16[2,128,2048]{2,1,0:T(8,128)(2,1)}, bf16[2,128,2048]{2,1,0:T(8,128)(2,1)}, u32[]{:S(2)}, u32[]{:S(2)}) collective-permute-start(bf16[2,128,2048]{2,1,0:T(8,128)(2,1)} %get-tuple-element.195), channel_id=1, source_target_pairs={{4,0},{8,4},{12,8},{5,1},{9,5},{13,9},{6,2},{10,6},{14,10},{7,3},{... | collective-permute-start | bytes 3145736 | tf_op jit(solution)/shard_map/ppermute | solution.py:363
  147.3 76.1 %collective-permute-start.8 = (bf16[512,2048]{1,0:T(8,128)(2,1)}, bf16[512,2048]{1,0:T(8,128)(2,1)}, u32[]{:S(2)}, u32[]{:S(2)}) collective-permute-start(bf16[512,2048]{1,0:T(8,128)(2,1)} %project.5), channel_id=1, source_target_pairs={{0,1},{1,0},{2,3},{3,2},{4,5},{5,4},{6,7},{7,6},{8,9},{9,8},{10,11... | collective-permute-start | bytes 6291464 | tf_op jit(solution)/shard_map/ppermute | solution.py:469
  167.5 12.3 %collective-permute-start.17 = (bf16[1,128,2048]{2,1,0:T(8,128)(2,1)S(1)}, bf16[1,128,2048]{2,1,0:T(8,128)(2,1)S(1)}, u32[]{:S(2)}, u32[]{:S(2)}) collective-permute-start(bf16[1,128,2048]{2,1,0:T(8,128)(2,1)S(1)} %get-tuple-element.196), channel_id=1, source_target_pairs={{0,4},{4,8},{8,12},{1,5},{5,9},{9,13},{2,6},{6,10},{10,14},{3,7},{... | collective-permute-start | bytes 1572872 | tf_op jit(solution)/shard_map/ppermute | solution.py:362
  169.0 15.0 %collective-permute-start.18 = (bf16[1,128,2048]{2,1,0:T(8,128)(2,1)S(1)}, bf16[1,128,2048]{2,1,0:T(8,128)(2,1)S(1)}, u32[]{:S(2)}, u32[]{:S(2)}) collective-permute-start(bf16[1,128,2048]{2,1,0:T(8,128)(2,1)S(1)} %get-tuple-element.197), channel_id=1, source_target_pairs={{4,0},{8,4},{12,8},{5,1},{9,5},{13,9},{6,2},{10,6},{14,10},{7,3},{... | collective-permute-start | bytes 1572872 | tf_op jit(solution)/shard_map/ppermute | solution.py:363
  174.2 49.2 %collective-permute-start.10 = (bf16[512,2048]{1,0:T(8,128)(2,1)}, bf16[512,2048]{1,0:T(8,128)(2,1)}, u32[]{:S(2)}, u32[]{:S(2)}) collective-permute-start(bf16[512,2048]{1,0:T(8,128)(2,1)} %add_convert_fusion), channel_id=1, source_target_pairs={{0,2},{1,3},{2,0},{3,1},{4,6},{5,7},{6,4},{7,5},{8,10},{9,11},{10,... | collective-permute-start | bytes 6291464 | tf_op jit(solution)/shard_map/ppermute | solution.py:468
  189.6 1.3 collective-permute-start.19
  191.0 31.6 %collective-permute-start.20 = (bf16[512,64]{0,1:T(8,128)(2,1)S(1)}, bf16[512,64]{0,1:T(8,128)(2,1)S(1)}, u32[]{:S(2)}, u32[]{:S(2)}) collective-permute-start(bf16[512,64]{0,1:T(8,128)(2,1)S(1)} %add_convert_fusion.2), channel_id=1, source_target_pairs={{0,2},{1,3},{2,0},{3,1},{4,6},{5,7},{6,4},{7,5},{8,10},{9,11},{10,... | collective-permute-start | bytes 196616 | tf_op jit(solution)/shard_map/ppermute | solution.py:387
  192.6 30.1 %copy-start.7 = (bf16[4,128,2048]{2,1,0:T(8,128)(2,1)S(1)}, bf16[4,128,2048]{2,1,0:T(8,128)(2,1)}, u32[]{:S(2)}) copy-start(bf16[4,128,2048]{2,1,0:T(8,128)(2,1)} %get-tuple-element.340) | copy-start | bytes 6291460

commit v3 on v2

--- a/solution.py
+++ b/solution.py
@@ -10,28 +10,65 @@
 
 HD = 128
 CAPS = (2, 2, 2, 1)
+PIECES = 4
+SMALL = pl.CostEstimate(flops=1, bytes_accessed=1, transcendentals=0)
 F32 = jnp.float32
 BF16 = jnp.bfloat16
 SMEM = pltpu.MemorySpace.SMEM
 VMEM = pltpu.MemorySpace.VMEM
 
 
+def cost(flops):
+    return pl.CostEstimate(flops=flops, bytes_accessed=1, transcendentals=0)
+
+
 def params(mib=32, **more):
     return pltpu.CompilerParams(vmem_limit_bytes=mib * 1024 * 1024, **more)
 
 
-def attend_kernel(order, scale, place, seg_q, seg_k, q_ref, key_ref, value_ref, own_ref, *refs):
+def attend_block(q, keys, values, bias, factor, peak, summed):
+    s = lax.dot_general(q, keys, (((1,), (1,)), ((), ())), preferred_element_type=F32)
+    if bias is not None:
+        s = s + bias
+    high = jnp.max(s, axis=1, keepdims=True)
+    high = high if peak is None else jnp.maximum(peak, high)
+    w = jnp.exp2((s - high) * factor)
+    o = jnp.dot(w.astype(BF16), values, preferred_element_type=F32)
+    if peak is not None:
+        o = summed * jnp.exp2((peak - high) * factor) + o
+    return high, o
+
+
+def near_kernel(factor, seg_q, seg_k, q_ref, sk_ref, sv_ref, pk_ref, pv_ref, out_ref, stat_ref, bias, both):
+    tokens, group = q_ref.shape[0], q_ref.shape[1] // HD
+
+    @pl.when(pl.program_id(0) == 0)
+    def _():
+        same = seg_q[:, 0:1] == seg_k[0:1, :]
+        last = seg_q[:, 1:2]
+        where_k = lax.broadcasted_iota(jnp.int32, bias.shape, 1)
+        bias[...] = jnp.where(same & (where_k <= last), 0.0, -1e30)
+        both[:, HD:] = jnp.ones((both.shape[0], HD), BF16)
+        both[:tokens, :HD] = sv_ref[...]
+        both[tokens:, :HD] = pv_ref[...]
+
+    for h in range(group):
+        q = q_ref[:, h * HD : (h + 1) * HD]
+        peak, summed = attend_block(q, sk_ref[...], both[:tokens], bias[...], factor, None, None)
+        peak, summed = attend_block(q, pk_ref[...], both[tokens:], None, factor, peak, summed)
+        at = slice(h * HD, (h + 1) * HD)
+        out_ref[:, at] = summed[:, :HD] / summed[:, HD:]
+        stat_ref[:, at] = peak * factor + jnp.log2(summed[:, HD:])
+
+
+def far_kernel(order, factor, slot, slots, place, q_ref, near_ref, stat_ref, *refs):
     hops = len(order)
     below, above = refs[:hops], refs[hops : 2 * hops]
-    out_ref, bias, ones_beside, held, sems = refs[2 * hops :]
-    tokens, group = q_ref.shape[0], q_ref.shape[1] // HD
-    rows = own_ref.shape[0]
-    slots = own_ref.shape[1] // (2 * HD)
-    slot = pl.program_id(0)
-
-    @pl.when(slot == 0)
+    out_ref, keys, both, held, sems = refs[2 * hops :]
+    group = q_ref.shape[1] // HD
+    rows = held.shape[1]
+    @pl.when(pl.program_id(0) == 0)
     def _():
-        pltpu.make_async_copy(own_ref, held.at[0], sems.at[0]).start()
         for step, choices in enumerate(order):
             for hop, from_below in sorted(set(choices)):
                 here = functools.reduce(
@@ -40,108 +77,133 @@
                 )
 
                 @pl.when(here)
-                def _(ref=(below if from_below else above)[hop - 1], to=step + 1):
+                def _(ref=(below if from_below else above)[hop - 1], to=step):
                     pltpu.make_async_copy(ref, held.at[to], sems.at[to]).start()
 
-        same = seg_q[:, 0:1] == seg_k[0:1, :]
-        last = seg_q[:, 1:2]
-        where_k = lax.broadcasted_iota(jnp.int32, bias.shape, 1)
-        bias[...] = jnp.where(same & (where_k <= last), 0.0, -1e30)
-        ones_beside[:, HD:] = jnp.ones((ones_beside.shape[0], HD), BF16)
-        for i in range(hops + 1):
-            pltpu.make_async_copy(own_ref, held.at[i], sems.at[i]).wait()
-
-    key_at = pl.ds(pl.multiple_of(slot * HD, HD), HD)
-    value_at = pl.ds(pl.multiple_of((slots + slot) * HD, HD), HD)
-    ones_beside[:tokens, :HD] = value_ref[...]
-    for i in range(hops + 1):
-        ones_beside[tokens + i * rows : tokens + (i + 1) * rows, :HD] = held[i, :, value_at]
-    dims = (((1,), (1,)), ((), ()))
-    factor = scale * math.log2(math.e)
+        both[:, HD:] = jnp.ones((both.shape[0], HD), BF16)
+        for i in range(hops):
+            pltpu.make_async_copy(below[0], held.at[i], sems.at[i]).wait()
+            keys[i * rows : (i + 1) * rows] = held[i, :, slot * HD : (slot + 1) * HD]
+            both[i * rows : (i + 1) * rows, :HD] = held[i, :, (slots + slot) * HD : (slots + slot + 1) * HD]
+
     for h in range(group):
-        q = q_ref[:, h * HD : (h + 1) * HD]
-        peak = None
-        for i in range(hops + 2):
-            keys = key_ref[...] if i == 0 else held[i - 1, :, key_at]
-            s = lax.dot_general(q, keys, dims, preferred_element_type=F32)
-            if i == 0:
-                s = s + bias[...]
-                at = slice(0, tokens)
-            else:
-                at = slice(tokens + (i - 1) * rows, tokens + i * rows)
-            high = jnp.max(s, axis=1, keepdims=True)
-            high = high if peak is None else jnp.maximum(peak, high)
-            w = jnp.exp2((s - high) * factor)
-            o = jnp.dot(w.astype(BF16), ones_beside[at, :], preferred_element_type=F32)
-            summed = o if peak is None else summed * jnp.exp2((peak - high) * factor) + o
-            peak = high
-        out_ref[:, h * HD : (h + 1) * HD] = (summed[:, :HD] / summed[:, HD:]).astype(BF16)
-
-
-def attend(z, q, seg_q, seg_k, keys, values, own, below, above):
+        at = slice(h * HD, (h + 1) * HD)
+        q = q_ref[:, at]
+        peak, summed = None, None
+        for i in range(hops):
+            block = slice(i * rows, (i + 1) * rows)
+            peak, summed = attend_block(q, keys[block], both[block], None, factor, peak, summed)
+        far, near = jnp.broadcast_to(peak * factor, q.shape), stat_ref[:, at]
+        high = jnp.maximum(far, near)
+        far, near = jnp.exp2(far - high), jnp.exp2(near - high)
+        result = summed[:, :HD] * far + near_ref[:, at] * near
+        out_ref[:, at] = (result / (summed[:, HD:] * far + near)).astype(BF16)
+
+
+FACTOR = math.log2(math.e) / math.sqrt(HD)
+
+
+def attend_near(slot, q, seg_q, seg_k, keys, values, prefix_keys, prefix_values):
     tokens, width = q.shape
-    rows = own.shape[0]
-    slots = own.shape[1] // (2 * HD)
+    rows, slots = prefix_keys.shape[0], prefix_keys.shape[1] // HD
     wide = width // slots
-    order = prefix_order(len(below) + 1)
-    n_keys = tokens + (len(below) + 1) * rows
+    halves = 2 if (wide // HD) % 2 == 0 else 1
+    one = lambda n: pl.BlockSpec((n, HD), lambda s: (0, slot))
+    out = pl.BlockSpec((tokens, wide // halves), lambda s: (0, s))
+    return pl.pallas_call(
+        functools.partial(near_kernel, FACTOR),
+        grid=(halves,),
+        out_shape=[jax.ShapeDtypeStruct((tokens, wide), F32)] * 2,
+        in_specs=[
+            pl.BlockSpec((tokens, 2), lambda s: (0, 0)),
+            pl.BlockSpec((1, tokens), lambda s: (0, 0)),
+            pl.BlockSpec((tokens, wide // halves), lambda s: (0, slot * halves + s)),
+            one(tokens),
+            one(tokens),
+            one(rows),
+            one(rows),
+        ],
+        out_specs=[out] * 2,
+        scratch_shapes=[
+            pltpu.VMEM((tokens, tokens), F32),
+            pltpu.VMEM((tokens + rows, 2 * HD), BF16),
+        ],
+        compiler_params=params(58),
+        cost_estimate=cost(16 * tokens * (tokens + rows) * wide),
+        name="attend_near",
+    )(seg_q, seg_k, q, keys, values, prefix_keys, prefix_values)
+
+
+def attend_far(slot, slots, z, q, near, stats, below, above):
+    tokens, wide = near.shape
+    rows, hops = below[0].shape[0], len(below)
+    halves = 2 if (wide // HD) % 2 == 0 else 1
+    one = pl.BlockSpec((tokens, wide // halves), lambda s: (0, s))
     anywhere = pl.BlockSpec(memory_space=pl.ANY)
     return pl.pallas_call(
-        functools.partial(attend_kernel, order, 1.0 / math.sqrt(HD)),
-        grid=(slots,),
-        out_shape=jax.ShapeDtypeStruct((tokens, width), BF16),
+        functools.partial(far_kernel, prefix_order(hops + 1), FACTOR, slot, slots),
+        grid=(halves,),
+        out_shape=jax.ShapeDtypeStruct((tokens, wide), BF16),
         in_specs=[
             pl.BlockSpec(memory_space=SMEM),
-            pl.BlockSpec((tokens, 2), lambda s: (0, 0)),
-            pl.BlockSpec((1, tokens), lambda s: (0, 0)),
-            pl.BlockSpec((tokens, wide), lambda s: (0, s)),
-            pl.BlockSpec((tokens, HD), lambda s: (0, s)),
-            pl.BlockSpec((tokens, HD), lambda s: (0, s)),
-            anywhere,
+            pl.BlockSpec((tokens, wide // halves), lambda s: (0, slot * halves + s)),
+            one,
+            one,
         ]
-        + [anywhere] * (2 * len(below)),
-        out_specs=pl.BlockSpec((tokens, wide), lambda s: (0, s)),
+        + [anywhere] * (2 * hops),
+        out_specs=one,
         scratch_shapes=[
-            pltpu.VMEM((tokens, tokens), F32),
-            pltpu.VMEM((n_keys, 2 * HD), BF16),
-            pltpu.VMEM((len(below) + 1,) + own.shape, BF16),
-            pltpu.SemaphoreType.DMA((len(below) + 1,)),
+            pltpu.VMEM((hops * rows, HD), BF16),
+            pltpu.VMEM((hops * rows, 2 * HD), BF16),
+            pltpu.VMEM((hops,) + below[0].shape, BF16),
+            pltpu.SemaphoreType.DMA((hops,)),
         ],
-        compiler_params=params(44),
-        cost_estimate=pl.CostEstimate(
-            flops=8 * tokens * n_keys * width, bytes_accessed=4 * tokens * width, transcendentals=0
-        ),
-        name="attend",
-    )(z, seg_q, seg_k, q, keys, values, own, *below, *above)
-
-
-def project_kernel(which, a_ref, w_ref, out_ref):
-    out_ref[...] = jnp.dot(a_ref[...], w_ref[...], preferred_element_type=F32).astype(BF16)
-
-
-def project(a, w, block, count):
-    rows, depth = a.shape
+        compiler_params=params(58),
+        cost_estimate=cost(16 * tokens * hops * rows * wide),
+        name="attend_far",
+    )(z, q, near, stats, *below, *above)
+
+
+def project_kernel(steps, n_parts, which, *refs):
+    a_refs, w_ref, out_refs = refs[:n_parts], refs[n_parts], refs[n_parts + 1 :]
+    part = a_refs[0].shape[1]
+    result = sum(
+        jnp.dot(a[...], w_ref[i * part : (i + 1) * part], preferred_element_type=F32)
+        for i, a in enumerate(a_refs)
+    ).astype(BF16)
+    for i, out_ref in enumerate(out_refs):
+
+        @pl.when(pl.program_id(0) // steps == i)
+        def _(out_ref=out_ref):
+            out_ref[...] = result
+
+
+def project(parts, w, blocks, count, weigh=0):
+    rows, depth = parts[0].shape[0], w.shape[0]
     wide = w.shape[1] // count
     tile = min(1024, wide)
     steps = wide // tile
+    n = blocks.shape[0]
+
+    def out_at(i):
+        return lambda j, which: (0, jnp.clip(j - i * steps, 0, steps - 1))
+
     return pl.pallas_call(
-        project_kernel,
-        out_shape=jax.ShapeDtypeStruct((rows, wide), BF16),
+        functools.partial(project_kernel, steps, len(parts)),
+        out_shape=[jax.ShapeDtypeStruct((rows, wide), BF16)] * n,
         grid_spec=pltpu.PrefetchScalarGridSpec(
             num_scalar_prefetch=1,
-            grid=(steps,),
+            grid=(n * steps,),
             in_specs=[
-                pl.BlockSpec((rows, depth), lambda j, which: (0, 0)),
-                pl.BlockSpec((depth, tile), lambda j, which: (0, which[0] * steps + j)),
+                *[pl.BlockSpec(a.shape, lambda j, which: (0, 0)) for a in parts],
+                pl.BlockSpec((depth, tile), lambda j, which: (0, which[j // steps] * steps + j % steps)),
             ],
-            out_specs=pl.BlockSpec((rows, tile), lambda j, which: (0, j)),
+            out_specs=[pl.BlockSpec((rows, tile), out_at(i)) for i in range(n)],
         ),
-        compiler_params=params(32),
-        cost_estimate=pl.CostEstimate(
-            flops=2 * rows * depth * wide, bytes_accessed=2 * depth * wide, transcendentals=0
-        ),
+        compiler_params=params(58),
+        cost_estimate=cost(1 + weigh * n * rows * depth * wide // 2),
         name="project",
-    )(block, a, w)
+    )(blocks, *parts, w)
 
 
 def most_slots(n_dp, requests):
@@ -159,7 +221,7 @@
     link = lax.broadcasted_iota(jnp.int32, (links,) + shape, 0)
     valid = (lane < n_dp * requests) & (row < 4)
     down = (row % 2) == 1
-    taker = lane // requests
+    taker = (z + n_dp - lane // requests) % n_dp
     holder = idx // per
     local = idx % per
     own = valid & (taker == holder)
@@ -169,7 +231,7 @@
     moving = valid & (src < dst)
     dst = jnp.where(moving, dst, 0)
     pos = jnp.where(moving, src, 0)
-    rank = dst * 256 + 255 - lane
+    rank = dst * 256 + 255 - (taker * requests + lane % requests)
     zero = jnp.zeros(shape, jnp.int32)
 
     def one_round(first, slots, pos, came, codes):
@@ -190,12 +252,15 @@
 
     came, codes = zero, zero
     first = 0
+
+    def left(pos):
+        return jnp.max(jnp.where(pos < dst, 1, 0))
+
+    unfinished = []
     for slots in CAPS:
+        unfinished.append(left(pos))
         pos, came, codes = one_round(first, slots, pos, came, codes)
         first += slots
-
-    def left(pos):
-        return jnp.max(jnp.where(pos < dst, 1, 0))
 
     def later(carry):
         k, _, pos, came, codes = carry
@@ -205,6 +270,7 @@
     used, _, _, came, codes = lax.while_loop(
         lambda c: (c[1] > 0) & (c[0] < limit), later, (jnp.int32(first), left(pos), pos, came, codes)
     )
+    used = jnp.where(unfinished[-1] > 0, used, first - CAPS[-1])
     place = jnp.where(own & (row == 0), local, 0)
     place = place + jnp.where(moving & (row == 0), per + came, 0)
     place = place + jnp.where(moving & (row == 1), per + limit + came, 0)
@@ -220,6 +286,7 @@
         out_shape=jax.ShapeDtypeStruct((8, 128), jnp.int32),
         in_specs=[pl.BlockSpec(memory_space=VMEM), pl.BlockSpec(memory_space=SMEM)],
         out_specs=pl.BlockSpec(memory_space=VMEM),
+        cost_estimate=SMALL,
         name="schedule",
     )(idx_rows, z)
 
@@ -284,6 +351,7 @@
         out_specs=[in_vmem] * 2,
         scratch_shapes=[pltpu.SemaphoreType.DMA((2, count, 2))],
         compiler_params=params(16),
+        cost_estimate=SMALL,
         name="pick",
     )(sched, *own, *ups, *downs)
 
@@ -293,7 +361,7 @@
     out, sems = refs[-2], refs[-1]
     own = (down_ref, up_ref)
     for r in range(requests):
-        code = sched[2, z[0] * requests + r]
+        code = sched[2, r]
         fetch(code, per, own, ups, downs, limit, out.at[r], sems.at[r])
     for r in range(requests):
         fetched(own, out.at[r], sems.at[r])
@@ -308,6 +376,7 @@
         out_specs=pl.BlockSpec(memory_space=VMEM),
         scratch_shapes=[pltpu.SemaphoreType.DMA((requests, 2))],
         compiler_params=params(16),
+        cost_estimate=SMALL,
         name="gather_own",
     )(sched, z, *own, *ups, *downs)
 
@@ -337,7 +406,7 @@
     _, up_all, down_all = lax.while_loop(
         lambda c: c[0] < sched[3, 0], step, (jnp.int32(made), up_all, down_all)
     )
-    places = lax.dynamic_slice(sched, (2, z[0] * requests), (1, requests))[0]
+    places = sched[2]
     picked = []
     for r in range(requests):
         code = places[r]
@@ -353,19 +422,33 @@
     return [(i, i + 1) for i in range(n - 1)], [(i + 1, i) for i in range(n - 1)]
 
 
-def bring_adapters(sched, z, own, requests, n_dp):
+def adapter_round(sched, own, ups, downs, requests, n_dp, after=None):
     up, down = line(n_dp)
+    sends = pick_sends(sched, own, ups, downs, len(ups), most_slots(n_dp, requests))
+    sends, after = lax.optimization_barrier((sends, after))
+    ups = ups + [lax.ppermute(sends[0], "dp", up)]
+    downs = downs + [lax.ppermute(sends[1], "dp", down)]
+    return ups, downs, after
+
+
+def last_adapters(sched, z, own, ups, downs, requests, n_dp):
     limit = most_slots(n_dp, requests)
-    ups, downs = [], []
-    for number in range(len(CAPS)):
-        sends = pick_sends(sched, own, ups, downs, number, limit)
-        ups.append(lax.ppermute(sends[0], "dp", up))
-        downs.append(lax.ppermute(sends[1], "dp", down))
-    return lax.cond(
-        sched[3, 0] > sum(CAPS),
-        lambda: later_rounds(sched, z, own, ups, downs, requests, limit, n_dp),
-        lambda: gather_own(sched, z, own, ups, downs, requests, limit),
-    )
+
+    def one_round():
+        return adapter_round(sched, own, ups, downs, requests, n_dp)[:2]
+
+    def enough():
+        return gather_own(sched, z, own, ups, downs, requests, limit)
+
+    def one_more():
+        return gather_own(sched, z, own, *one_round(), requests, limit)
+
+    def many_more():
+        return later_rounds(sched, z, own, *one_round(), requests, limit, n_dp)
+
+    used = sched[3, 0]
+    short = (used > sum(CAPS[:-1])).astype(jnp.int32) + (used > sum(CAPS)).astype(jnp.int32)
+    return lax.switch(short, (enough, one_more, many_more))
 
 
 def by_core(n):
@@ -421,66 +504,113 @@
     ti = lax.axis_index("tensor").astype(jnp.int32)
     up, down = line(n_dp)
 
-    everyone = lax.all_gather(request_adapter_index, ("groups", "dp"), axis=0, tiled=True)
-    everyone = jnp.pad(everyone.reshape(n_groups, -1), ((0, 0), (0, 128 - n_dp * requests)))
-    gi = lax.axis_index("groups")
-    mine = lax.dynamic_index_in_dim(everyone, gi, 0)
-    other = lax.dynamic_index_in_dim(everyone, (gi + 1) % n_groups, 0)
-    idx_rows = jnp.concatenate([mine, mine, other, other, jnp.zeros((4, 128), jnp.int32)], axis=0)
-
     own_rows = jnp.concatenate([shared_prefix_key_slots, shared_prefix_value_slots], axis=1)
     below, above = [own_rows], [own_rows]
-    for hop in range(1, n_dp):
-        below.append(lax.ppermute(below[-1], "dp", up[hop - 1 :]))
-        above.append(lax.ppermute(above[-1], "dp", down[: n_dp - hop]))
+    hop_first = (lax.ppermute(own_rows, "dp", up), lax.ppermute(own_rows, "dp", down))
+
+    known = jnp.concatenate(
+        [request_adapter_index]
+        + [
+            lax.ppermute(request_adapter_index, "dp", [(i, (i + s) % n_dp) for i in range(n_dp)])
+            for s in range(1, n_dp)
+        ],
+        axis=1,
+    )
 
     position = jnp.arange(tokens, dtype=jnp.int32)
     seg_ends = jnp.cumsum(lengths[0])
     request_of = jnp.sum((position[:, None] >= seg_ends[None, :]).astype(jnp.int32), axis=1)
     seg_q = jnp.stack([request_of, position], axis=1)
     seg_k = request_of[None]
-
-    down_rows = jnp.transpose(adapter_down_factors, (0, 2, 1))
-    idx_rows, _ = lax.optimization_barrier((idx_rows, (below[1], above[1])))
+    slots = shared_prefix_key_slots.shape[1] // HD
+
+    def near_part(slot, q):
+        return attend_near(
+            slot,
+            q,
+            seg_q,
+            seg_k,
+            suffix_rotated_key_slots,
+            suffix_value_slots,
+            shared_prefix_key_slots,
+            shared_prefix_value_slots,
+        )
+
+    nears = [near_part(0, queries)]
+    hop_first, nears, known = lax.optimization_barrier((hop_first, nears, known))
+    queries_here, hop_first = lax.optimization_barrier((queries, hop_first))
+    nears += [near_part(slot, queries_here) for slot in range(1, slots)]
+    for hop in range(1, n_dp):
+        if hop == 1:
+            from_below, from_above = hop_first
+        else:
+            from_below, from_above = below[-1], above[-1]
+            if hop == 3:
+                from_below, from_above, nears = lax.optimization_barrier(
+                    (from_below, from_above, nears)
+                )
+            from_below = lax.ppermute(from_below, "dp", up[hop - 1 :])
+            from_above = lax.ppermute(from_above, "dp", down[: n_dp - hop])
+        below.append(from_below)
+        above.append(from_above)
+
+    own = (jnp.transpose(adapter_down_factors, (0, 2, 1)), adapter_up_factors)
+    other = lax.ppermute(known, "groups", [(i, (i + 1) % n_groups) for i in range(n_groups)])
+    rows = jnp.concatenate([known, known, other, other], axis=0)
+    idx_rows = jnp.pad(rows, ((0, 8 - rows.shape[0]), (0, 128 - rows.shape[1])))
     sched = make_schedule(n_dp, requests, per, idx_rows, z)
-    picked = bring_adapters(sched, z, (down_rows, adapter_up_factors), requests, n_dp)
+    if n_dp > 2:
+        sched, below[2], above[2] = lax.optimization_barrier((sched, below[2], above[2]))
+    ups, downs, nears = adapter_round(sched, own, [], [], requests, n_dp, nears)
+    attended = [
+        attend_far(slot, slots, z, queries, *nears[slot], below[1:], above[1:])
+        for slot in range(slots)
+    ]
+    ups, downs, attended = adapter_round(sched, own, ups, downs, requests, n_dp, attended)
+    if n_tensor == 4:
+        core, chip = by_core(n_tensor), by_chip(n_tensor)
+
+        def share(parts, owners, weigh=0):
+            pieces = jnp.arange(PIECES, dtype=jnp.int32)
+            blocks = jnp.concatenate([owner * PIECES + pieces for owner in owners])
+            return project(parts, output_weight_matrix, blocks, n_tensor * PIECES, weigh)
+
+        far = share(attended, (ti ^ 3, ti ^ 2), 8)
+        far_other, far_same = far[:PIECES], far[PIECES:]
+        far_other, ups, downs = lax.optimization_barrier((far_other, ups, downs))
+        from_core = [lax.ppermute(x, "tensor", core) for x in far_other]
+        sends = [added(mine, came) for mine, came in zip(far_same, from_core)]
+        sched, sends = lax.optimization_barrier((sched, sends))
+        arriving = [lax.ppermute(x, "tensor", chip) for x in sends]
+    ups, downs, again = adapter_round(sched, own, ups, downs, requests, n_dp, attended)
+    if n_tensor == 4:
+        near = share(again, (ti ^ 1, ti), 4)
+        near_other, near_same = near[:PIECES], near[PIECES:]
+        near_from_core = [lax.ppermute(x, "tensor", core) for x in near_other]
+        sched, arriving[:2] = lax.optimization_barrier((sched, arriving[:2]))
+    picked = last_adapters(sched, z, own, ups, downs, requests, n_dp)
+    if n_tensor == 4:
+        picked, arriving[2:-1] = lax.optimization_barrier((picked, arriving[2:-1]))
     rank = picked.shape[1] // 2
     picked_down, picked_up = picked[:, :rank], picked[:, rank:]
-
-    attended = attend(
-        z,
-        queries,
-        seg_q,
-        seg_k,
-        suffix_rotated_key_slots,
-        suffix_value_slots,
-        own_rows,
-        below[1:],
-        above[1:],
-    )
-    if n_tensor == 4:
-        far_other, far_same, near_other, near_same = (
-            project(attended, output_weight_matrix, (ti ^ m).reshape(1), n_tensor)
-            for m in (3, 2, 1, 0)
-        )
-        core, chip = by_core(n_tensor), by_chip(n_tensor)
-        send = added(far_same, lax.ppermute(far_other, "tensor", core))
-        arriving = lax.ppermute(send, "tensor", chip)
-        near = near_same.astype(F32) + lax.ppermute(near_other, "tensor", core).astype(F32)
-        base = near + arriving.astype(F32)
-    else:
-        whole = project(attended, output_weight_matrix, jnp.zeros((1,), jnp.int32), 1)
-        share = lax.psum_scatter(whole, "tensor", scatter_dimension=1, tiled=True)
-        base = share.astype(F32)
-
     select = request_of[:, None] == jnp.arange(requests, dtype=jnp.int32)[None, :]
     first = lax.dot_general(
-        attended,
+        jnp.concatenate(attended, axis=1),
         picked_down.reshape(-1, width),
         (((1,), (1,)), ((), ())),
         preferred_element_type=F32,
     ).reshape(tokens, requests, -1)
     partial_shrink = jnp.sum(jnp.where(select[:, :, None], first, 0.0), axis=1).astype(BF16)
+    if n_tensor == 4:
+        bases = [
+            mine.astype(F32) + near.astype(F32) + far.astype(F32)
+            for mine, near, far in zip(near_same, near_from_core, arriving)
+        ]
+        base = jnp.concatenate(bases, axis=1)
+    else:
+        (whole,) = project(attended, output_weight_matrix, jnp.zeros((1,), jnp.int32), 1)
+        share = lax.psum_scatter(whole, "tensor", scatter_dimension=1, tiled=True)
+        base = share.astype(F32)
     shrink = all_sum(partial_shrink, n_tensor)
     spread = jnp.where(select[:, :, None], shrink[:, None, :], 0).reshape(tokens, -1)
     expand = jnp.dot(

time: 229 us -> 188 us (0.82)
  waiting for transfers between devices: 72.7 us -> 25.9 us
  blocking collectives: 25.9 us -> 0 us
  Pallas kernels: 75.7 us -> 90.1 us
  starting transfers between devices: 35.9 us -> 42.2 us
  other arithmetic: 10 us -> 15 us
    all_gather x1 -> x0, blocking collectives: 25.9 us -> none  [per_device(): lax.all_gather(request_adapter_index, ('groups', 'dp'), axis=0, tiled=True)]
    ppermute x17 -> x28, waiting for transfers between devices: 48.6 us -> 24.4 us  [the longest x3 8.17 us: adapter_round(): downs = downs + [lax.ppermute(sends[1], 'dp', down)]]
    ppermute x1, waiting for transfers between devices: 22.9 us -> 1.51 us  [all_sum(): return added(x, lax.ppermute(x, 'tensor', by_chip(n_tensor)))]
    pallas_call x5 -> x6, Pallas kernels: 58.1 us -> 76.2 us  [the longest x2 33.1 us: project(): pl.pallas_call(functools.partial(project_kernel, steps, len(parts)), out_...]
    ppermute x17 -> x28, starting transfers between devices: 34.3 us -> 40.5 us  [the longest x3 11.1 us: adapter_round(): ups = ups + [lax.ppermute(sends[0], 'dp', up)]]
    convert_element_type x1 -> x0, other arithmetic: 5.14 us -> none  [per_device(): return (base + expand).astype(BF16)]
    add x0 -> x6, other arithmetic: none -> 4.54 us  [the longest x4 4.53 us: per_device(): mine.astype(F32) + near.astype(F32) + far.astype(F32)]
    convert_element_type x3 -> x6, other arithmetic: 3.92 us -> 8.22 us  [added(): return (a.astype(F32) + b.astype(F32)).astype(BF16)]
  transfers between devices with their start and end apart: 19 -> 30, of which waited for: 8 -> 8; matrix products, arithmetic and copies ran while one was open for 4% -> 10% of each run, Pallas kernels for 31% -> 47%
where the time goes in v3:
time: 188 us; the launch traced here: 186 us
  Pallas kernels  90.1 us (48%)
  starting transfers between devices  42.2 us (22%)
  waiting for transfers between devices  25.9 us (14%)
  other arithmetic  15 us (8%)
  local copies, waits for them, and re-layouts  6.17 us (3%)
  matrix products  4.7 us (2%)
    pallas_call x2, Pallas kernels, project(): pl.pallas_call(functools.partial(project_kernel, steps, len(parts)), out_...  33.1 us
    pallas_call x2, Pallas kernels, attend_far(): pl.pallas_call(functools.partial(far_kernel, prefix_order(hops + 1), FACT...  25.5 us
    pallas_call x2, Pallas kernels, attend_near(): pl.pallas_call(functools.partial(near_kernel, FACTOR), grid=(halves,), ou...  17.7 us
    ppermute x3, starting transfers between devices, adapter_round(): ups = ups + [lax.ppermute(sends[0], 'dp', up)]  11.1 us
    convert_element_type x6, other arithmetic, added(): return (a.astype(F32) + b.astype(F32)).astype(BF16)  8.22 us
    ppermute x3, waiting for transfers between devices, adapter_round(): downs = downs + [lax.ppermute(sends[1], 'dp', down)]  8.17 us
    pallas_call x3, Pallas kernels, pick_sends(): pl.pallas_call(functools.partial(pick_kernel, first, count, own[0].shape[...  7.9 us
    ppermute x4, waiting for transfers between devices, per_device(): arriving = [lax.ppermute(x, 'tensor', chip) for x in sends]  6.77 us
  transfers between devices with their start and end apart: 30, of which 8 were waited for; matrix products, arithmetic and copies ran while one was open for 10% of the time, Pallas kernels for 47%

profile of v3, /device:TPU:0, one launch (start us, length us, event | category | flops | bytes accessed | tf_op | source)
XLA Modules:
  0.0 186.2 jit_solution(10502493556746375202)
XLA Ops:
  1.9 5.0 %collective-permute-start.6 = (bf16[512,512]{1,0:T(8,128)(2,1)S(1)}, bf16[512,512]{1,0:T(8,128)(2,1)S(1)}, u32[]{:S(2)}, u32[]{:S(2)}) collective-permute-start(bf16[512,512]{1,0:T(8,128)(2,1)S(1)} %constant_dynamic-update-slice_fusion.8), channel_id=1, source_target_pairs={{0,4},{4,8},{8,12},{1,5},{5,9},{9,13},{2,6},{6,10},{10,14},{3,7},{... | collective-permute-start | bytes 1572872 | tf_op jit(solution)/shard_map/ppermute | solution.py:509
  8.2 4.7 %collective-permute-start.10 = (s32[1,4]{1,0:T(1,128)}, s32[1,4]{1,0:T(1,128)S(1)}, u32[]{:S(2)}, u32[]{:S(2)}) collective-permute-start(s32[1,4]{1,0:T(1,128)} %param.21), channel_id=1, source_target_pairs={{0,12},{4,0},{8,4},{12,8},{1,13},{5,1},{9,5},{13,9},{2,14},{6,2},{... | collective-permute-start | bytes 56 | tf_op jit(solution)/shard_map/ppermute | solution.py:514
  15.7 8.8 %attend_near.2 = (f32[512,1024]{1,0:T(8,128)}, f32[512,1024]{1,0:T(8,128)}) custom-call(s32[512,2]{1,0:T(8,128)} %copy.14.seg_q, s32[1,512]{1,0:T(1,128)} %bitcast.89, bf16[512,2048]{1,0:T(8,128)(2,1)} %q_ref.6, bf16[512,256]{1,0:T(8,128)(2,1)} %sk_ref.3, bf16[512,256]{1,0:T(8,128)(2,1)} %sv_ref.3, bf16[512,256]{1,0:T(8,128)(2,1)} %pk_ref.3, ...), custom_call_target="tpu_custom_call" | custom-call | flops 8589934592 | bytes 1 | tf_op jit(solution)/shard_map/attend_near/pallas_call | solution.py:113
  27.4 8.9 %attend_near.3 = (f32[512,1024]{1,0:T(8,128)}, f32[512,1024]{1,0:T(8,128)}) custom-call(s32[512,2]{1,0:T(8,128)} %copy.14.seg_q, s32[1,512]{1,0:T(1,128)} %bitcast.90, bf16[512,2048]{1,0:T(8,128)(2,1)} %q_ref.6, bf16[512,256]{1,0:T(8,128)(2,1)} %sk_ref.3, bf16[512,256]{1,0:T(8,128)(2,1)} %sv_ref.3, bf16[512,256]{1,0:T(8,128)(2,1)} %pk_ref.3, ...), custom_call_target="tpu_custom_call" | custom-call | flops 8589934592 | bytes 1 | tf_op jit(solution)/shard_map/attend_near/pallas_call | solution.py:113
  36.3 6.4 %collective-permute-done.13.refs_4_ = bf16[512,512]{1,0:T(8,128)(2,1)} collective-permute-done((bf16[512,512]{1,0:T(8,128)(2,1)S(1)}, bf16[512,512]{1,0:T(8,128)(2,1)}, u32[]{:S(2)}, u32[]{:S(2)}) %collective-permute-start.13) | collective-permute-done | bytes 524320 | tf_op jit(solution)/shard_map/ppermute | solution.py:553
  46.8 2.0 %collective-permute-done.11 = s32[1,16]{1,0:T(1,128)S(1)} collective-permute-done((s32[1,16]{1,0:T(1,128)S(1)}, s32[1,16]{1,0:T(1,128)S(1)}, u32[]{:S(2)}, u32[]{:S(2)}) %collective-permute-start.11) | collective-permute-done | bytes 96 | tf_op jit(solution)/shard_map/ppermute | solution.py:558
  49.5 2.6 %schedule.1.sched = s32[8,128]{1,0:T(8,128)} custom-call(s32[8,128]{1,0:T(8,128)} %pad.4.idx_ref, s32[1]{0:T(128)} %bitcast.39.z_ref.place), custom_call_target="tpu_custom_call" | custom-call | flops 1 | bytes 1 | tf_op jit(solution)/shard_map/schedule/pallas_call | solution.py:284
  52.1 2.5 %pick.7 = (bf16[2,128,2048]{2,1,0:T(8,128)(2,1)S(1)}, bf16[2,128,2048]{2,1,0:T(8,128)(2,1)S(1)}) custom-call(s32[8,128]{1,0:T(8,128)} %schedule.1.sched, bf16[16,64,2048]{2,1,0:T(8,128)(2,1)} %bitcast.82, bf16[16,64,2048]{2,1,0:T(8,128)(2,1)} %up_ref.5), custom_call_target="tpu_custom_call" | custom-call | flops 1 | bytes 1 | tf_op jit(solution)/shard_map/pick/pallas_call | solution.py:347
  54.5 4.5 %collective-permute-start.14 = (bf16[2,128,2048]{2,1,0:T(8,128)(2,1)S(1)}, bf16[2,128,2048]{2,1,0:T(8,128)(2,1)S(1)}, u32[]{:S(2)}, u32[]{:S(2)}) collective-permute-start(bf16[2,128,2048]{2,1,0:T(8,128)(2,1)S(1)} %get-tuple-element.294), channel_id=1, source_target_pairs={{0,4},{4,8},{8,12},{1,5},{5,9},{9,13},{2,6},{6,10},{10,14},{3,7},{... | collective-permute-start | bytes 3145736 | tf_op jit(solution)/shard_map/ppermute | solution.py:429
  62.1 12.7 %attend_far.3.refs_1_ = bf16[512,1024]{1,0:T(8,128)(2,1)} custom-call(s32[1]{0:T(128)} %bitcast.39.z_ref.place, bf16[512,2048]{1,0:T(8,128)(2,1)} %q_ref.6, f32[512,1024]{1,0:T(8,128)} %get-tuple-element.304.near_ref, f32[512,1024]{1,0:T(8,128)} %get-tuple-element.305.stat_ref, bf16[512,512]{1,0:T(8,128)(2,1)} %copy-done.14, ...), custom_call_target="tpu_custom_call" | custom-call | flops 12884901888 | bytes 1 | tf_op jit(solution)/shard_map/attend_far/pallas_call | solution.py:143
  74.8 12.7 %attend_far.2.refs_0_ = bf16[512,1024]{1,0:T(8,128)(2,1)} custom-call(s32[1]{0:T(128)} %bitcast.39.z_ref.place, bf16[512,2048]{1,0:T(8,128)(2,1)} %q_ref.6, f32[512,1024]{1,0:T(8,128)} %get-tuple-element.298.near_ref, f32[512,1024]{1,0:T(8,128)} %get-tuple-element.299.stat_ref, bf16[512,512]{1,0:T(8,128)(2,1)} %copy-done.14, ...), custom_call_target="tpu_custom_call" | custom-call | flops 12884901888 | bytes 1 | tf_op jit(solution)/shard_map/attend_far/pallas_call | solution.py:143
  87.6 2.6 %pick.8 = (bf16[2,128,2048]{2,1,0:T(8,128)(2,1)S(1)}, bf16[2,128,2048]{2,1,0:T(8,128)(2,1)S(1)}) custom-call(s32[8,128]{1,0:T(8,128)} %schedule.1.sched, bf16[16,64,2048]{2,1,0:T(8,128)(2,1)} %bitcast.83, bf16[16,64,2048]{2,1,0:T(8,128)(2,1)} %up_ref.5, bf16[2,128,2048]{2,1,0:T(8,128)(2,1)S(1)} %collective-permute-done.14.refs_0_, ...), custom_call_target="tpu_custom_call" | custom-call | flops 1 | bytes 1 | tf_op jit(solution)/shard_map/pick/pallas_call | solution.py:347
  90.2 4.0 %collective-permute-start.18 = (bf16[2,128,2048]{2,1,0:T(8,128)(2,1)S(1)}, bf16[2,128,2048]{2,1,0:T(8,128)(2,1)S(1)}, u32[]{:S(2)}, u32[]{:S(2)}) collective-permute-start(bf16[2,128,2048]{2,1,0:T(8,128)(2,1)S(1)} %get-tuple-element.313), channel_id=1, source_target_pairs={{0,4},{4,8},{8,12},{1,5},{5,9},{9,13},{2,6},{6,10},{10,14},{3,7},{... | collective-permute-start | bytes 3145736 | tf_op jit(solution)/shard_map/ppermute | solution.py:429
  95.5 16.5 %project.2 = (bf16[512,512]{1,0:T(8,128)(2,1)}, bf16[512,512]{1,0:T(8,128)(2,1)}, bf16[512,512]{1,0:T(8,128)(2,1)}, bf16[512,512]{1,0:T(8,128)(2,1)}, bf16[512,5...) custom-call(s32[8]{0:T(128)} %pad_add_fusion.4.which, ...), custom_call_target="tpu_custom_call" | custom-call | flops 17179869184 | bytes 1 | tf_op jit(solution)/shard_map/project/pallas_call | solution.py:191
  112.5 4.3 %collective-permute-done.19.refs_3_ = bf16[2,128,2048]{2,1,0:T(8,128)(2,1)} collective-permute-done((bf16[2,128,2048]{2,1,0:T(8,128)(2,1)S(1)}, bf16[2,128,2048]{2,1,0:T(8,128)(2,1)}, u32[]{:S(2)}, u32[]{:S(2)}) %collective-permute-start.19) | collective-permute-done | bytes 1048608 | tf_op jit(solution)/shard_map/ppermute | solution.py:430
  119.1 2.1 %add_convert_fusion = bf16[512,512]{1,0:T(8,128)(2,1)} fusion(bf16[512,512]{1,0:T(8,128)(2,1)} %collective-permute-done.23, bf16[512,512]{1,0:T(8,128)(2,1)} %get-tuple-element.320), kind=kLoop, calls=%fused_computation.51 | loop fusion | flops 1048576 | bytes 1572864 | tf_op jit(solution)/shard_map/convert_element_type | solution.py:463
  121.2 2.1 %add_convert_fusion.1 = bf16[512,512]{1,0:T(8,128)(2,1)} fusion(bf16[512,512]{1,0:T(8,128)(2,1)} %collective-permute-done.22, bf16[512,512]{1,0:T(8,128)(2,1)} %get-tuple-element.318), kind=kLoop, calls=%fused_computation.52 | loop fusion | flops 1048576 | bytes 1572864 | tf_op jit(solution)/shard_map/convert_element_type | solution.py:463
  123.3 2.0 %add_convert_fusion.2 = bf16[512,512]{1,0:T(8,128)(2,1)} fusion(bf16[512,512]{1,0:T(8,128)(2,1)S(1)} %collective-permute-done.21, bf16[512,512]{1,0:T(8,128)(2,1)} %get-tuple-element.316), kind=kLoop, calls=%fused_computation.53 | loop fusion | flops 1048576 | bytes 1572864 | tf_op jit(solution)/shard_map/convert_element_type | solution.py:463
  125.3 2.0 %add_convert_fusion.3 = bf16[512,512]{1,0:T(8,128)(2,1)} fusion(bf16[512,512]{1,0:T(8,128)(2,1)S(1)} %collective-permute-done.20, bf16[512,512]{1,0:T(8,128)(2,1)} %get-tuple-element.308), kind=kLoop, calls=%fused_computation.54 | loop fusion | flops 1048576 | bytes 1572864 | tf_op jit(solution)/shard_map/convert_element_type | solution.py:463
  129.3 2.8 %pick.9 = (bf16[2,128,2048]{2,1,0:T(8,128)(2,1)S(1)}, bf16[2,128,2048]{2,1,0:T(8,128)(2,1)S(1)}) custom-call(s32[8,128]{1,0:T(8,128)} %schedule.1.sched, bf16[16,64,2048]{2,1,0:T(8,128)(2,1)} %bitcast.84, bf16[16,64,2048]{2,1,0:T(8,128)(2,1)} %up_ref.5, bf16[2,128,2048]{2,1,0:T(8,128)(2,1)S(1)} %collective-permute-done.14.refs_0_, ...), custom_call_target="tpu_custom_call" | custom-call | flops 1 | bytes 1 | tf_op jit(solution)/shard_map/pick/pallas_call | solution.py:347
  132.1 2.6 %collective-permute-start.29 = (bf16[2,128,2048]{2,1,0:T(8,128)(2,1)S(1)}, bf16[2,128,2048]{2,1,0:T(8,128)(2,1)}, u32[]{:S(2)}, u32[]{:S(2)}) collective-permute-start(bf16[2,128,2048]{2,1,0:T(8,128)(2,1)S(1)} %get-tuple-element.342), channel_id=1, source_target_pairs={{0,4},{4,8},{8,12},{1,5},{5,9},{9,13},{2,6},{6,10},{10,14},{3,7},{... | collective-permute-start | bytes 3145736 | tf_op jit(solution)/shard_map/ppermute | solution.py:429
  136.0 16.5 %project.3 = (bf16[512,512]{1,0:T(8,128)(2,1)}, bf16[512,512]{1,0:T(8,128)(2,1)}, bf16[512,512]{1,0:T(8,128)(2,1)}, bf16[512,512]{1,0:T(8,128)(2,1)}, bf16[512,5...) custom-call(s32[8]{0:T(128)} %pad_add_fusion.2.which, ...), custom_call_target="tpu_custom_call" | custom-call | flops 8589934592 | bytes 1 | tf_op jit(solution)/shard_map/project/pallas_call | solution.py:191
  153.1 1.6 collective-permute-start.31
  157.2 3.9 %collective-permute-done.30 = bf16[2,128,2048]{2,1,0:T(8,128)(2,1)} collective-permute-done((bf16[2,128,2048]{2,1,0:T(8,128)(2,1)S(1)}, bf16[2,128,2048]{2,1,0:T(8,128)(2,1)}, u32[]{:S(2)}, u32[]{:S(2)}) %collective-permute-start.30) | collective-permute-done | bytes 1048608 | tf_op jit(solution)/shard_map/ppermute | solution.py:430
  161.1 3.7 %conditional.1 = (bf16[4,128,2048]{2,1,0:T(8,128)(2,1)}) conditional(s32[]{:T(128)} %bitcast.41, (s32[8,128]{1,0:T(8,128)}, s32[1]{0:T(128)}, bf16[16,64,2048]{2,1,0:T(8,128)(2,1)}, bf16[16,64,2048]{2,1,0:T(8,128)(2,1)}, bf16[2,128,2048]{2,1,0:T(8,128)(2,1)S(1)}, /*index=5*/bf16[2,128,2048]{2,1,0:T(8,128)(2,1)S(1)}, ...), branch_computations={%region_2.3_spmd, %region_3.4_spmd, %region_4.7_spmd} | conditional | flops 12058696 | bytes 72353256 | solution.py:451
  161.1 3.4 %gather_own.2 = bf16[4,128,2048]{2,1,0:T(8,128)(2,1)} custom-call(s32[8,128]{1,0:T(8,128)} %get-tuple-element.157.sched, s32[1]{0:T(128)} %get-tuple-element.158.z, bf16[16,64,2048]{2,1,0:T(8,128)(2,1)} %get-tuple-element.159.down_ref, bf16[16,64,2048]{2,1,0:T(8,128)(2,1)} %get-tuple-element.160.up_ref, ...), custom_call_target="tpu_custom_call" | custom-call | flops 1 | bytes 1 | tf_op jit(solution)/shard_map/cond/branch_0_fun/gather_own/pallas_call | solution.py:372
  166.9 1.5 convert_add_fusion.3
  168.5 1.6 convert_add_fusion.2
  170.0 2.6 %fusion.9 = bf16[512,64]{0,1:T(8,128)(2,1)S(1)} fusion(bf16[512,1024]{1,0:T(8,128)(2,1)} %attend_far.3.refs_1_, bf16[512,1024]{1,0:T(8,128)(2,1)} %attend_far.2.refs_0_, bf16[4,128,2048]{2,1,0:T(8,128)(2,1)} %get-tuple-element.494, pred[512,4]{0,1:T(4,128)(4,1)S(1)} %iota_compare_fusion), kind=kOutput, calls=%fused_computation.44 | convolution fusion | flops 541294592 | bytes 3213312 | tf_op jit(solution)/shard_map/dot_general | solution.py:597
  172.7 6.8 %collective-permute-done.33 = bf16[512,512]{1,0:T(8,128)(2,1)S(1)} collective-permute-done((bf16[512,512]{1,0:T(8,128)(2,1)}, bf16[512,512]{1,0:T(8,128)(2,1)S(1)}, u32[]{:S(2)}, u32[]{:S(2)}) %collective-permute-start.33) | collective-permute-done | bytes 524320 | tf_op jit(solution)/shard_map/ppermute | solution.py:584
  179.7 1.6 collective-permute-start.35
  184.1 2.1 %fusion.4 = bf16[512,2048]{1,0:T(8,128)(2,1)} fusion(f32[512,512]{1,0:T(8,128)S(1)} %convert_add_fusion, f32[512,512]{1,0:T(8,128)S(1)} %convert_add_fusion.1, f32[512,512]{1,0:T(8,128)S(1)} %convert_add_fusion.2, f32[512,512]{1,0:T(8,128)S(1)} %convert_add_fusion.3, bf16[4,128,2048]{2,1,0:T(8,128)(2,1)S(1)} %copy-done.3, ...), kind=kOutput, calls=%fused_computation.38 | convolution fusion | flops 542244864 | bytes 7407616 | tf_op jit(solution)/shard_map/dot_general | solution.py:616
  (90 shorter events, 30.8 us)
Async XLA Ops:
  1.9 22.7 %collective-permute-start.6 = (bf16[512,512]{1,0:T(8,128)(2,1)S(1)}, bf16[512,512]{1,0:T(8,128)(2,1)S(1)}, u32[]{:S(2)}, u32[]{:S(2)}) collective-permute-start(bf16[512,512]{1,0:T(8,128)(2,1)S(1)} %constant_dynamic-update-slice_fusion.8), channel_id=1, source_target_pairs={{0,4},{4,8},{8,12},{1,5},{5,9},{9,13},{2,6},{6,10},{10,14},{3,7},{... | collective-permute-start | bytes 1572872 | tf_op jit(solution)/shard_map/ppermute | solution.py:509
  6.9 17.7 %collective-permute-start.7 = (bf16[512,512]{1,0:T(8,128)(2,1)S(1)}, bf16[512,512]{1,0:T(8,128)(2,1)S(1)}, u32[]{:S(2)}, u32[]{:S(2)}) collective-permute-start(bf16[512,512]{1,0:T(8,128)(2,1)S(1)} %constant_dynamic-update-slice_fusion.8), channel_id=1, source_target_pairs={{4,0},{8,4},{12,8},{5,1},{9,5},{13,9},{6,2},{10,6},{14,10},{7,3},{... | collective-permute-start | bytes 1572872 | tf_op jit(solution)/shard_map/ppermute | solution.py:509
  8.2 16.3 %collective-permute-start.10 = (s32[1,4]{1,0:T(1,128)}, s32[1,4]{1,0:T(1,128)S(1)}, u32[]{:S(2)}, u32[]{:S(2)}) collective-permute-start(s32[1,4]{1,0:T(1,128)} %param.21), channel_id=1, source_target_pairs={{0,12},{4,0},{8,4},{12,8},{1,13},{5,1},{9,5},{13,9},{2,14},{6,2},{... | collective-permute-start | bytes 56 | tf_op jit(solution)/shard_map/ppermute | solution.py:514
  12.9 11.6 %collective-permute-start.8 = (s32[1,4]{1,0:T(1,128)}, s32[1,4]{1,0:T(1,128)S(1)}, u32[]{:S(2)}, u32[]{:S(2)}) collective-permute-start(s32[1,4]{1,0:T(1,128)} %param.21), channel_id=1, source_target_pairs={{0,4},{4,8},{8,12},{12,0},{1,5},{5,9},{9,13},{13,1},{2,6},{6,10},{... | collective-permute-start | bytes 56 | tf_op jit(solution)/shard_map/ppermute | solution.py:514
  12.9 11.6 %collective-permute-start.9 = (s32[1,4]{1,0:T(1,128)}, s32[1,4]{1,0:T(1,128)S(1)}, u32[]{:S(2)}, u32[]{:S(2)}) collective-permute-start(s32[1,4]{1,0:T(1,128)} %param.21), channel_id=1, source_target_pairs={{0,8},{4,12},{8,0},{12,4},{1,9},{5,13},{9,1},{13,5},{2,10},{6,14},... | collective-permute-start | bytes 56 | tf_op jit(solution)/shard_map/ppermute | solution.py:514
  24.6 11.7 %collective-permute-start.12 = (bf16[512,512]{1,0:T(8,128)(2,1)S(1)}, bf16[512,512]{1,0:T(8,128)(2,1)}, u32[]{:S(2)}, u32[]{:S(2)}) collective-permute-start(bf16[512,512]{1,0:T(8,128)(2,1)S(1)} %collective-permute-done.6.refs_0_), channel_id=1, source_target_pairs={{4,8},{8,12},{5,9},{9,13},{6,10},{10,14},{7,11},{11,15},{20,24},{2... | collective-permute-start | bytes 1572872 | tf_op jit(solution)/shard_map/ppermute | solution.py:552
  26.1 16.6 %collective-permute-start.13 = (bf16[512,512]{1,0:T(8,128)(2,1)S(1)}, bf16[512,512]{1,0:T(8,128)(2,1)}, u32[]{:S(2)}, u32[]{:S(2)}) collective-permute-start(bf16[512,512]{1,0:T(8,128)(2,1)S(1)} %collective-permute-done.7.refs_3_), channel_id=1, source_target_pairs={{4,0},{8,4},{5,1},{9,5},{6,2},{10,6},{7,3},{11,7},{20,16},{24,20},... | collective-permute-start | bytes 1572872 | tf_op jit(solution)/shard_map/ppermute | solution.py:553
  42.7 17.8 %collective-permute-start.16 = (bf16[512,512]{1,0:T(8,128)(2,1)}, bf16[512,512]{1,0:T(8,128)(2,1)S(1)}, u32[]{:S(2)}, u32[]{:S(2)}) collective-permute-start(bf16[512,512]{1,0:T(8,128)(2,1)} %collective-permute-done.12.refs_1_), channel_id=1, source_target_pairs={{8,12},{9,13},{10,14},{11,15},{24,28},{25,29},{26,30},{27,31}} | collective-permute-start | bytes 1572872 | tf_op jit(solution)/shard_map/ppermute | solution.py:552
  43.4 17.2 %collective-permute-start.17 = (bf16[512,512]{1,0:T(8,128)(2,1)}, bf16[512,512]{1,0:T(8,128)(2,1)S(1)}, u32[]{:S(2)}, u32[]{:S(2)}) collective-permute-start(bf16[512,512]{1,0:T(8,128)(2,1)} %collective-permute-done.13.refs_4_), channel_id=1, source_target_pairs={{4,0},{5,1},{6,2},{7,3},{20,16},{21,17},{22,18},{23,19}} | collective-permute-start | bytes 1572872 | tf_op jit(solution)/shard_map/ppermute | solution.py:553
  45.3 3.5 %collective-permute-start.11 = (s32[1,16]{1,0:T(1,128)S(1)}, s32[1,16]{1,0:T(1,128)S(1)}, u32[]{:S(2)}, u32[]{:S(2)}) collective-permute-start(s32[1,16]{1,0:T(1,128)S(1)} %pad_add_fusion.3), channel_id=1, source_target_pairs={{0,16},{16,0},{1,17},{17,1},{2,18},{18,2},{3,19},{19,3},{4,20},{20... | collective-permute-start | bytes 200 | tf_op jit(solution)/shard_map/ppermute | solution.py:558
  54.5 33.0 %collective-permute-start.14 = (bf16[2,128,2048]{2,1,0:T(8,128)(2,1)S(1)}, bf16[2,128,2048]{2,1,0:T(8,128)(2,1)S(1)}, u32[]{:S(2)}, u32[]{:S(2)}) collective-permute-start(bf16[2,128,2048]{2,1,0:T(8,128)(2,1)S(1)} %get-tuple-element.294), channel_id=1, source_target_pairs={{0,4},{4,8},{8,12},{1,5},{5,9},{9,13},{2,6},{6,10},{10,14},{3,7},{... | collective-permute-start | bytes 3145736 | tf_op jit(solution)/shard_map/ppermute | solution.py:429
  59.0 28.5 %collective-permute-start.15 = (bf16[2,128,2048]{2,1,0:T(8,128)(2,1)S(1)}, bf16[2,128,2048]{2,1,0:T(8,128)(2,1)S(1)}, u32[]{:S(2)}, u32[]{:S(2)}) collective-permute-start(bf16[2,128,2048]{2,1,0:T(8,128)(2,1)S(1)} %get-tuple-element.295), channel_id=1, source_target_pairs={{4,0},{8,4},{12,8},{5,1},{9,5},{13,9},{6,2},{10,6},{14,10},{7,3},{... | collective-permute-start | bytes 3145736 | tf_op jit(solution)/shard_map/ppermute | solution.py:430
  90.2 22.3 %collective-permute-start.18 = (bf16[2,128,2048]{2,1,0:T(8,128)(2,1)S(1)}, bf16[2,128,2048]{2,1,0:T(8,128)(2,1)S(1)}, u32[]{:S(2)}, u32[]{:S(2)}) collective-permute-start(bf16[2,128,2048]{2,1,0:T(8,128)(2,1)S(1)} %get-tuple-element.313), channel_id=1, source_target_pairs={{0,4},{4,8},{8,12},{1,5},{5,9},{9,13},{2,6},{6,10},{10,14},{3,7},{... | collective-permute-start | bytes 3145736 | tf_op jit(solution)/shard_map/ppermute | solution.py:429
  94.2 22.6 %collective-permute-start.19 = (bf16[2,128,2048]{2,1,0:T(8,128)(2,1)S(1)}, bf16[2,128,2048]{2,1,0:T(8,128)(2,1)}, u32[]{:S(2)}, u32[]{:S(2)}) collective-permute-start(bf16[2,128,2048]{2,1,0:T(8,128)(2,1)S(1)} %get-tuple-element.314), channel_id=1, source_target_pairs={{4,0},{8,4},{12,8},{5,1},{9,5},{13,9},{6,2},{10,6},{14,10},{7,3},{... | collective-permute-start | bytes 3145736 | tf_op jit(solution)/shard_map/ppermute | solution.py:430
  116.8 2.3 %collective-permute-start.23 = (bf16[512,512]{1,0:T(8,128)(2,1)}, bf16[512,512]{1,0:T(8,128)(2,1)}, u32[]{:S(2)}, u32[]{:S(2)}) collective-permute-start(bf16[512,512]{1,0:T(8,128)(2,1)} %get-tuple-element.321), channel_id=1, source_target_pairs={{0,1},{1,0},{2,3},{3,2},{4,5},{5,4},{6,7},{7,6},{8,9},{9,8},{10,11... | collective-permute-start | bytes 1572872 | tf_op jit(solution)/shard_map/ppermute | solution.py:581
  116.8 4.4 %collective-permute-start.22 = (bf16[512,512]{1,0:T(8,128)(2,1)}, bf16[512,512]{1,0:T(8,128)(2,1)}, u32[]{:S(2)}, u32[]{:S(2)}) collective-permute-start(bf16[512,512]{1,0:T(8,128)(2,1)} %get-tuple-element.319), channel_id=1, source_target_pairs={{0,1},{1,0},{2,3},{3,2},{4,5},{5,4},{6,7},{7,6},{8,9},{9,8},{10,11... | collective-permute-start | bytes 1572872 | tf_op jit(solution)/shard_map/ppermute | solution.py:581
  118.0 5.3 %collective-permute-start.21 = (bf16[512,512]{1,0:T(8,128)(2,1)}, bf16[512,512]{1,0:T(8,128)(2,1)S(1)}, u32[]{:S(2)}, u32[]{:S(2)}) collective-permute-start(bf16[512,512]{1,0:T(8,128)(2,1)} %get-tuple-element.317), channel_id=1, source_target_pairs={{0,1},{1,0},{2,3},{3,2},{4,5},{5,4},{6,7},{7,6},{8,9},{9,8},{10,11... | collective-permute-start | bytes 1572872 | tf_op jit(solution)/shard_map/ppermute | solution.py:581
  118.0 7.3 %collective-permute-start.20 = (bf16[512,512]{1,0:T(8,128)(2,1)}, bf16[512,512]{1,0:T(8,128)(2,1)S(1)}, u32[]{:S(2)}, u32[]{:S(2)}) collective-permute-start(bf16[512,512]{1,0:T(8,128)(2,1)} %get-tuple-element.315), channel_id=1, source_target_pairs={{0,1},{1,0},{2,3},{3,2},{4,5},{5,4},{6,7},{7,6},{8,9},{9,8},{10,11... | collective-permute-start | bytes 1572872 | tf_op jit(solution)/shard_map/ppermute | solution.py:581
  127.3 25.3 %collective-permute-start.25 = (bf16[512,512]{1,0:T(8,128)(2,1)}, bf16[512,512]{1,0:T(8,128)(2,1)}, u32[]{:S(2)}, u32[]{:S(2)}) collective-permute-start(bf16[512,512]{1,0:T(8,128)(2,1)} %add_convert_fusion.3), channel_id=1, source_target_pairs={{0,2},{1,3},{2,0},{3,1},{4,6},{5,7},{6,4},{7,5},{8,10},{9,11},{10,... | collective-permute-start | bytes 1572872 | tf_op jit(solution)/shard_map/ppermute | solution.py:584
  128.8 24.3 %collective-permute-start.26 = (bf16[512,512]{1,0:T(8,128)(2,1)}, bf16[512,512]{1,0:T(8,128)(2,1)S(1)}, u32[]{:S(2)}, u32[]{:S(2)}) collective-permute-start(bf16[512,512]{1,0:T(8,128)(2,1)} %add_convert_fusion.2), channel_id=1, source_target_pairs={{0,2},{1,3},{2,0},{3,1},{4,6},{5,7},{6,4},{7,5},{8,10},{9,11},{10,... | collective-permute-start | bytes 1572872 | tf_op jit(solution)/shard_map/ppermute | solution.py:584
  132.1 20.9 %copy-start.12 = (s32[512]{0:T(512)S(1)}, s32[512]{0:T(512)}, u32[]{:S(2)}) copy-start(s32[512]{0:T(512)} %copy-done.11) | copy-start | bytes 6148
  132.1 25.0 %collective-permute-start.29 = (bf16[2,128,2048]{2,1,0:T(8,128)(2,1)S(1)}, bf16[2,128,2048]{2,1,0:T(8,128)(2,1)}, u32[]{:S(2)}, u32[]{:S(2)}) collective-permute-start(bf16[2,128,2048]{2,1,0:T(8,128)(2,1)S(1)} %get-tuple-element.342), channel_id=1, source_target_pairs={{0,4},{4,8},{8,12},{1,5},{5,9},{9,13},{2,6},{6,10},{10,14},{3,7},{... | collective-permute-start | bytes 3145736 | tf_op jit(solution)/shard_map/ppermute | solution.py:429
  134.7 26.3 %collective-permute-start.30 = (bf16[2,128,2048]{2,1,0:T(8,128)(2,1)S(1)}, bf16[2,128,2048]{2,1,0:T(8,128)(2,1)}, u32[]{:S(2)}, u32[]{:S(2)}) collective-permute-start(bf16[2,128,2048]{2,1,0:T(8,128)(2,1)S(1)} %get-tuple-element.343), channel_id=1, source_target_pairs={{4,0},{8,4},{12,8},{5,1},{9,5},{13,9},{6,2},{10,6},{14,10},{7,3},{... | collective-permute-start | bytes 3145736 | tf_op jit(solution)/shard_map/ppermute | solution.py:430
  152.5 12.8 %collective-permute-start.24 = (bf16[512,512]{1,0:T(8,128)(2,1)}, bf16[512,512]{1,0:T(8,128)(2,1)}, u32[]{:S(2)}, u32[]{:S(2)}) collective-permute-start(bf16[512,512]{1,0:T(8,128)(2,1)} %get-tuple-element.332), channel_id=1, source_target_pairs={{0,1},{1,0},{2,3},{3,2},{4,5},{5,4},{6,7},{7,6},{8,9},{9,8},{10,11... | collective-permute-start | bytes 1572872 | tf_op jit(solution)/shard_map/ppermute | solution.py:589
  152.6 15.9 %collective-permute-start.27 = (bf16[512,512]{1,0:T(8,128)(2,1)}, bf16[512,512]{1,0:T(8,128)(2,1)}, u32[]{:S(2)}, u32[]{:S(2)}) collective-permute-start(bf16[512,512]{1,0:T(8,128)(2,1)} %get-tuple-element.337), channel_id=1, source_target_pairs={{0,1},{1,0},{2,3},{3,2},{4,5},{5,4},{6,7},{7,6},{8,9},{9,8},{10,11... | collective-permute-start | bytes 1572872 | tf_op jit(solution)/shard_map/ppermute | solution.py:589
  153.1 16.9 %collective-permute-start.31 = (bf16[512,512]{1,0:T(8,128)(2,1)}, bf16[512,512]{1,0:T(8,128)(2,1)}, u32[]{:S(2)}, u32[]{:S(2)}) collective-permute-start(bf16[512,512]{1,0:T(8,128)(2,1)} %add_convert_fusion.1), channel_id=1, source_target_pairs={{0,2},{1,3},{2,0},{3,1},{4,6},{5,7},{6,4},{7,5},{8,10},{9,11},{10,... | collective-permute-start | bytes 1572872 | tf_op jit(solution)/shard_map/ppermute | solution.py:584
  164.8 19.3 %copy-start.3 = (bf16[4,128,2048]{2,1,0:T(8,128)(2,1)S(1)}, bf16[4,128,2048]{2,1,0:T(8,128)(2,1)}, u32[]{:S(2)}) copy-start(bf16[4,128,2048]{2,1,0:T(8,128)(2,1)} %get-tuple-element.494) | copy-start | bytes 6291460
  164.8 16.5 %collective-permute-start.28 = (bf16[512,512]{1,0:T(8,128)(2,1)}, bf16[512,512]{1,0:T(8,128)(2,1)S(1)}, u32[]{:S(2)}, u32[]{:S(2)}) collective-permute-start(bf16[512,512]{1,0:T(8,128)(2,1)} %get-tuple-element.340), channel_id=1, source_target_pairs={{0,1},{1,0},{2,3},{3,2},{4,5},{5,4},{6,7},{7,6},{8,9},{9,8},{10,11... | collective-permute-start | bytes 1572872 | tf_op jit(solution)/shard_map/ppermute | solution.py:589
  164.9 7.8 %collective-permute-start.32 = (bf16[512,512]{1,0:T(8,128)(2,1)}, bf16[512,512]{1,0:T(8,128)(2,1)S(1)}, u32[]{:S(2)}, u32[]{:S(2)}) collective-permute-start(bf16[512,512]{1,0:T(8,128)(2,1)} %get-tuple-element.347), channel_id=1, source_target_pairs={{0,1},{1,0},{2,3},{3,2},{4,5},{5,4},{6,7},{7,6},{8,9},{9,8},{10,11... | collective-permute-start | bytes 1572872 | tf_op jit(solution)/shard_map/ppermute | solution.py:589
  165.4 14.1 %collective-permute-start.33 = (bf16[512,512]{1,0:T(8,128)(2,1)}, bf16[512,512]{1,0:T(8,128)(2,1)S(1)}, u32[]{:S(2)}, u32[]{:S(2)}) collective-permute-start(bf16[512,512]{1,0:T(8,128)(2,1)} %add_convert_fusion), channel_id=1, source_target_pairs={{0,2},{1,3},{2,0},{3,1},{4,6},{5,7},{6,4},{7,5},{8,10},{9,11},{10,... | collective-permute-start | bytes 1572872 | tf_op jit(solution)/shard_map/ppermute | solution.py:584
  172.7 7.1 %collective-permute-start.34 = (bf16[512,64]{0,1:T(8,128)(2,1)S(1)}, bf16[512,64]{0,1:T(8,128)(2,1)S(1)}, u32[]{:S(2)}, u32[]{:S(2)}) collective-permute-start(bf16[512,64]{0,1:T(8,128)(2,1)S(1)} %fusion.9), channel_id=1, source_target_pairs={{0,1},{1,0},{2,3},{3,2},{4,5},{5,4},{6,7},{7,6},{8,9},{9,8},{10,11... | collective-permute-start | bytes 196616 | tf_op jit(solution)/shard_map/ppermute | solution.py:469
  179.7 4.3 %collective-permute-start.35 = (bf16[512,64]{0,1:T(8,128)(2,1)S(1)}, bf16[512,64]{0,1:T(8,128)(2,1)S(1)}, u32[]{:S(2)}, u32[]{:S(2)}) collective-permute-start(bf16[512,64]{0,1:T(8,128)(2,1)S(1)} %add_convert_fusion.5), channel_id=1, source_target_pairs={{0,2},{1,3},{2,0},{3,1},{4,6},{5,7},{6,4},{7,5},{8,10},{9,11},{10,... | collective-permute-start | bytes 196616 | tf_op jit(solution)/shard_map/ppermute | solution.py:470
  (9 other events, 73.9 us)

commit v4 on v3

--- a/solution.py
+++ b/solution.py
@@ -39,7 +39,7 @@
     return high, o
 
 
-def near_kernel(factor, seg_q, seg_k, q_ref, sk_ref, sv_ref, pk_ref, pv_ref, out_ref, stat_ref, bias, both):
+def near_kernel(factor, halves, seg_q, seg_k, q_ref, sk_ref, sv_ref, pk_ref, pv_ref, out_ref, stat_ref, bias, both):
     tokens, group = q_ref.shape[0], q_ref.shape[1] // HD
 
     @pl.when(pl.program_id(0) == 0)
@@ -49,6 +49,9 @@
         where_k = lax.broadcasted_iota(jnp.int32, bias.shape, 1)
         bias[...] = jnp.where(same & (where_k <= last), 0.0, -1e30)
         both[:, HD:] = jnp.ones((both.shape[0], HD), BF16)
+
+    @pl.when(pl.program_id(0) % halves == 0)
+    def _():
         both[:tokens, :HD] = sv_ref[...]
         both[tokens:, :HD] = pv_ref[...]
 
@@ -61,12 +64,15 @@
         stat_ref[:, at] = peak * factor + jnp.log2(summed[:, HD:])
 
 
-def far_kernel(order, factor, slot, slots, place, q_ref, near_ref, stat_ref, *refs):
+def far_kernel(order, factor, halves, place, q_ref, near_ref, stat_ref, *refs):
     hops = len(order)
     below, above = refs[:hops], refs[hops : 2 * hops]
     out_ref, keys, both, held, sems = refs[2 * hops :]
     group = q_ref.shape[1] // HD
     rows = held.shape[1]
+    slots = held.shape[2] // (2 * HD)
+    slot = pl.program_id(0) // halves
+
     @pl.when(pl.program_id(0) == 0)
     def _():
         for step, choices in enumerate(order):
@@ -83,8 +89,14 @@
         both[:, HD:] = jnp.ones((both.shape[0], HD), BF16)
         for i in range(hops):
             pltpu.make_async_copy(below[0], held.at[i], sems.at[i]).wait()
-            keys[i * rows : (i + 1) * rows] = held[i, :, slot * HD : (slot + 1) * HD]
-            both[i * rows : (i + 1) * rows, :HD] = held[i, :, (slots + slot) * HD : (slots + slot + 1) * HD]
+
+    @pl.when(pl.program_id(0) % halves == 0)
+    def _():
+        key_at = pl.ds(pl.multiple_of(slot * HD, HD), HD)
+        value_at = pl.ds(pl.multiple_of((slots + slot) * HD, HD), HD)
+        for i in range(hops):
+            keys[i * rows : (i + 1) * rows] = held[i, :, key_at]
+            both[i * rows : (i + 1) * rows, :HD] = held[i, :, value_at]
 
     for h in range(group):
         at = slice(h * HD, (h + 1) * HD)
@@ -103,55 +115,50 @@
 FACTOR = math.log2(math.e) / math.sqrt(HD)
 
 
-def attend_near(slot, q, seg_q, seg_k, keys, values, prefix_keys, prefix_values):
+def attend_near(q, seg_q, seg_k, keys, values, prefix_keys, prefix_values):
     tokens, width = q.shape
     rows, slots = prefix_keys.shape[0], prefix_keys.shape[1] // HD
-    wide = width // slots
-    halves = 2 if (wide // HD) % 2 == 0 else 1
-    one = lambda n: pl.BlockSpec((n, HD), lambda s: (0, slot))
-    out = pl.BlockSpec((tokens, wide // halves), lambda s: (0, s))
+    halves = 2 if (width // slots // HD) % 2 == 0 else 1
+    wide = width // slots // halves
+    part = pl.BlockSpec((tokens, wide), lambda s: (0, s))
+    one = lambda n: pl.BlockSpec((n, HD), lambda s: (0, s // halves))
     return pl.pallas_call(
-        functools.partial(near_kernel, FACTOR),
-        grid=(halves,),
-        out_shape=[jax.ShapeDtypeStruct((tokens, wide), F32)] * 2,
+        functools.partial(near_kernel, FACTOR, halves),
+        grid=(slots * halves,),
+        out_shape=[jax.ShapeDtypeStruct((tokens, width), F32)] * 2,
         in_specs=[
             pl.BlockSpec((tokens, 2), lambda s: (0, 0)),
             pl.BlockSpec((1, tokens), lambda s: (0, 0)),
-            pl.BlockSpec((tokens, wide // halves), lambda s: (0, slot * halves + s)),
+            part,
             one(tokens),
             one(tokens),
             one(rows),
             one(rows),
         ],
-        out_specs=[out] * 2,
+        out_specs=[part] * 2,
         scratch_shapes=[
             pltpu.VMEM((tokens, tokens), F32),
             pltpu.VMEM((tokens + rows, 2 * HD), BF16),
         ],
         compiler_params=params(58),
-        cost_estimate=cost(16 * tokens * (tokens + rows) * wide),
+        cost_estimate=cost(16 * tokens * (tokens + rows) * width),
         name="attend_near",
     )(seg_q, seg_k, q, keys, values, prefix_keys, prefix_values)
 
 
-def attend_far(slot, slots, z, q, near, stats, below, above):
-    tokens, wide = near.shape
+def attend_far(z, q, near, stats, below, above):
+    tokens, width = q.shape
     rows, hops = below[0].shape[0], len(below)
-    halves = 2 if (wide // HD) % 2 == 0 else 1
-    one = pl.BlockSpec((tokens, wide // halves), lambda s: (0, s))
+    slots = below[0].shape[1] // (2 * HD)
+    halves = 2 if (width // slots // HD) % 2 == 0 else 1
+    part = pl.BlockSpec((tokens, width // slots // halves), lambda s: (0, s))
     anywhere = pl.BlockSpec(memory_space=pl.ANY)
     return pl.pallas_call(
-        functools.partial(far_kernel, prefix_order(hops + 1), FACTOR, slot, slots),
-        grid=(halves,),
-        out_shape=jax.ShapeDtypeStruct((tokens, wide), BF16),
-        in_specs=[
-            pl.BlockSpec(memory_space=SMEM),
-            pl.BlockSpec((tokens, wide // halves), lambda s: (0, slot * halves + s)),
-            one,
-            one,
-        ]
-        + [anywhere] * (2 * hops),
-        out_specs=one,
+        functools.partial(far_kernel, prefix_order(hops + 1), FACTOR, halves),
+        grid=(slots * halves,),
+        out_shape=jax.ShapeDtypeStruct((tokens, width), BF16),
+        in_specs=[pl.BlockSpec(memory_space=SMEM), part, part, part] + [anywhere] * (2 * hops),
+        out_specs=part,
         scratch_shapes=[
             pltpu.VMEM((hops * rows, HD), BF16),
             pltpu.VMEM((hops * rows, 2 * HD), BF16),
@@ -159,51 +166,81 @@
             pltpu.SemaphoreType.DMA((hops,)),
         ],
         compiler_params=params(58),
-        cost_estimate=cost(16 * tokens * hops * rows * wide),
+        cost_estimate=cost(16 * tokens * hops * rows * width),
         name="attend_far",
     )(z, q, near, stats, *below, *above)
 
 
-def project_kernel(steps, n_parts, which, *refs):
-    a_refs, w_ref, out_refs = refs[:n_parts], refs[n_parts], refs[n_parts + 1 :]
-    part = a_refs[0].shape[1]
-    result = sum(
-        jnp.dot(a[...], w_ref[i * part : (i + 1) * part], preferred_element_type=F32)
-        for i, a in enumerate(a_refs)
-    ).astype(BF16)
-    for i, out_ref in enumerate(out_refs):
-
-        @pl.when(pl.program_id(0) // steps == i)
-        def _(out_ref=out_ref):
-            out_ref[...] = result
-
-
-def project(parts, w, blocks, count, weigh=0):
+def project_kernel(per_tile, wide, n_parts, which, *refs):
+    a_refs, w_ref = refs[:n_parts], refs[n_parts]
+    outs, done, sems = refs[n_parts + 1 : -2], refs[-2], refs[-1]
+    step = pl.program_id(0)
+    a = jnp.concatenate([ref[...] for ref in a_refs], axis=1)
+    done[step] = jnp.dot(a, w_ref[...], preferred_element_type=F32).astype(BF16)
+
+    def leaving(i):
+        piece = done.at[i // per_tile, :, (i % per_tile) * wide : (i % per_tile + 1) * wide]
+        return pltpu.make_async_copy(piece, outs[i], sems.at[i])
+
+    for i in range(len(outs)):
+
+        @pl.when(step == i // per_tile)
+        def _(i=i):
+            leaving(i).start()
+
+    @pl.when(step == pl.num_programs(0) - 1)
+    def _():
+        for i in range(len(outs)):
+            leaving(i).wait()
+
+
+def project(parts, w, owners, count, pieces, weigh=0):
     rows, depth = parts[0].shape[0], w.shape[0]
-    wide = w.shape[1] // count
-    tile = min(1024, wide)
-    steps = wide // tile
-    n = blocks.shape[0]
-
-    def out_at(i):
-        return lambda j, which: (0, jnp.clip(j - i * steps, 0, steps - 1))
-
+    block = w.shape[1] // count
+    wide = block // pieces
+    tile = max(wide, min(1024, block))
+    per_tile, tiles = tile // wide, block // tile
+    n = owners.shape[0]
     return pl.pallas_call(
-        functools.partial(project_kernel, steps, len(parts)),
-        out_shape=[jax.ShapeDtypeStruct((rows, wide), BF16)] * n,
+        functools.partial(project_kernel, per_tile, wide, len(parts)),
+        out_shape=[jax.ShapeDtypeStruct((rows, wide), BF16)] * (n * pieces),
         grid_spec=pltpu.PrefetchScalarGridSpec(
             num_scalar_prefetch=1,
-            grid=(n * steps,),
+            grid=(n * tiles,),
             in_specs=[
                 *[pl.BlockSpec(a.shape, lambda j, which: (0, 0)) for a in parts],
-                pl.BlockSpec((depth, tile), lambda j, which: (0, which[j // steps] * steps + j % steps)),
+                pl.BlockSpec((depth, tile), lambda j, which: (0, which[j // tiles] * tiles + j % tiles)),
             ],
-            out_specs=[pl.BlockSpec((rows, tile), out_at(i)) for i in range(n)],
+            out_specs=[pl.BlockSpec(memory_space=pl.ANY)] * (n * pieces),
+            scratch_shapes=[
+                pltpu.VMEM((n * tiles, rows, tile), BF16),
+                pltpu.SemaphoreType.DMA((n * pieces,)),
+            ],
         ),
         compiler_params=params(58),
-        cost_estimate=cost(1 + weigh * n * rows * depth * wide // 2),
+        cost_estimate=cost(1 + weigh * n * rows * depth * block // 2),
         name="project",
-    )(blocks, *parts, w)
+    )(owners, *parts, w)
+
+
+def add_kernel(n, *refs):
+    for a, b, out in zip(refs[:n], refs[n : 2 * n], refs[2 * n :]):
+        out[...] = (a[...].astype(F32) + b[...].astype(F32)).astype(BF16)
+
+
+def add_all(first, second):
+    n, (rows, wide) = len(first), first[0].shape
+    block = pl.BlockSpec((rows // 4, wide), lambda i: (i, 0))
+    return pl.pallas_call(
+        functools.partial(add_kernel, n),
+        grid=(4,),
+        out_shape=[jax.ShapeDtypeStruct((rows, wide), BF16)] * n,
+        in_specs=[block] * (2 * n),
+        out_specs=[block] * n,
+        compiler_params=params(58),
+        cost_estimate=SMALL,
+        name="add_all",
+    )(*first, *second)
 
 
 def most_slots(n_dp, requests):
@@ -522,32 +559,28 @@
     request_of = jnp.sum((position[:, None] >= seg_ends[None, :]).astype(jnp.int32), axis=1)
     seg_q = jnp.stack([request_of, position], axis=1)
     seg_k = request_of[None]
-    slots = shared_prefix_key_slots.shape[1] // HD
-
-    def near_part(slot, q):
-        return attend_near(
-            slot,
-            q,
-            seg_q,
-            seg_k,
-            suffix_rotated_key_slots,
-            suffix_value_slots,
-            shared_prefix_key_slots,
-            shared_prefix_value_slots,
-        )
-
-    nears = [near_part(0, queries)]
-    hop_first, nears, known = lax.optimization_barrier((hop_first, nears, known))
+    hop_first, known = lax.optimization_barrier((hop_first, known))
     queries_here, hop_first = lax.optimization_barrier((queries, hop_first))
-    nears += [near_part(slot, queries_here) for slot in range(1, slots)]
+    near = attend_near(
+        queries_here,
+        seg_q,
+        seg_k,
+        suffix_rotated_key_slots,
+        suffix_value_slots,
+        shared_prefix_key_slots,
+        shared_prefix_value_slots,
+    )
+    other = lax.ppermute(known, "groups", [(i, (i + 1) % n_groups) for i in range(n_groups)])
+    rows = jnp.concatenate([known, known, other, other], axis=0)
+    idx_rows = jnp.pad(rows, ((0, 8 - rows.shape[0]), (0, 128 - rows.shape[1])))
     for hop in range(1, n_dp):
         if hop == 1:
             from_below, from_above = hop_first
         else:
             from_below, from_above = below[-1], above[-1]
             if hop == 3:
-                from_below, from_above, nears = lax.optimization_barrier(
-                    (from_below, from_above, nears)
+                from_below, from_above, near, idx_rows = lax.optimization_barrier(
+                    (from_below, from_above, near, idx_rows)
                 )
             from_below = lax.ppermute(from_below, "dp", up[hop - 1 :])
             from_above = lax.ppermute(from_above, "dp", down[: n_dp - hop])
@@ -555,31 +588,23 @@
         above.append(from_above)
 
     own = (jnp.transpose(adapter_down_factors, (0, 2, 1)), adapter_up_factors)
-    other = lax.ppermute(known, "groups", [(i, (i + 1) % n_groups) for i in range(n_groups)])
-    rows = jnp.concatenate([known, known, other, other], axis=0)
-    idx_rows = jnp.pad(rows, ((0, 8 - rows.shape[0]), (0, 128 - rows.shape[1])))
     sched = make_schedule(n_dp, requests, per, idx_rows, z)
     if n_dp > 2:
         sched, below[2], above[2] = lax.optimization_barrier((sched, below[2], above[2]))
-    ups, downs, nears = adapter_round(sched, own, [], [], requests, n_dp, nears)
-    attended = [
-        attend_far(slot, slots, z, queries, *nears[slot], below[1:], above[1:])
-        for slot in range(slots)
-    ]
+    ups, downs, near = adapter_round(sched, own, [], [], requests, n_dp, near)
+    attended = attend_far(z, queries, *near, below[1:], above[1:])
     ups, downs, attended = adapter_round(sched, own, ups, downs, requests, n_dp, attended)
     if n_tensor == 4:
         core, chip = by_core(n_tensor), by_chip(n_tensor)
 
-        def share(parts, owners, weigh=0):
-            pieces = jnp.arange(PIECES, dtype=jnp.int32)
-            blocks = jnp.concatenate([owner * PIECES + pieces for owner in owners])
-            return project(parts, output_weight_matrix, blocks, n_tensor * PIECES, weigh)
+        def share(parts, owners, weigh):
+            return project([parts], output_weight_matrix, jnp.stack(owners), n_tensor, PIECES, weigh)
 
         far = share(attended, (ti ^ 3, ti ^ 2), 8)
         far_other, far_same = far[:PIECES], far[PIECES:]
         far_other, ups, downs = lax.optimization_barrier((far_other, ups, downs))
         from_core = [lax.ppermute(x, "tensor", core) for x in far_other]
-        sends = [added(mine, came) for mine, came in zip(far_same, from_core)]
+        sends = add_all(far_same, from_core)
         sched, sends = lax.optimization_barrier((sched, sends))
         arriving = [lax.ppermute(x, "tensor", chip) for x in sends]
     ups, downs, again = adapter_round(sched, own, ups, downs, requests, n_dp, attended)
@@ -595,7 +620,7 @@
     picked_down, picked_up = picked[:, :rank], picked[:, rank:]
     select = request_of[:, None] == jnp.arange(requests, dtype=jnp.int32)[None, :]
     first = lax.dot_general(
-        jnp.concatenate(attended, axis=1),
+        attended,
         picked_down.reshape(-1, width),
         (((1,), (1,)), ((), ())),
         preferred_element_type=F32,
@@ -608,7 +633,7 @@
         ]
         base = jnp.concatenate(bases, axis=1)
     else:
-        (whole,) = project(attended, output_weight_matrix, jnp.zeros((1,), jnp.int32), 1)
+        (whole,) = project([attended], output_weight_matrix, jnp.zeros((1,), jnp.int32), 1, 1)
         share = lax.psum_scatter(whole, "tensor", scatter_dimension=1, tiled=True)
         base = share.astype(F32)
     shrink = all_sum(partial_shrink, n_tensor)

time: 188 us -> 185 us (0.984)
  waiting for transfers between devices: 25.9 us -> 35.9 us
  Pallas kernels: 90.1 us -> 83.3 us
  other arithmetic: 15 us -> 8.54 us
    ppermute x3, waiting for transfers between devices: 0.01 us -> 8.47 us  [per_device(): lax.ppermute(request_adapter_index, 'dp', [(i, (i + s) % n_dp) for i in r...]
    convert_element_type x6 -> x2, other arithmetic: 8.22 us -> 0.04 us  [added(): return (a.astype(F32) + b.astype(F32)).astype(BF16)]
    ppermute x2, waiting for transfers between devices: 6.37 us -> 1.37 us  [per_device(): from_above = lax.ppermute(from_above, 'dp', down[:n_dp - hop])]
    pallas_call x2 -> x1, Pallas kernels: 25.5 us -> 21.5 us  [attend_far(): pl.pallas_call(functools.partial(far_kernel, prefix_order(hops + 1), FACT...]
    ppermute x3, waiting for transfers between devices: 0.46 us -> 4.17 us  [adapter_round(): ups = ups + [lax.ppermute(sends[0], 'dp', up)]]
    pallas_call x4, Pallas kernels: 50.7 us -> 47.9 us  [the longest x2 28.6 us: project(): pl.pallas_call(functools.partial(project_kernel, per_tile, wide, len(part...]
    ppermute x4, waiting for transfers between devices: 0.56 us -> 2.83 us  [per_device(): from_core = [lax.ppermute(x, 'tensor', core) for x in far_other]]
    ppermute x1, waiting for transfers between devices: 2.05 us -> 0.01 us  [per_device(): lax.ppermute(known, 'groups', [(i, (i + 1) % n_groups) for i in range(n_g...]
  transfers between devices with their start and end apart: 30 -> 30, of which waited for: 8 -> 14; matrix products, arithmetic and copies ran while one was open for 10% -> 8% of each run, Pallas kernels for 47% -> 42%
where the time goes in v4:
time: 185 us; the launch traced here: 183 us
  Pallas kernels  83.3 us (45%)
  starting transfers between devices  43.4 us (23%)
  waiting for transfers between devices  35.9 us (19%)
  other arithmetic  8.54 us (5%)
  local copies, waits for them, and re-layouts  5.46 us (3%)
  matrix products  4.7 us (3%)
    pallas_call x2, Pallas kernels, project(): pl.pallas_call(functools.partial(project_kernel, per_tile, wide, len(part...  28.6 us
    pallas_call x1, Pallas kernels, attend_far(): pl.pallas_call(functools.partial(far_kernel, prefix_order(hops + 1), FACT...  21.5 us
    pallas_call x1, Pallas kernels, attend_near(): pl.pallas_call(functools.partial(near_kernel, FACTOR, halves), grid=(slot...  15 us
    ppermute x3, starting transfers between devices, adapter_round(): ups = ups + [lax.ppermute(sends[0], 'dp', up)]  12.2 us
    ppermute x3, waiting for transfers between devices, adapter_round(): downs = downs + [lax.ppermute(sends[1], 'dp', down)]  9.43 us
    ppermute x3, waiting for transfers between devices, per_device(): lax.ppermute(request_adapter_index, 'dp', [(i, (i + s) % n_dp) for i in r...  8.47 us
    ppermute x4, waiting for transfers between devices, per_device(): arriving = [lax.ppermute(x, 'tensor', chip) for x in sends]  8.1 us
    pallas_call x3, Pallas kernels, pick_sends(): pl.pallas_call(functools.partial(pick_kernel, first, count, own[0].shape[...  7.61 us
  transfers between devices with their start and end apart: 30, of which 14 were waited for; matrix products, arithmetic and copies ran while one was open for 8% of the time, Pallas kernels for 42%

profile of v4, /device:TPU:0, one launch (start us, length us, event | category | flops | bytes accessed | tf_op | source)
XLA Modules:
  0.0 183.1 jit_solution(8257672656963576541)
XLA Ops:
  1.9 5.0 %collective-permute-start.6 = (bf16[512,512]{1,0:T(8,128)(2,1)S(1)}, bf16[512,512]{1,0:T(8,128)(2,1)S(1)}, u32[]{:S(2)}, u32[]{:S(2)}) collective-permute-start(bf16[512,512]{1,0:T(8,128)(2,1)S(1)} %constant_dynamic-update-slice_fusion.8), channel_id=1, source_target_pairs={{0,4},{4,8},{8,12},{1,5},{5,9},{9,13},{2,6},{6,10},{10,14},{3,7},{... | collective-permute-start | bytes 1572872 | tf_op jit(solution)/shard_map/ppermute | solution.py:546
  8.2 4.7 %collective-permute-start.10 = (s32[1,4]{1,0:T(1,128)}, s32[1,4]{1,0:T(1,128)S(1)}, u32[]{:S(2)}, u32[]{:S(2)}) collective-permute-start(s32[1,4]{1,0:T(1,128)} %param.21), channel_id=1, source_target_pairs={{0,12},{4,0},{8,4},{12,8},{1,13},{5,1},{9,5},{13,9},{2,14},{6,2},{... | collective-permute-start | bytes 56 | tf_op jit(solution)/shard_map/ppermute | solution.py:551
  15.7 6.5 %collective-permute-done.10 = s32[1,4]{1,0:T(1,128)S(1)} collective-permute-done((s32[1,4]{1,0:T(1,128)}, s32[1,4]{1,0:T(1,128)S(1)}, u32[]{:S(2)}, u32[]{:S(2)}) %collective-permute-start.10) | collective-permute-done | bytes 48 | tf_op jit(solution)/shard_map/ppermute | solution.py:551
  22.3 1.9 %collective-permute-done.8 = s32[1,4]{1,0:T(1,128)S(1)} collective-permute-done((s32[1,4]{1,0:T(1,128)}, s32[1,4]{1,0:T(1,128)S(1)}, u32[]{:S(2)}, u32[]{:S(2)}) %collective-permute-start.8) | collective-permute-done | bytes 48 | tf_op jit(solution)/shard_map/ppermute | solution.py:551
  27.7 1.6 collective-permute-start.13
  29.2 15.0 %attend_near.1 = (f32[512,2048]{1,0:T(8,128)}, f32[512,2048]{1,0:T(8,128)}) custom-call(s32[512,2]{1,0:T(8,128)} %copy.13.seg_q, s32[1,512]{1,0:T(1,128)} %bitcast.93, bf16[512,2048]{1,0:T(8,128)(2,1)} %q_ref.2, bf16[512,256]{1,0:T(8,128)(2,1)} %sk_ref.1, bf16[512,256]{1,0:T(8,128)(2,1)} %sv_ref.1, bf16[512,256]{1,0:T(8,128)(2,1)} %pk_ref.1, ...), custom_call_target="tpu_custom_call" | custom-call | flops 17179869184 | bytes 1 | tf_op jit(solution)/shard_map/attend_near/pallas_call | solution.py:125
  47.5 2.6 %schedule.1.sched = s32[8,128]{1,0:T(8,128)} custom-call(s32[8,128]{1,0:T(8,128)} %pad.4.idx_ref, s32[1]{0:T(128)} %bitcast.41.z_ref.place), custom_call_target="tpu_custom_call" | custom-call | flops 1 | bytes 1 | tf_op jit(solution)/shard_map/schedule/pallas_call | solution.py:321
  50.1 2.4 %pick.7 = (bf16[2,128,2048]{2,1,0:T(8,128)(2,1)S(1)}, bf16[2,128,2048]{2,1,0:T(8,128)(2,1)S(1)}) custom-call(s32[8,128]{1,0:T(8,128)} %schedule.1.sched, bf16[16,64,2048]{2,1,0:T(8,128)(2,1)} %bitcast.86, bf16[16,64,2048]{2,1,0:T(8,128)(2,1)} %up_ref.5), custom_call_target="tpu_custom_call" | custom-call | flops 1 | bytes 1 | tf_op jit(solution)/shard_map/pick/pallas_call | solution.py:384
  52.5 5.0 %collective-permute-start.14 = (bf16[2,128,2048]{2,1,0:T(8,128)(2,1)S(1)}, bf16[2,128,2048]{2,1,0:T(8,128)(2,1)S(1)}, u32[]{:S(2)}, u32[]{:S(2)}) collective-permute-start(bf16[2,128,2048]{2,1,0:T(8,128)(2,1)S(1)} %get-tuple-element.284), channel_id=1, source_target_pairs={{0,4},{4,8},{8,12},{1,5},{5,9},{9,13},{2,6},{6,10},{10,14},{3,7},{... | collective-permute-start | bytes 3145736 | tf_op jit(solution)/shard_map/ppermute | solution.py:466
  61.1 21.5 %attend_far.1.refs_0_ = bf16[512,2048]{1,0:T(8,128)(2,1)} custom-call(s32[1]{0:T(128)} %bitcast.41.z_ref.place, bf16[512,2048]{1,0:T(8,128)(2,1)} %q_ref.2, f32[512,2048]{1,0:T(8,128)} %get-tuple-element.288.near_ref, f32[512,2048]{1,0:T(8,128)} %get-tuple-element.289.stat_ref, bf16[512,512]{1,0:T(8,128)(2,1)} %copy-done.12, ...), custom_call_target="tpu_custom_call" | custom-call | flops 25769803776 | bytes 1 | tf_op jit(solution)/shard_map/attend_far/pallas_call | solution.py:156
  82.9 2.6 %pick.8 = (bf16[2,128,2048]{2,1,0:T(8,128)(2,1)S(1)}, bf16[2,128,2048]{2,1,0:T(8,128)(2,1)S(1)}) custom-call(s32[8,128]{1,0:T(8,128)} %schedule.1.sched, bf16[16,64,2048]{2,1,0:T(8,128)(2,1)} %bitcast.87, bf16[16,64,2048]{2,1,0:T(8,128)(2,1)} %up_ref.5, bf16[2,128,2048]{2,1,0:T(8,128)(2,1)S(1)} %collective-permute-done.14.refs_0_, ...), custom_call_target="tpu_custom_call" | custom-call | flops 1 | bytes 1 | tf_op jit(solution)/shard_map/pick/pallas_call | solution.py:384
  85.5 3.9 %collective-permute-start.18 = (bf16[2,128,2048]{2,1,0:T(8,128)(2,1)S(1)}, bf16[2,128,2048]{2,1,0:T(8,128)(2,1)S(1)}, u32[]{:S(2)}, u32[]{:S(2)}) collective-permute-start(bf16[2,128,2048]{2,1,0:T(8,128)(2,1)S(1)} %get-tuple-element.303), channel_id=1, source_target_pairs={{0,4},{4,8},{8,12},{1,5},{5,9},{9,13},{2,6},{6,10},{10,14},{3,7},{... | collective-permute-start | bytes 3145736 | tf_op jit(solution)/shard_map/ppermute | solution.py:466
  91.0 14.3 %project.2 = (bf16[512,512]{1,0:T(8,128)(2,1)}, bf16[512,512]{1,0:T(8,128)(2,1)}, bf16[512,512]{1,0:T(8,128)(2,1)}, bf16[512,512]{1,0:T(8,128)(2,1)}, bf16[512,5...) custom-call(s32[2]{0:T(128)} %pad_add_fusion.4.which, ...), custom_call_target="tpu_custom_call" | custom-call | flops 17179869184 | bytes 1 | tf_op jit(solution)/shard_map/project/pallas_call | solution.py:204
  105.3 4.2 %collective-permute-done.18.refs_1_ = bf16[2,128,2048]{2,1,0:T(8,128)(2,1)S(1)} collective-permute-done((bf16[2,128,2048]{2,1,0:T(8,128)(2,1)S(1)}, bf16[2,128,2048]{2,1,0:T(8,128)(2,1)S(1)}, u32[]{:S(2)}, u32[]{:S(2)}) %collective-permute-start.18) | collective-permute-done | bytes 1048608 | tf_op jit(solution)/shard_map/ppermute | solution.py:466
  109.4 4.3 %collective-permute-done.19.refs_3_ = bf16[2,128,2048]{2,1,0:T(8,128)(2,1)} collective-permute-done((bf16[2,128,2048]{2,1,0:T(8,128)(2,1)S(1)}, bf16[2,128,2048]{2,1,0:T(8,128)(2,1)}, u32[]{:S(2)}, u32[]{:S(2)}) %collective-permute-start.19) | collective-permute-done | bytes 1048608 | tf_op jit(solution)/shard_map/ppermute | solution.py:467
  118.2 4.3 %add_all.1 = (bf16[512,512]{1,0:T(8,128)(2,1)}, bf16[512,512]{1,0:T(8,128)(2,1)}, bf16[512,512]{1,0:T(8,128)(2,1)}, bf16[512,512]{1,0:T(8,128)(2,1)}) custom-call(bf16[512,512]{1,0:T(8,128)(2,1)} %get-tuple-element.295.refs_0_, bf16[512,512]{1,0:T(8,128)(2,1)} %get-tuple-element.296.refs_1_, bf16[512,512]{1,0:T(8,128)(2,1)} %get-tuple-element.297.refs_2_, ...), custom_call_target="tpu_custom_call" | custom-call | flops 1 | bytes 1 | tf_op jit(solution)/shard_map/add_all/pallas_call | solution.py:234
  122.5 1.6 collective-permute-start.25
  124.6 2.6 %pick.9 = (bf16[2,128,2048]{2,1,0:T(8,128)(2,1)S(1)}, bf16[2,128,2048]{2,1,0:T(8,128)(2,1)S(1)}) custom-call(s32[8,128]{1,0:T(8,128)} %schedule.1.sched, bf16[16,64,2048]{2,1,0:T(8,128)(2,1)} %bitcast.88, bf16[16,64,2048]{2,1,0:T(8,128)(2,1)} %up_ref.5, bf16[2,128,2048]{2,1,0:T(8,128)(2,1)S(1)} %collective-permute-done.14.refs_0_, ...), custom_call_target="tpu_custom_call" | custom-call | flops 1 | bytes 1 | tf_op jit(solution)/shard_map/pick/pallas_call | solution.py:384
  127.2 3.2 %collective-permute-start.29 = (bf16[2,128,2048]{2,1,0:T(8,128)(2,1)S(1)}, bf16[2,128,2048]{2,1,0:T(8,128)(2,1)}, u32[]{:S(2)}, u32[]{:S(2)}) collective-permute-start(bf16[2,128,2048]{2,1,0:T(8,128)(2,1)S(1)} %get-tuple-element.332), channel_id=1, source_target_pairs={{0,4},{4,8},{8,12},{1,5},{5,9},{9,13},{2,6},{6,10},{10,14},{3,7},{... | collective-permute-start | bytes 3145736 | tf_op jit(solution)/shard_map/ppermute | solution.py:466
  131.7 14.3 %project.3 = (bf16[512,512]{1,0:T(8,128)(2,1)}, bf16[512,512]{1,0:T(8,128)(2,1)}, bf16[512,512]{1,0:T(8,128)(2,1)}, bf16[512,512]{1,0:T(8,128)(2,1)}, bf16[512,5...) custom-call(s32[2]{0:T(128)} %pad_add_fusion.2.which, ...), custom_call_target="tpu_custom_call" | custom-call | flops 8589934592 | bytes 1 | tf_op jit(solution)/shard_map/project/pallas_call | solution.py:204
  148.0 1.5 collective-permute-start.31
  151.9 4.8 %collective-permute-done.30 = bf16[2,128,2048]{2,1,0:T(8,128)(2,1)} collective-permute-done((bf16[2,128,2048]{2,1,0:T(8,128)(2,1)S(1)}, bf16[2,128,2048]{2,1,0:T(8,128)(2,1)}, u32[]{:S(2)}, u32[]{:S(2)}) %collective-permute-start.30) | collective-permute-done | bytes 1048608 | tf_op jit(solution)/shard_map/ppermute | solution.py:467
  156.8 3.9 %conditional.1 = (bf16[4,128,2048]{2,1,0:T(8,128)(2,1)}) conditional(s32[]{:T(128)} %bitcast.45, (s32[8,128]{1,0:T(8,128)}, s32[1]{0:T(128)}, bf16[16,64,2048]{2,1,0:T(8,128)(2,1)}, bf16[16,64,2048]{2,1,0:T(8,128)(2,1)}, bf16[2,128,2048]{2,1,0:T(8,128)(2,1)S(1)}, /*index=5*/bf16[2,128,2048]{2,1,0:T(8,128)(2,1)S(1)}, ...), branch_computations={%region_2.3_spmd, %region_3.4_spmd, %region_4.7_spmd} | conditional | flops 12058696 | bytes 72353256 | solution.py:488
  156.8 3.7 %gather_own.2 = bf16[4,128,2048]{2,1,0:T(8,128)(2,1)} custom-call(s32[8,128]{1,0:T(8,128)} %get-tuple-element.157.sched, s32[1]{0:T(128)} %get-tuple-element.158.z, bf16[16,64,2048]{2,1,0:T(8,128)(2,1)} %get-tuple-element.159.down_ref, bf16[16,64,2048]{2,1,0:T(8,128)(2,1)} %get-tuple-element.160.up_ref, ...), custom_call_target="tpu_custom_call" | custom-call | flops 1 | bytes 1 | tf_op jit(solution)/shard_map/cond/branch_0_fun/gather_own/pallas_call | solution.py:409
  161.3 1.5 collective-permute-start.33
  162.8 1.5 convert_add_fusion.3
  164.4 1.6 convert_add_fusion.2
  165.9 2.6 %fusion.10 = bf16[512,64]{0,1:T(8,128)(2,1)S(1)} fusion(bf16[512,2048]{1,0:T(8,128)(2,1)} %attend_far.1.refs_0_, bf16[4,128,2048]{2,1,0:T(8,128)(2,1)} %get-tuple-element.480, pred[512,4]{0,1:T(4,128)(4,1)S(1)} %iota_compare_fusion), kind=kOutput, calls=%fused_computation.42 | convolution fusion | flops 537100288 | bytes 3213312 | tf_op jit(solution)/shard_map/dot_general | solution.py:622
  168.6 6.8 %collective-permute-done.33 = bf16[512,512]{1,0:T(8,128)(2,1)S(1)} collective-permute-done((bf16[512,512]{1,0:T(8,128)(2,1)}, bf16[512,512]{1,0:T(8,128)(2,1)S(1)}, u32[]{:S(2)}, u32[]{:S(2)}) %collective-permute-start.33) | collective-permute-done | bytes 524320 | tf_op jit(solution)/shard_map/ppermute | solution.py:609
  176.7 1.6 collective-permute-start.35
  179.5 1.5 collective-permute-done.35
  181.0 2.1 %fusion.4 = bf16[512,2048]{1,0:T(8,128)(2,1)} fusion(f32[512,512]{1,0:T(8,128)S(1)} %convert_add_fusion, f32[512,512]{1,0:T(8,128)S(1)} %convert_add_fusion.1, f32[512,512]{1,0:T(8,128)S(1)} %convert_add_fusion.2, f32[512,512]{1,0:T(8,128)S(1)} %convert_add_fusion.3, bf16[4,128,2048]{2,1,0:T(8,128)(2,1)S(1)} %copy-done.3, ...), kind=kOutput, calls=%fused_computation.38 | convolution fusion | flops 542244864 | bytes 7407616 | tf_op jit(solution)/shard_map/dot_general | solution.py:641
  (79 shorter events, 30.5 us)
Async XLA Ops:
  1.9 23.0 %collective-permute-start.6 = (bf16[512,512]{1,0:T(8,128)(2,1)S(1)}, bf16[512,512]{1,0:T(8,128)(2,1)S(1)}, u32[]{:S(2)}, u32[]{:S(2)}) collective-permute-start(bf16[512,512]{1,0:T(8,128)(2,1)S(1)} %constant_dynamic-update-slice_fusion.8), channel_id=1, source_target_pairs={{0,4},{4,8},{8,12},{1,5},{5,9},{9,13},{2,6},{6,10},{10,14},{3,7},{... | collective-permute-start | bytes 1572872 | tf_op jit(solution)/shard_map/ppermute | solution.py:546
  6.9 18.0 %collective-permute-start.7 = (bf16[512,512]{1,0:T(8,128)(2,1)S(1)}, bf16[512,512]{1,0:T(8,128)(2,1)S(1)}, u32[]{:S(2)}, u32[]{:S(2)}) collective-permute-start(bf16[512,512]{1,0:T(8,128)(2,1)S(1)} %constant_dynamic-update-slice_fusion.8), channel_id=1, source_target_pairs={{4,0},{8,4},{12,8},{5,1},{9,5},{13,9},{6,2},{10,6},{14,10},{7,3},{... | collective-permute-start | bytes 1572872 | tf_op jit(solution)/shard_map/ppermute | solution.py:546
  8.2 14.0 %collective-permute-start.10 = (s32[1,4]{1,0:T(1,128)}, s32[1,4]{1,0:T(1,128)S(1)}, u32[]{:S(2)}, u32[]{:S(2)}) collective-permute-start(s32[1,4]{1,0:T(1,128)} %param.21), channel_id=1, source_target_pairs={{0,12},{4,0},{8,4},{12,8},{1,13},{5,1},{9,5},{13,9},{2,14},{6,2},{... | collective-permute-start | bytes 56 | tf_op jit(solution)/shard_map/ppermute | solution.py:551
  12.9 11.3 %collective-permute-start.8 = (s32[1,4]{1,0:T(1,128)}, s32[1,4]{1,0:T(1,128)S(1)}, u32[]{:S(2)}, u32[]{:S(2)}) collective-permute-start(s32[1,4]{1,0:T(1,128)} %param.21), channel_id=1, source_target_pairs={{0,4},{4,8},{8,12},{12,0},{1,5},{5,9},{9,13},{13,1},{2,6},{6,10},{... | collective-permute-start | bytes 56 | tf_op jit(solution)/shard_map/ppermute | solution.py:551
  12.9 11.3 %collective-permute-start.9 = (s32[1,4]{1,0:T(1,128)}, s32[1,4]{1,0:T(1,128)S(1)}, u32[]{:S(2)}, u32[]{:S(2)}) collective-permute-start(s32[1,4]{1,0:T(1,128)} %param.21), channel_id=1, source_target_pairs={{0,8},{4,12},{8,0},{12,4},{1,9},{5,13},{9,1},{13,5},{2,10},{6,14},... | collective-permute-start | bytes 56 | tf_op jit(solution)/shard_map/ppermute | solution.py:551
  24.9 19.9 %collective-permute-start.11 = (bf16[512,512]{1,0:T(8,128)(2,1)S(1)}, bf16[512,512]{1,0:T(8,128)(2,1)}, u32[]{:S(2)}, u32[]{:S(2)}) collective-permute-start(bf16[512,512]{1,0:T(8,128)(2,1)S(1)} %collective-permute-done.6.refs_0_), channel_id=1, source_target_pairs={{4,8},{8,12},{5,9},{9,13},{6,10},{10,14},{7,11},{11,15},{20,24},{2... | collective-permute-start | bytes 1572872 | tf_op jit(solution)/shard_map/ppermute | solution.py:585
  26.4 18.5 %collective-permute-start.12 = (bf16[512,512]{1,0:T(8,128)(2,1)S(1)}, bf16[512,512]{1,0:T(8,128)(2,1)}, u32[]{:S(2)}, u32[]{:S(2)}) collective-permute-start(bf16[512,512]{1,0:T(8,128)(2,1)S(1)} %collective-permute-done.7.refs_3_), channel_id=1, source_target_pairs={{4,0},{8,4},{5,1},{9,5},{6,2},{10,6},{7,3},{11,7},{20,16},{24,20},... | collective-permute-start | bytes 1572872 | tf_op jit(solution)/shard_map/ppermute | solution.py:586
  27.7 16.6 %collective-permute-start.13 = (s32[1,16]{1,0:T(1,128)S(1)}, s32[1,16]{1,0:T(1,128)S(1)}, u32[]{:S(2)}, u32[]{:S(2)}) collective-permute-start(s32[1,16]{1,0:T(1,128)S(1)} %pad_add_fusion.3), channel_id=1, source_target_pairs={{0,16},{16,0},{1,17},{17,1},{2,18},{18,2},{3,19},{19,3},{4,20},{20... | collective-permute-start | bytes 200 | tf_op jit(solution)/shard_map/ppermute | solution.py:573
  44.9 14.0 %collective-permute-start.16 = (bf16[512,512]{1,0:T(8,128)(2,1)}, bf16[512,512]{1,0:T(8,128)(2,1)S(1)}, u32[]{:S(2)}, u32[]{:S(2)}) collective-permute-start(bf16[512,512]{1,0:T(8,128)(2,1)} %collective-permute-done.11.refs_1_), channel_id=1, source_target_pairs={{8,12},{9,13},{10,14},{11,15},{24,28},{25,29},{26,30},{27,31}} | collective-permute-start | bytes 1572872 | tf_op jit(solution)/shard_map/ppermute | solution.py:585
  45.6 14.7 %collective-permute-start.17 = (bf16[512,512]{1,0:T(8,128)(2,1)}, bf16[512,512]{1,0:T(8,128)(2,1)S(1)}, u32[]{:S(2)}, u32[]{:S(2)}) collective-permute-start(bf16[512,512]{1,0:T(8,128)(2,1)} %collective-permute-done.12.refs_4_), channel_id=1, source_target_pairs={{4,0},{5,1},{6,2},{7,3},{20,16},{21,17},{22,18},{23,19}} | collective-permute-start | bytes 1572872 | tf_op jit(solution)/shard_map/ppermute | solution.py:586
  52.5 30.1 %collective-permute-start.14 = (bf16[2,128,2048]{2,1,0:T(8,128)(2,1)S(1)}, bf16[2,128,2048]{2,1,0:T(8,128)(2,1)S(1)}, u32[]{:S(2)}, u32[]{:S(2)}) collective-permute-start(bf16[2,128,2048]{2,1,0:T(8,128)(2,1)S(1)} %get-tuple-element.284), channel_id=1, source_target_pairs={{0,4},{4,8},{8,12},{1,5},{5,9},{9,13},{2,6},{6,10},{10,14},{3,7},{... | collective-permute-start | bytes 3145736 | tf_op jit(solution)/shard_map/ppermute | solution.py:466
  57.6 25.3 %collective-permute-start.15 = (bf16[2,128,2048]{2,1,0:T(8,128)(2,1)S(1)}, bf16[2,128,2048]{2,1,0:T(8,128)(2,1)S(1)}, u32[]{:S(2)}, u32[]{:S(2)}) collective-permute-start(bf16[2,128,2048]{2,1,0:T(8,128)(2,1)S(1)} %get-tuple-element.285), channel_id=1, source_target_pairs={{4,0},{8,4},{12,8},{5,1},{9,5},{13,9},{6,2},{10,6},{14,10},{7,3},{... | collective-permute-start | bytes 3145736 | tf_op jit(solution)/shard_map/ppermute | solution.py:467
  85.5 23.9 %collective-permute-start.18 = (bf16[2,128,2048]{2,1,0:T(8,128)(2,1)S(1)}, bf16[2,128,2048]{2,1,0:T(8,128)(2,1)S(1)}, u32[]{:S(2)}, u32[]{:S(2)}) collective-permute-start(bf16[2,128,2048]{2,1,0:T(8,128)(2,1)S(1)} %get-tuple-element.303), channel_id=1, source_target_pairs={{0,4},{4,8},{8,12},{1,5},{5,9},{9,13},{2,6},{6,10},{10,14},{3,7},{... | collective-permute-start | bytes 3145736 | tf_op jit(solution)/shard_map/ppermute | solution.py:466
  89.5 24.2 %collective-permute-start.19 = (bf16[2,128,2048]{2,1,0:T(8,128)(2,1)S(1)}, bf16[2,128,2048]{2,1,0:T(8,128)(2,1)}, u32[]{:S(2)}, u32[]{:S(2)}) collective-permute-start(bf16[2,128,2048]{2,1,0:T(8,128)(2,1)S(1)} %get-tuple-element.304), channel_id=1, source_target_pairs={{4,0},{8,4},{12,8},{5,1},{9,5},{13,9},{6,2},{10,6},{14,10},{7,3},{... | collective-permute-start | bytes 3145736 | tf_op jit(solution)/shard_map/ppermute | solution.py:467
  113.7 2.3 %collective-permute-start.20 = (bf16[512,512]{1,0:T(8,128)(2,1)}, bf16[512,512]{1,0:T(8,128)(2,1)}, u32[]{:S(2)}, u32[]{:S(2)}) collective-permute-start(bf16[512,512]{1,0:T(8,128)(2,1)} %get-tuple-element.305), channel_id=1, source_target_pairs={{0,1},{1,0},{2,3},{3,2},{4,5},{5,4},{6,7},{7,6},{8,9},{9,8},{10,11... | collective-permute-start | bytes 1572872 | tf_op jit(solution)/shard_map/ppermute | solution.py:606
  113.7 3.0 %collective-permute-start.21 = (bf16[512,512]{1,0:T(8,128)(2,1)}, bf16[512,512]{1,0:T(8,128)(2,1)}, u32[]{:S(2)}, u32[]{:S(2)}) collective-permute-start(bf16[512,512]{1,0:T(8,128)(2,1)} %get-tuple-element.306), channel_id=1, source_target_pairs={{0,1},{1,0},{2,3},{3,2},{4,5},{5,4},{6,7},{7,6},{8,9},{9,8},{10,11... | collective-permute-start | bytes 1572872 | tf_op jit(solution)/shard_map/ppermute | solution.py:606
  114.2 3.2 %collective-permute-start.22 = (bf16[512,512]{1,0:T(8,128)(2,1)}, bf16[512,512]{1,0:T(8,128)(2,1)}, u32[]{:S(2)}, u32[]{:S(2)}) collective-permute-start(bf16[512,512]{1,0:T(8,128)(2,1)} %get-tuple-element.307), channel_id=1, source_target_pairs={{0,1},{1,0},{2,3},{3,2},{4,5},{5,4},{6,7},{7,6},{8,9},{9,8},{10,11... | collective-permute-start | bytes 1572872 | tf_op jit(solution)/shard_map/ppermute | solution.py:606
  114.2 4.0 %collective-permute-start.23 = (bf16[512,512]{1,0:T(8,128)(2,1)}, bf16[512,512]{1,0:T(8,128)(2,1)}, u32[]{:S(2)}, u32[]{:S(2)}) collective-permute-start(bf16[512,512]{1,0:T(8,128)(2,1)} %get-tuple-element.308), channel_id=1, source_target_pairs={{0,1},{1,0},{2,3},{3,2},{4,5},{5,4},{6,7},{7,6},{8,9},{9,8},{10,11... | collective-permute-start | bytes 1572872 | tf_op jit(solution)/shard_map/ppermute | solution.py:606
  122.5 23.6 %collective-permute-start.25 = (bf16[512,512]{1,0:T(8,128)(2,1)}, bf16[512,512]{1,0:T(8,128)(2,1)}, u32[]{:S(2)}, u32[]{:S(2)}) collective-permute-start(bf16[512,512]{1,0:T(8,128)(2,1)} %get-tuple-element.323), channel_id=1, source_target_pairs={{0,2},{1,3},{2,0},{3,1},{4,6},{5,7},{6,4},{7,5},{8,10},{9,11},{10,... | collective-permute-start | bytes 1572872 | tf_op jit(solution)/shard_map/ppermute | solution.py:609
  124.1 23.9 %collective-permute-start.26 = (bf16[512,512]{1,0:T(8,128)(2,1)}, bf16[512,512]{1,0:T(8,128)(2,1)S(1)}, u32[]{:S(2)}, u32[]{:S(2)}) collective-permute-start(bf16[512,512]{1,0:T(8,128)(2,1)} %get-tuple-element.324), channel_id=1, source_target_pairs={{0,2},{1,3},{2,0},{3,1},{4,6},{5,7},{6,4},{7,5},{8,10},{9,11},{10,... | collective-permute-start | bytes 1572872 | tf_op jit(solution)/shard_map/ppermute | solution.py:609
  127.2 19.4 %copy-start.11 = (s32[512]{0:T(512)S(1)}, s32[512]{0:T(512)}, u32[]{:S(2)}) copy-start(s32[512]{0:T(512)} %copy-done.10) | copy-start | bytes 6148
  127.2 24.7 %collective-permute-start.29 = (bf16[2,128,2048]{2,1,0:T(8,128)(2,1)S(1)}, bf16[2,128,2048]{2,1,0:T(8,128)(2,1)}, u32[]{:S(2)}, u32[]{:S(2)}) collective-permute-start(bf16[2,128,2048]{2,1,0:T(8,128)(2,1)S(1)} %get-tuple-element.332), channel_id=1, source_target_pairs={{0,4},{4,8},{8,12},{1,5},{5,9},{9,13},{2,6},{6,10},{10,14},{3,7},{... | collective-permute-start | bytes 3145736 | tf_op jit(solution)/shard_map/ppermute | solution.py:466
  130.4 26.3 %collective-permute-start.30 = (bf16[2,128,2048]{2,1,0:T(8,128)(2,1)S(1)}, bf16[2,128,2048]{2,1,0:T(8,128)(2,1)}, u32[]{:S(2)}, u32[]{:S(2)}) collective-permute-start(bf16[2,128,2048]{2,1,0:T(8,128)(2,1)S(1)} %get-tuple-element.333), channel_id=1, source_target_pairs={{4,0},{8,4},{12,8},{5,1},{9,5},{13,9},{6,2},{10,6},{14,10},{7,3},{... | collective-permute-start | bytes 3145736 | tf_op jit(solution)/shard_map/ppermute | solution.py:467
  146.0 15.3 %collective-permute-start.24 = (bf16[512,512]{1,0:T(8,128)(2,1)}, bf16[512,512]{1,0:T(8,128)(2,1)}, u32[]{:S(2)}, u32[]{:S(2)}) collective-permute-start(bf16[512,512]{1,0:T(8,128)(2,1)} %get-tuple-element.322), channel_id=1, source_target_pairs={{0,1},{1,0},{2,3},{3,2},{4,5},{5,4},{6,7},{7,6},{8,9},{9,8},{10,11... | collective-permute-start | bytes 1572872 | tf_op jit(solution)/shard_map/ppermute | solution.py:614
  146.1 18.2 %collective-permute-start.27 = (bf16[512,512]{1,0:T(8,128)(2,1)}, bf16[512,512]{1,0:T(8,128)(2,1)}, u32[]{:S(2)}, u32[]{:S(2)}) collective-permute-start(bf16[512,512]{1,0:T(8,128)(2,1)} %get-tuple-element.327), channel_id=1, source_target_pairs={{0,1},{1,0},{2,3},{3,2},{4,5},{5,4},{6,7},{7,6},{8,9},{9,8},{10,11... | collective-permute-start | bytes 1572872 | tf_op jit(solution)/shard_map/ppermute | solution.py:614
  148.0 18.0 %collective-permute-start.31 = (bf16[512,512]{1,0:T(8,128)(2,1)}, bf16[512,512]{1,0:T(8,128)(2,1)}, u32[]{:S(2)}, u32[]{:S(2)}) collective-permute-start(bf16[512,512]{1,0:T(8,128)(2,1)} %get-tuple-element.334), channel_id=1, source_target_pairs={{0,2},{1,3},{2,0},{3,1},{4,6},{5,7},{6,4},{7,5},{8,10},{9,11},{10,... | collective-permute-start | bytes 1572872 | tf_op jit(solution)/shard_map/ppermute | solution.py:609
  160.7 20.3 %copy-start.3 = (bf16[4,128,2048]{2,1,0:T(8,128)(2,1)S(1)}, bf16[4,128,2048]{2,1,0:T(8,128)(2,1)}, u32[]{:S(2)}) copy-start(bf16[4,128,2048]{2,1,0:T(8,128)(2,1)} %get-tuple-element.480) | copy-start | bytes 6291460
  160.7 17.6 %collective-permute-start.28 = (bf16[512,512]{1,0:T(8,128)(2,1)}, bf16[512,512]{1,0:T(8,128)(2,1)S(1)}, u32[]{:S(2)}, u32[]{:S(2)}) collective-permute-start(bf16[512,512]{1,0:T(8,128)(2,1)} %get-tuple-element.330), channel_id=1, source_target_pairs={{0,1},{1,0},{2,3},{3,2},{4,5},{5,4},{6,7},{7,6},{8,9},{9,8},{10,11... | collective-permute-start | bytes 1572872 | tf_op jit(solution)/shard_map/ppermute | solution.py:614
  160.8 7.9 %collective-permute-start.32 = (bf16[512,512]{1,0:T(8,128)(2,1)}, bf16[512,512]{1,0:T(8,128)(2,1)S(1)}, u32[]{:S(2)}, u32[]{:S(2)}) collective-permute-start(bf16[512,512]{1,0:T(8,128)(2,1)} %get-tuple-element.337), channel_id=1, source_target_pairs={{0,1},{1,0},{2,3},{3,2},{4,5},{5,4},{6,7},{7,6},{8,9},{9,8},{10,11... | collective-permute-start | bytes 1572872 | tf_op jit(solution)/shard_map/ppermute | solution.py:614
  161.3 14.1 %collective-permute-start.33 = (bf16[512,512]{1,0:T(8,128)(2,1)}, bf16[512,512]{1,0:T(8,128)(2,1)S(1)}, u32[]{:S(2)}, u32[]{:S(2)}) collective-permute-start(bf16[512,512]{1,0:T(8,128)(2,1)} %get-tuple-element.338), channel_id=1, source_target_pairs={{0,2},{1,3},{2,0},{3,1},{4,6},{5,7},{6,4},{7,5},{8,10},{9,11},{10,... | collective-permute-start | bytes 1572872 | tf_op jit(solution)/shard_map/ppermute | solution.py:609
  168.6 8.1 %collective-permute-start.34 = (bf16[512,64]{0,1:T(8,128)(2,1)S(1)}, bf16[512,64]{0,1:T(8,128)(2,1)S(1)}, u32[]{:S(2)}, u32[]{:S(2)}) collective-permute-start(bf16[512,64]{0,1:T(8,128)(2,1)S(1)} %fusion.10), channel_id=1, source_target_pairs={{0,1},{1,0},{2,3},{3,2},{4,5},{5,4},{6,7},{7,6},{8,9},{9,8},{10,11... | collective-permute-start | bytes 196616 | tf_op jit(solution)/shard_map/ppermute | solution.py:506
  176.7 4.3 %collective-permute-start.35 = (bf16[512,64]{0,1:T(8,128)(2,1)S(1)}, bf16[512,64]{0,1:T(8,128)(2,1)S(1)}, u32[]{:S(2)}, u32[]{:S(2)}) collective-permute-start(bf16[512,64]{0,1:T(8,128)(2,1)S(1)} %add_convert_fusion.1), channel_id=1, source_target_pairs={{0,2},{1,3},{2,0},{3,1},{4,6},{5,7},{6,4},{7,5},{8,10},{9,11},{10,... | collective-permute-start | bytes 196616 | tf_op jit(solution)/shard_map/ppermute | solution.py:507
  (7 other events, 81.7 us)
